TPU v7x, 32 devices: a whole 2x2x4 slice. The times are simulated.
32 devices in a mesh: rep: 2 (over x), node: 4 (over y, core), local: 4 (over z).
Axes of the slice: x: 2, y: 2, z: 4, core: 2. Of those that a mesh axis runs over, the one named last changes fastest.
Arguments:
- grad_out: bfloat16 [512, 3584], P(('rep', 'node', 'local')), parts along dimension 0, may hold values from -6 to 6
- saved_input: bfloat16 [512, 3584], P(('rep', 'node', 'local')), parts along dimension 0, may hold values from -6 to 6
- gate_weight: bfloat16 [8, 3584, 1024], P('node', None, 'local'), may hold values from -0.09375 to 0.09375
- up_weight: bfloat16 [8, 3584, 1024], P('node', None, 'local'), may hold values from -0.09375 to 0.09375
- down_weight: bfloat16 [8, 1024, 3584], P('node', 'local'), may hold values from -0.1875 to 0.1875
- expert_ids: int32 [512, 6], P(('rep', 'node', 'local')), parts along dimension 0, may hold values from 0 to 7, as said below
- gate_num: int32 [512, 6], P(('rep', 'node', 'local')), parts along dimension 0, may hold values from 16 to 255
Outputs:
- grad_input: bfloat16 [512, 3584], P(('rep', 'node', 'local')), parts along dimension 0
- grad_gate_weight: bfloat16 [16, 3584, 1024], P(('rep', 'node'), None, 'local'), parts along dimension 0
- grad_up_weight: bfloat16 [16, 3584, 1024], P(('rep', 'node'), None, 'local'), parts along dimension 0
- grad_down_weight: bfloat16 [16, 1024, 3584], P(('rep', 'node'), 'local'), parts along dimension 0
There are 2 independent parts, one for each index of `rep`. A program takes and returns all parts, laid end to end along the dimension named above; an argument that names none is the same for every part. Nothing has to cross between parts.
Inputs may be any that keep to these rules, and one draw needn't show every extreme that they name: `expert_ids`: each token names 6 different experts lying in exactly 4 node groups (expert e in group e // 2): both experts of 2 of these groups and one expert of each other. Of the 16 tokens of one device, at most 16 visit any one node group; one node group is visited by exactly 16 tokens of every device.
All inputs are finite; a program needn't handle non-finite values.
Results may differ from a plain program's by a relative error of at most 0.0064.
Values may be sent and summed in bfloat16 or wider, within the bound.
No kernel may reach another device: no remote copies, remote signals or barrier semaphores. Data moves between devices by JAX's collectives and lax.ppermute only.
A program may use at most 192 MiB of HBM per device.

v0:
```python
import jax
import jax.numpy as jnp
from jax import lax
from jax.sharding import PartitionSpec as P

LIMIT = 4


gate_scale = 1.0 / 256.0


def spread_rows(source, groups, local_count):
    widened = jnp.broadcast_to(source[:, None], (groups, local_count) + source.shape[1:])
    return widened.reshape((groups * local_count,) + source.shape[1:])


def per_device(grad_out, saved_input, gate_weight, up_weight, down_weight, expert_ids, gate_num):
    tokens_here = grad_out.shape[0]
    model_width = grad_out.shape[1]
    groups = lax.axis_size("node")
    local_count = lax.axis_size("local")
    experts_here = gate_weight.shape[0]
    capacity = min(tokens_here, 2 * LIMIT * tokens_here // groups)
    group_of = expert_ids // experts_here
    visits = jnp.any(
        group_of[:, :, None] == jnp.arange(groups, dtype=jnp.int32)[None, None, :], axis=1
    ).astype(jnp.int32)
    before = jnp.cumsum(visits, axis=0) - visits
    slot_hit = (before[:, :, None] == jnp.arange(capacity, dtype=jnp.int32)[None, None, :]) & (
        visits[:, :, None] == 1
    )
    select = jnp.transpose(slot_hit, (1, 2, 0)).astype(jnp.bfloat16)
    expert_hot = (
        expert_ids[:, :, None] == jnp.arange(groups * experts_here, dtype=jnp.int32)[None, None, :]
    ).astype(jnp.float32)
    gate_values = jnp.sum(
        expert_hot * (gate_num.astype(jnp.float32) * gate_scale)[:, :, None], axis=1
    )
    gate_table = gate_values.reshape(tokens_here, groups, experts_here)
    send_input = jnp.einsum(
        "gct,td->gcd", select, saved_input, preferred_element_type=jnp.float32
    ).astype(jnp.bfloat16)
    send_grad = jnp.einsum(
        "gct,td->gcd", select, grad_out, preferred_element_type=jnp.float32
    ).astype(jnp.bfloat16)
    send_gate = jnp.einsum("gct,tge->gce", select.astype(jnp.float32), gate_table).astype(
        jnp.bfloat16
    )
    got_input, got_grad, got_gate = (
        lax.all_to_all(
            spread_rows(send_input, groups, local_count),
            ("node", "local"),
            split_axis=0,
            concat_axis=0,
            tiled=True,
        ),
        lax.all_to_all(
            spread_rows(send_grad, groups, local_count),
            ("node", "local"),
            split_axis=0,
            concat_axis=0,
            tiled=True,
        ),
        lax.all_to_all(
            spread_rows(send_gate, groups, local_count),
            ("node", "local"),
            split_axis=0,
            concat_axis=0,
            tiled=True,
        ),
    )
    rows_input = got_input.reshape(groups, local_count, capacity, model_width)
    rows_grad = got_grad.reshape(groups, local_count, capacity, model_width)
    rows_gate = got_gate.reshape(groups, local_count, capacity, experts_here)
    row_count = groups * local_count * capacity
    inputs = rows_input.reshape(row_count, model_width)
    row_grads = rows_grad.reshape(row_count, model_width)
    row_gates = rows_gate.reshape(row_count, experts_here)
    contract_rows = (((0,), (0,)), ((), ()))
    contract_cols = (((1,), (1,)), ((), ()))
    gate_grads = []
    up_grads = []
    down_grads = []
    pieces = []
    columns = []
    for expert in range(experts_here):
        gate_act = jnp.dot(inputs, gate_weight[expert], preferred_element_type=jnp.float32)
        up_act = jnp.dot(inputs, up_weight[expert], preferred_element_type=jnp.float32)
        sigmoid_val = jax.nn.sigmoid(gate_act)
        hidden = (gate_act * sigmoid_val * up_act).astype(jnp.bfloat16)
        scaled = (
            row_gates[:, expert : expert + 1].astype(jnp.float32) * row_grads.astype(jnp.float32)
        ).astype(jnp.bfloat16)
        down_grads.append(
            lax.dot_general(
                hidden, scaled, contract_rows, preferred_element_type=jnp.float32
            ).astype(jnp.bfloat16)
        )
        back_grad = lax.dot_general(
            scaled, down_weight[expert], contract_cols, preferred_element_type=jnp.float32
        )
        grad_gate_act = (
            back_grad * up_act * sigmoid_val * (1.0 + gate_act * (1.0 - sigmoid_val))
        ).astype(jnp.bfloat16)
        grad_up_act = (back_grad * gate_act * sigmoid_val).astype(jnp.bfloat16)
        gate_grads.append(
            lax.dot_general(
                inputs, grad_gate_act, contract_rows, preferred_element_type=jnp.float32
            ).astype(jnp.bfloat16)
        )
        up_grads.append(
            lax.dot_general(
                inputs, grad_up_act, contract_rows, preferred_element_type=jnp.float32
            ).astype(jnp.bfloat16)
        )
        pieces.append(grad_gate_act)
        pieces.append(grad_up_act)
        columns.append(gate_weight[expert])
        columns.append(up_weight[expert])
    activations = jnp.concatenate(pieces, axis=1)
    stacked = jnp.concatenate(columns, axis=1)
    partial_value = lax.dot_general(
        activations, stacked, contract_cols, preferred_element_type=jnp.float32
    )
    returned = lax.all_to_all(
        partial_value.reshape(groups * local_count, capacity, model_width),
        ("node", "local"),
        split_axis=0,
        concat_axis=0,
        tiled=True,
    )
    group_grads = jnp.sum(
        returned.reshape(groups, local_count, capacity, model_width), axis=1
    ).astype(jnp.bfloat16)
    grad_input = jnp.einsum(
        "gct,gcd->td", select, group_grads, preferred_element_type=jnp.float32
    ).astype(jnp.bfloat16)
    return (grad_input, jnp.stack(gate_grads), jnp.stack(up_grads), jnp.stack(down_grads))


def solution(mesh):
    in_specs = (
        P(("rep", "node", "local"), None),
        P(("rep", "node", "local"), None),
        P("node", None, "local"),
        P("node", None, "local"),
        P("node", "local", None),
        P(("rep", "node", "local"), None),
        P(("rep", "node", "local"), None),
    )
    out_specs = (
        P(("rep", "node", "local"), None),
        P(("rep", "node"), None, "local"),
        P(("rep", "node"), None, "local"),
        P(("rep", "node"), "local", None),
    )
    return jax.shard_map(
        per_device, mesh=mesh, in_specs=in_specs, out_specs=out_specs, check_vma=False
    )
```

profile of v0, /device:TPU:0, one launch (start us, length us, event | category | flops | bytes accessed | tf_op | source)
XLA Modules:
  0.0 220.1 jit_solution(17732803886470195900)
XLA Ops:
  0.6 0.7 add_select_fusion
  3.9 7.4 %all-to-all-start = ((bf16[16,16,2]{1,2,0:T(2,128)(2,1)}), bf16[16,16,2]{1,2,0:T(2,128)(2,1)S(1)}, u32[]{:S(2)}, u32[]{:S(2)}) async-start(bf16[16,16,2]{1,2,0:T(2,128)(2,1)} %bitcast.3), calls=%async_computation | async-start | bytes 16384 | tf_op jit(solution)/shard_map/all_to_all | solution.py:64
  11.7 5.9 %all-to-all-done = bf16[16,16,2]{1,2,0:T(2,128)(2,1)S(1)} async-done(((bf16[16,16,2]{1,2,0:T(2,128)(2,1)}), bf16[16,16,2]{1,2,0:T(2,128)(2,1)S(1)}, u32[]{:S(2)}, u32[]{:S(2)}) %all-to-all-start) | async-done | bytes 1056 | tf_op jit(solution)/shard_map/all_to_all | solution.py:64
  17.6 1.4 broadcast_in_dim.8
  19.0 3.8 %all-to-all-start.2 = ((bf16[16,16,3584]{2,1,0:T(8,128)(2,1)}), bf16[16,16,3584]{2,1,0:T(8,128)(2,1)S(1)}, u32[]{:S(2)}, u32[]{:S(2)}) async-start(bf16[16,16,3584]{2,1,0:T(8,128)(2,1)} %bitcast.96), calls=%async_computation.2 | async-start | bytes 3670016 | tf_op jit(solution)/shard_map/all_to_all | solution.py:50
  23.3 43.4 %all-to-all-done.2 = bf16[16,16,3584]{2,1,0:T(8,128)(2,1)S(1)} async-done(((bf16[16,16,3584]{2,1,0:T(8,128)(2,1)}), bf16[16,16,3584]{2,1,0:T(8,128)(2,1)S(1)}, u32[]{:S(2)}, u32[]{:S(2)}) %all-to-all-start.2) | async-done | bytes 1835040 | tf_op jit(solution)/shard_map/all_to_all | solution.py:50
  66.7 1.4 broadcast_in_dim.7
  68.1 4.4 %all-to-all-start.1 = ((bf16[16,16,3584]{2,1,0:T(8,128)(2,1)}), bf16[16,16,3584]{2,1,0:T(8,128)(2,1)}, u32[]{:S(2)}, u32[]{:S(2)}) async-start(bf16[16,16,3584]{2,1,0:T(8,128)(2,1)} %bitcast.95), calls=%async_computation.1 | async-start | bytes 3670016 | tf_op jit(solution)/shard_map/all_to_all | solution.py:57
  72.5 6.3 %slice_bitcast_fusion.2 = (bf16[3584,256]{1,0:T(8,128)(2,1)}, bf16[3584,256]{1,0:T(8,128)(2,1)}, bf16[3584,256]{1,0:T(8,128)(2,1)}, bf16[3584,256]{1,0:T(8,128)(2,1)}) fusion(bf16[2,3584,256]{2,1,0:T(8,128)(2,1)} %param.9, bf16[2,3584,256]{2,1,0:T(8,128)(2,1)} %param.10), kind=kLoop, calls=%fused_computation.43 | loop fusion | bytes 14680064 | tf_op jit(solution)/shard_map/squeeze | solution.py:87
  79.1 2.5 %fusion.60 = f32[256,256]{0,1:T(8,128)S(1)} fusion(bf16[256,3584]{1,0:T(8,128)(2,1)S(1)} %bitcast.87, bf16[2,3584,256]{2,1,0:T(8,128)(2,1)} %param.10), kind=kOutput, calls=%fused_computation.100 | convolution fusion | flops 469762048 | bytes 3932160 | tf_op jit(solution)/shard_map/dot_general | solution.py:88
  81.7 0.8 fusion.58
  82.5 33.8 %all-to-all-done.1 = bf16[16,16,3584]{2,1,0:T(8,128)(2,1)} async-done(((bf16[16,16,3584]{2,1,0:T(8,128)(2,1)}), bf16[16,16,3584]{2,1,0:T(8,128)(2,1)}, u32[]{:S(2)}, u32[]{:S(2)}) %all-to-all-start.1) | async-done | bytes 1835040 | tf_op jit(solution)/shard_map/all_to_all | solution.py:57
  116.3 2.7 %fusion.15 = (bf16[16,16,3584]{2,1,0:T(8,128)(2,1)S(1)}, bf16[16,16,3584]{2,1,0:T(8,128)(2,1)S(1)}) fusion(bf16[16,16,3584]{2,1,0:T(8,128)(2,1)} %all-to-all-done.1, f32[16,16]{1,0:T(8,128)S(1)} %mul.100, f32[16,16]{1,0:T(8,128)S(1)} %mul.109), kind=kLoop, calls=%fused_computation.31 | loop fusion | flops 4587520 | bytes 5507072 | tf_op jit(solution)/shard_map/convert_element_type | solution.py:93
  120.4 1.4 copy-done.2
  121.7 0.9 multiply_convert_fusion.3
  122.7 0.9 multiply_convert_fusion.5
  125.4 3.6 %fusion = f32[256,3584]{1,0:T(8,128)} fusion(bf16[3584,256]{1,0:T(8,128)(2,1)S(1)} %copy-done.5, bf16[3584,256]{1,0:T(8,128)(2,1)S(1)} %copy-done.4, bf16[3584,256]{1,0:T(8,128)(2,1)S(1)} %copy-done.6, bf16[3584,256]{1,0:T(8,128)(2,1)S(1)} %copy-done.3, bf16[256,256]{0,1:T(8,128)(2,1)S(1)} %get-tuple-element.17, bf16[256,256]{0,1:T(8,128)(2,1)S(1)} %get-tuple-element.16, ...), kind=kOutput, calls=%fused_computation | convolution fusion | flops 1910505472 | bytes 11534336 | tf_op jit(solution)/shard_map/dot_general | solution.py:122
  129.0 4.7 %all-to-all-start.3 = ((f32[16,16,3584]{2,1,0:T(8,128)}), f32[16,16,3584]{2,1,0:T(8,128)}, u32[]{:S(2)}, u32[]{:S(2)}) async-start(f32[16,16,3584]{2,1,0:T(8,128)} %bitcast.97), calls=%async_computation.3 | async-start | bytes 7340032 | tf_op jit(solution)/shard_map/all_to_all | solution.py:125
  136.5 2.5 %fusion.17 = (bf16[256,3584]{1,0:T(8,128)(2,1)S(1)}, bf16[256,3584]{1,0:T(8,128)(2,1)S(1)}) fusion(bf16[16,16,3584]{2,1,0:T(8,128)(2,1)} %all-to-all-done.1, f32[256]{0:T(256)S(1)} %bitcast.100, f32[256]{0:T(256)S(1)} %bitcast.101), kind=kLoop, calls=%fused_computation.33 | loop fusion | flops 4587520 | bytes 5507072 | tf_op jit(solution)/shard_map/convert_element_type | solution.py:93
  140.4 2.2 pad_maximum_fusion.2
  142.5 3.4 %pad_maximum_fusion = (bf16[2,3584,256]{2,1,0:T(8,128)(2,1)}, bf16[2,3584,256]{2,1,0:T(8,128)(2,1)}) fusion(bf16[1,3584,256]{2,1,0:T(8,128)(2,1)S(1)} %fusion.9, bf16[1,3584,256]{2,1,0:T(8,128)(2,1)S(1)} %fusion.8, bf16[1,3584,256]{2,1,0:T(8,128)(2,1)S(1)} %fusion.11, bf16[1,3584,256]{2,1,0:T(8,128)(2,1)S(1)} %fusion.10), kind=kLoop, calls=%fused_computation.24 | loop fusion | flops 3670016 | bytes 14680064 | tf_op jit(solution)/shard_map/stack | solution.py:138
  145.9 70.8 %all-to-all-done.3 = f32[16,16,3584]{2,1,0:T(8,128)} async-done(((f32[16,16,3584]{2,1,0:T(8,128)}), f32[16,16,3584]{2,1,0:T(8,128)}, u32[]{:S(2)}, u32[]{:S(2)}) %all-to-all-start.3) | async-done | bytes 3670048 | tf_op jit(solution)/shard_map/all_to_all | solution.py:125
  216.7 2.4 %bitcast_reduce_fusion = bf16[4,16,3584]{2,1,0:T(8,128)(2,1)S(1)} fusion(f32[16,16,3584]{2,1,0:T(8,128)} %all-to-all-done.3), kind=kLoop, calls=%fused_computation.35 | loop fusion | flops 688128 | bytes 4128768 | tf_op jit(solution)/shard_map/reduce_sum | solution.py:132
  219.1 1.0 fusion.14
  (44 shorter events, 11.0 us)
Async XLA Ops:
  0.6 10.7 %copy-start = (bf16[16,3584]{1,0:T(8,128)(2,1)S(1)}, bf16[16,3584]{1,0:T(8,128)(2,1)}, u32[]{:S(2)}) copy-start(bf16[16,3584]{1,0:T(8,128)(2,1)} %param.8) | copy-start | bytes 344068
  3.9 13.7 %all-to-all-start = ((bf16[16,16,2]{1,2,0:T(2,128)(2,1)}), bf16[16,16,2]{1,2,0:T(2,128)(2,1)S(1)}, u32[]{:S(2)}, u32[]{:S(2)}) async-start(bf16[16,16,2]{1,2,0:T(2,128)(2,1)} %bitcast.3), calls=%async_computation | async-start | bytes 16384 | tf_op jit(solution)/shard_map/all_to_all | solution.py:64
  19.0 3.9 %copy-start.7 = (bf16[16,3584]{1,0:T(8,128)(2,1)S(1)}, bf16[16,3584]{1,0:T(8,128)(2,1)}, u32[]{:S(2)}) copy-start(bf16[16,3584]{1,0:T(8,128)(2,1)} %param.7) | copy-start | bytes 344068
  19.0 47.6 %all-to-all-start.2 = ((bf16[16,16,3584]{2,1,0:T(8,128)(2,1)}), bf16[16,16,3584]{2,1,0:T(8,128)(2,1)S(1)}, u32[]{:S(2)}, u32[]{:S(2)}) async-start(bf16[16,16,3584]{2,1,0:T(8,128)(2,1)} %bitcast.96), calls=%async_computation.2 | async-start | bytes 3670016 | tf_op jit(solution)/shard_map/all_to_all | solution.py:50
  68.1 48.2 %all-to-all-start.1 = ((bf16[16,16,3584]{2,1,0:T(8,128)(2,1)}), bf16[16,16,3584]{2,1,0:T(8,128)(2,1)}, u32[]{:S(2)}, u32[]{:S(2)}) async-start(bf16[16,16,3584]{2,1,0:T(8,128)(2,1)} %bitcast.95), calls=%async_computation.1 | async-start | bytes 3670016 | tf_op jit(solution)/shard_map/all_to_all | solution.py:57
  79.1 2.6 %copy-start.1 = (bf16[2,3584,256]{2,1,0:T(8,128)(2,1)S(1)}, bf16[2,3584,256]{2,1,0:T(8,128)(2,1)}, u32[]{:S(2)}) copy-start(bf16[2,3584,256]{2,1,0:T(8,128)(2,1)} %param.10) | copy-start | bytes 11010052
  116.3 2.7 %copy-start.8 = (bf16[2,256,3584]{2,1,0:T(8,128)(2,1)S(1)}, bf16[2,256,3584]{2,1,0:T(8,128)(2,1)}, u32[]{:S(2)}) copy-start(bf16[2,256,3584]{2,1,0:T(8,128)(2,1)} %param.11) | copy-start | bytes 11010052
  119.7 2.0 copy-start.2
  121.7 1.9 copy-start.6
  122.6 1.6 copy-start.3
  122.7 2.2 copy-start.4
  122.7 2.7 %copy-start.5 = (bf16[3584,256]{1,0:T(8,128)(2,1)S(1)}, bf16[3584,256]{1,0:T(8,128)(2,1)}, u32[]{:S(2)}) copy-start(bf16[3584,256]{1,0:T(8,128)(2,1)} %get-tuple-element.24) | copy-start | bytes 5505028
  129.0 87.7 %all-to-all-start.3 = ((f32[16,16,3584]{2,1,0:T(8,128)}), f32[16,16,3584]{2,1,0:T(8,128)}, u32[]{:S(2)}, u32[]{:S(2)}) async-start(f32[16,16,3584]{2,1,0:T(8,128)} %bitcast.97), calls=%async_computation.3 | async-start | bytes 7340032 | tf_op jit(solution)/shard_map/all_to_all | solution.py:125
where the time goes:
time: 221 us; the launch traced here: 220 us
  waiting for transfers between devices  154 us (70%)
  starting transfers between devices  20.3 us (9%)
  matrix products  16.2 us (7%)
  other arithmetic  15.3 us (7%)
  local copies, waits for them, and re-layouts  13.5 us (6%)
    all_to_all x1, waiting for transfers between devices, per_device(): lax.all_to_all(partial_value.reshape(groups * local_count, capacity, mode...  70.8 us
    all_to_all x1, waiting for transfers between devices, per_device(): lax.all_to_all(spread_rows(send_input, groups, local_count), ('node', 'lo...  43.4 us
    all_to_all x1, waiting for transfers between devices, per_device(): lax.all_to_all(spread_rows(send_grad, groups, local_count), ('node', 'loc...  33.8 us
    all_to_all x1, starting transfers between devices, per_device(): lax.all_to_all(spread_rows(send_gate, groups, local_count), ('node', 'loc...  7.39 us
    squeeze x1, local copies, waits for them, and re-layouts, per_device(): gate_weight[expert]  6.31 us
    all_to_all x1, waiting for transfers between devices, per_device(): lax.all_to_all(spread_rows(send_gate, groups, local_count), ('node', 'loc...  5.9 us
    convert_element_type x2, other arithmetic, per_device(): scaled = (row_gates[:, expert:expert + 1].astype(jnp.float32) * row_grads...  5.13 us
    all_to_all x1, starting transfers between devices, per_device(): lax.all_to_all(partial_value.reshape(groups * local_count, capacity, mode...  4.69 us
  transfers between devices with their start and end apart: 4, of which 4 were waited for; matrix products, arithmetic and copies ran while one was open for 10% of the time, Pallas kernels for 0%

commit v1 on v0

--- a/solution.py
+++ b/solution.py
@@ -14,7 +14,7 @@
     return widened.reshape((groups * local_count,) + source.shape[1:])
 
 
-def per_device(grad_out, saved_input, gate_weight, up_weight, down_weight, expert_ids, gate_num):
+def slots_per_device(grad_out, saved_input, gate_weight, up_weight, down_weight, expert_ids, gate_num):
     tokens_here = grad_out.shape[0]
     model_width = grad_out.shape[1]
     groups = lax.axis_size("node")
@@ -138,7 +138,150 @@
     return (grad_input, jnp.stack(gate_grads), jnp.stack(up_grads), jnp.stack(down_grads))
 
 
+def ring_moves(local_count):
+    ring_len = 2 * local_count
+
+    def place(core, spot):
+        spot = spot % ring_len
+        if spot < local_count:
+            return core * local_count + spot
+        return (2 + core) * local_count + ring_len - 1 - spot
+
+    spots = range(ring_len)
+    forth = [(place(0, i), place(0, i + 1)) for i in spots]
+    forth += [(place(1, i), place(1, i - 1)) for i in spots]
+    back = [(there, here) for here, there in forth]
+    swap = [(place(core, i), place(1 - core, i)) for i in spots for core in (0, 1)]
+    return forth, back, swap
+
+
+def move(value, pairs):
+    return lax.ppermute(value, ("node", "local"), pairs)
+
+
+def gather_ring(mine, local_count, moves):
+    forth, _, swap = moves
+    rows = mine.shape[0]
+    other = move(mine, swap)
+    block = jnp.concatenate([mine, other], axis=0)
+    near = [mine]
+    far = [other]
+    for _ in range(local_count - 1):
+        block = move(block, forth)
+        near.append(block)
+        far.append(move(block, swap))
+    last = move(block[:rows], forth)
+    near.append(last)
+    far.append(move(last, swap))
+    return jnp.concatenate(near + far, axis=0)
+
+
+def reduce_ring(partial_value, local_count, moves):
+    _, back, swap = moves
+    total_rows = partial_value.shape[0]
+    half = total_rows // 2
+    rows = half // (2 * local_count)
+    wide = jnp.float32
+    from_other = move(partial_value[half:], swap)
+
+    def own(start, count):
+        return partial_value[start : start + count].astype(wide) + from_other[
+            start : start + count
+        ].astype(wide)
+
+    start = half - rows
+    moving = move(own(start, rows).astype(jnp.bfloat16), back)
+    for _ in range(local_count - 1):
+        start -= 2 * rows
+        held = own(start, 2 * rows)
+        arrived = moving.astype(wide)
+        if arrived.shape[0] == rows:
+            held = jnp.concatenate([held[:rows] + arrived, held[rows:]], axis=0)
+        else:
+            held = held + arrived
+        moving = move(held.astype(jnp.bfloat16), back)
+    crossed = move(moving[rows:], swap)
+    return (own(0, rows) + moving[:rows].astype(wide) + crossed.astype(wide)).astype(jnp.bfloat16)
+
+
+def ring_per_device(
+    grad_out, saved_input, gate_weight, up_weight, down_weight, expert_ids, gate_num
+):
+    model_width = grad_out.shape[1]
+    groups = lax.axis_size("node")
+    local_count = lax.axis_size("local")
+    experts_here = gate_weight.shape[0]
+    experts = groups * experts_here
+    moves = ring_moves(local_count)
+    expert_hot = expert_ids[:, :, None] == jnp.arange(128, dtype=jnp.int32)[None, None, :]
+    gates = jnp.sum(
+        jnp.where(expert_hot, (gate_num.astype(jnp.float32) * gate_scale)[:, :, None], 0.0), axis=1
+    ).astype(jnp.bfloat16)
+    grads_gates = jnp.concatenate([grad_out, gates], axis=1)
+    inputs = gather_ring(saved_input, local_count, moves)
+    rows_all = gather_ring(grads_gates, local_count, moves)
+    row_grads = rows_all[:, :model_width]
+    row_gates = rows_all[:, model_width:]
+    first = lax.axis_index("node") * experts_here
+    column = jnp.arange(128, dtype=jnp.int32)[None, :]
+    contract_rows = (((0,), (0,)), ((), ()))
+    contract_cols = (((1,), (1,)), ((), ()))
+    gate_grads = []
+    up_grads = []
+    down_grads = []
+    partial_value = None
+    for expert in range(experts_here):
+        gate = jnp.sum(
+            jnp.where(column == first + expert, row_gates.astype(jnp.float32), 0.0),
+            axis=1,
+            keepdims=True,
+        )
+        gate_act = jnp.dot(inputs, gate_weight[expert], preferred_element_type=jnp.float32)
+        up_act = jnp.dot(inputs, up_weight[expert], preferred_element_type=jnp.float32)
+        sigmoid_val = jax.nn.sigmoid(gate_act)
+        hidden = (gate * gate_act * sigmoid_val * up_act).astype(jnp.bfloat16)
+        down_grads.append(
+            lax.dot_general(
+                hidden, row_grads, contract_rows, preferred_element_type=jnp.float32
+            ).astype(jnp.bfloat16)
+        )
+        back_grad = gate * lax.dot_general(
+            row_grads, down_weight[expert], contract_cols, preferred_element_type=jnp.float32
+        )
+        grad_gate_act = (
+            back_grad * up_act * sigmoid_val * (1.0 + gate_act * (1.0 - sigmoid_val))
+        ).astype(jnp.bfloat16)
+        grad_up_act = (back_grad * gate_act * sigmoid_val).astype(jnp.bfloat16)
+        gate_grads.append(
+            lax.dot_general(
+                inputs, grad_gate_act, contract_rows, preferred_element_type=jnp.float32
+            ).astype(jnp.bfloat16)
+        )
+        up_grads.append(
+            lax.dot_general(
+                inputs, grad_up_act, contract_rows, preferred_element_type=jnp.float32
+            ).astype(jnp.bfloat16)
+        )
+        for grad, weight in ((grad_gate_act, gate_weight), (grad_up_act, up_weight)):
+            term = lax.dot_general(
+                grad, weight[expert], contract_cols, preferred_element_type=jnp.float32
+            )
+            partial_value = term if partial_value is None else partial_value + term
+    partial_value = partial_value.astype(jnp.bfloat16)
+    parts = 2
+    width = model_width // parts
+    grad_input = jnp.concatenate(
+        [
+            reduce_ring(partial_value[:, i * width : (i + 1) * width], local_count, moves)
+            for i in range(parts)
+        ],
+        axis=1,
+    )
+    return (grad_input, jnp.stack(gate_grads), jnp.stack(up_grads), jnp.stack(down_grads))
+
+
 def solution(mesh):
+    per_device = ring_per_device if mesh.shape["node"] == LIMIT else slots_per_device
     in_specs = (
         P(("rep", "node", "local"), None),
         P(("rep", "node", "local"), None),

time: 221 us -> 97.3 us (0.44)
  waiting for transfers between devices: 154 us -> 32.1 us
  starting transfers between devices: 20.3 us -> 28.7 us
  matrix products: 16.2 us -> 12.7 us
  other arithmetic: 15.3 us -> 11.8 us
  local copies, waits for them, and re-layouts: 13.5 us -> 10.6 us
    all_to_all x4 -> x0, waiting for transfers between devices: 154 us -> none  [the longest x1 70.8 us: per_device(): lax.all_to_all(partial_value.reshape(groups * local_count, capacity, mode...]
    ppermute x0 -> x30, waiting for transfers between devices: none -> 32.1 us  [move(): return lax.ppermute(value, ('node', 'local'), pairs)]
    ppermute x0 -> x30, starting transfers between devices: none -> 28.7 us  [move(): return lax.ppermute(value, ('node', 'local'), pairs)]
    all_to_all x4 -> x0, starting transfers between devices: 20.3 us -> none  [the longest x1 7.39 us: per_device(): lax.all_to_all(spread_rows(send_gate, groups, local_count), ('node', 'loc...]
    unnamed x18 -> x25, local copies, waits for them, and re-layouts: 3.26 us -> 9.85 us
    squeeze x1 -> x0, local copies, waits for them, and re-layouts: 6.31 us -> none  [per_device(): gate_weight[expert]]
    convert_element_type x4 -> x7, other arithmetic: 5.16 us -> 0.3 us  [the longest x4 0.21 us: reduce_ring(): moving = move(held.astype(jnp.bfloat16), back)]
    dot_general x17 -> x16, matrix products: 16.2 us -> 12.7 us  [the longest x2 2.91 us: ring_per_device(): jnp.dot(inputs, gate_weight[expert], preferred_element_type=jnp.float32)]
  transfers between devices with their start and end apart: 4 -> 30, of which waited for: 4 -> 18; matrix products, arithmetic and copies ran while one was open for 10% -> 28% of each run, Pallas kernels for 0% -> 0%
where the time goes in v1:
time: 97.3 us; the launch traced here: 96.9 us
  waiting for transfers between devices  32.1 us (33%)
  starting transfers between devices  28.7 us (29%)
  matrix products  12.7 us (13%)
  other arithmetic  11.8 us (12%)
  local copies, waits for them, and re-layouts  10.6 us (11%)
  between operations  1 us (1%)
    ppermute x30, waiting for transfers between devices, move(): return lax.ppermute(value, ('node', 'local'), pairs)  32.1 us
    ppermute x30, starting transfers between devices, move(): return lax.ppermute(value, ('node', 'local'), pairs)  28.7 us
    unnamed x25, local copies, waits for them, and re-layouts  9.85 us
    dot_general x2, matrix products, ring_per_device(): jnp.dot(inputs, gate_weight[expert], preferred_element_type=jnp.float32)  2.91 us
    dot_general x4, matrix products, ring_per_device(): lax.dot_general(grad, weight[expert], contract_cols, preferred_element_ty...  2.83 us
    another operation x1, other arithmetic, ring_per_device(): jnp.stack(down_grads)  2.15 us
    another operation x1, other arithmetic, ring_per_device(): jnp.stack(gate_grads)  2.15 us
    another operation x1, other arithmetic, ring_per_device(): jnp.stack(up_grads)  2.15 us
  transfers between devices with their start and end apart: 30, of which 18 were waited for; matrix products, arithmetic and copies ran while one was open for 28% of the time, Pallas kernels for 0%

profile of v1, /device:TPU:0, one launch (start us, length us, event | category | flops | bytes accessed | tf_op | source)
XLA Modules:
  0.0 96.9 jit_solution(17867687129136402053)
XLA Ops:
  3.7 1.6 %constant_dynamic-update-slice_fusion.19 = bf16[256,3584]{1,0:T(8,128)(2,1)} fusion(bf16[16,3584]{1,0:T(8,128)(2,1)} %param.8), kind=kLoop, calls=%fused_computation.111 | loop fusion | bytes 229376
  6.1 3.1 %collective-permute-start.10 = (bf16[32,3584]{1,0:T(8,128)(2,1)S(1)}, bf16[32,3584]{1,0:T(8,128)(2,1)S(1)}, u32[]{:S(2)}, u32[]{:S(2)}) collective-permute-start(bf16[32,3584]{1,0:T(8,128)(2,1)S(1)} %pad_maximum_fusion.4), channel_id=1, source_target_pairs={{0,1},{1,2},{2,3},{3,11},{11,10},{10,9},{9,8},{8,0},{4,12},{5,4},{... | collective-permute-start | bytes 688136 | tf_op jit(solution)/shard_map/ppermute | solution.py:159
  10.1 1.6 %collective-permute-start.1 = (bf16[32,3712]{1,0:T(8,128)(2,1)S(1)}, bf16[32,3712]{1,0:T(8,128)(2,1)S(1)}, u32[]{:S(2)}, u32[]{:S(2)}) collective-permute-start(bf16[32,3712]{1,0:T(8,128)(2,1)S(1)} %pad_maximum_fusion.3), channel_id=1, source_target_pairs={{0,1},{1,2},{2,3},{3,11},{11,10},{10,9},{9,8},{8,0},{4,12},{5,4},{... | collective-permute-start | bytes 712712 | tf_op jit(solution)/shard_map/ppermute | solution.py:159
  13.2 2.1 %collective-permute-start.11 = (bf16[32,3584]{1,0:T(8,128)(2,1)S(1)}, bf16[32,3584]{1,0:T(8,128)(2,1)S(1)}, u32[]{:S(2)}, u32[]{:S(2)}) collective-permute-start(bf16[32,3584]{1,0:T(8,128)(2,1)S(1)} %collective-permute-done.10), channel_id=1, source_target_pairs={{0,1},{1,2},{2,3},{3,11},{11,10},{10,9},{9,8},{8,0},{4,12},{5,4},{... | collective-permute-start | bytes 688136 | tf_op jit(solution)/shard_map/ppermute | solution.py:159
  16.3 1.6 %collective-permute-start.2 = (bf16[32,3712]{1,0:T(8,128)(2,1)S(1)}, bf16[32,3712]{1,0:T(8,128)(2,1)S(1)}, u32[]{:S(2)}, u32[]{:S(2)}) collective-permute-start(bf16[32,3712]{1,0:T(8,128)(2,1)S(1)} %collective-permute-done.1), channel_id=1, source_target_pairs={{0,1},{1,2},{2,3},{3,11},{11,10},{10,9},{9,8},{8,0},{4,12},{5,4},{... | collective-permute-start | bytes 712712 | tf_op jit(solution)/shard_map/ppermute | solution.py:159
  19.2 2.1 %collective-permute-start.12 = (bf16[32,3584]{1,0:T(8,128)(2,1)S(1)}, bf16[32,3584]{1,0:T(8,128)(2,1)S(1)}, u32[]{:S(2)}, u32[]{:S(2)}) collective-permute-start(bf16[32,3584]{1,0:T(8,128)(2,1)S(1)} %collective-permute-done.11), channel_id=1, source_target_pairs={{0,1},{1,2},{2,3},{3,11},{11,10},{10,9},{9,8},{8,0},{4,12},{5,4},{... | collective-permute-start | bytes 688136 | tf_op jit(solution)/shard_map/ppermute | solution.py:159
  22.4 1.6 %collective-permute-start.3 = (bf16[32,3712]{1,0:T(8,128)(2,1)S(1)}, bf16[32,3712]{1,0:T(8,128)(2,1)S(1)}, u32[]{:S(2)}, u32[]{:S(2)}) collective-permute-start(bf16[32,3712]{1,0:T(8,128)(2,1)S(1)} %collective-permute-done.2), channel_id=1, source_target_pairs={{0,1},{1,2},{2,3},{3,11},{11,10},{10,9},{9,8},{8,0},{4,12},{5,4},{... | collective-permute-start | bytes 712712 | tf_op jit(solution)/shard_map/ppermute | solution.py:159
  25.9 2.6 %collective-permute-done.3 = bf16[32,3712]{1,0:T(8,128)(2,1)S(1)} collective-permute-done((bf16[32,3712]{1,0:T(8,128)(2,1)S(1)}, bf16[32,3712]{1,0:T(8,128)(2,1)S(1)}, u32[]{:S(2)}, u32[]{:S(2)}) %collective-permute-start.3) | collective-permute-done | bytes 237600 | tf_op jit(solution)/shard_map/ppermute | solution.py:159
  28.5 1.6 %collective-permute-start.13 = (bf16[16,3584]{1,0:T(8,128)(2,1)S(1)}, bf16[16,3584]{1,0:T(8,128)(2,1)S(1)}, u32[]{:S(2)}, u32[]{:S(2)}) collective-permute-start(bf16[16,3584]{1,0:T(8,128)(2,1)S(1)} %slice.183), channel_id=1, source_target_pairs={{0,1},{1,2},{2,3},{3,11},{11,10},{10,9},{9,8},{8,0},{4,12},{5,4},{... | collective-permute-start | bytes 344072 | tf_op jit(solution)/shard_map/ppermute | solution.py:159
  30.1 3.2 %collective-permute-done.13 = bf16[16,3584]{1,0:T(8,128)(2,1)S(1)} collective-permute-done((bf16[16,3584]{1,0:T(8,128)(2,1)S(1)}, bf16[16,3584]{1,0:T(8,128)(2,1)S(1)}, u32[]{:S(2)}, u32[]{:S(2)}) %collective-permute-start.13) | collective-permute-done | bytes 114720 | tf_op jit(solution)/shard_map/ppermute | solution.py:159
  34.6 1.6 %collective-permute-start.4 = (bf16[16,3712]{1,0:T(8,128)(2,1)S(1)}, bf16[16,3712]{1,0:T(8,128)(2,1)S(1)}, u32[]{:S(2)}, u32[]{:S(2)}) collective-permute-start(bf16[16,3712]{1,0:T(8,128)(2,1)S(1)} %slice.180), channel_id=1, source_target_pairs={{0,1},{1,2},{2,3},{3,11},{11,10},{10,9},{9,8},{8,0},{4,12},{5,4},{... | collective-permute-start | bytes 356360 | tf_op jit(solution)/shard_map/ppermute | solution.py:159
  37.7 1.8 %collective-permute-done.4 = bf16[16,3712]{1,0:T(8,128)(2,1)S(1)} collective-permute-done((bf16[16,3712]{1,0:T(8,128)(2,1)S(1)}, bf16[16,3712]{1,0:T(8,128)(2,1)S(1)}, u32[]{:S(2)}, u32[]{:S(2)}) %collective-permute-start.4) | collective-permute-done | bytes 118816 | tf_op jit(solution)/shard_map/ppermute | solution.py:159
  41.5 2.3 %fusion.17 = f32[256,256]{1,0:T(8,128)S(1)} fusion(bf16[256,3584]{1,0:T(8,128)(2,1)} %constant_dynamic-update-slice_fusion.10, bf16[2,3584,256]{2,1,0:T(8,128)(2,1)S(1)} %copy-done.1), kind=kOutput, calls=%fused_computation.29 | convolution fusion | flops 469762048 | bytes 3932160 | tf_op jit(solution)/shard_map/dot_general | solution.py:239
  53.0 1.7 %collective-permute-done.18 = bf16[128,1792]{1,0:T(8,128)(2,1)S(1)} collective-permute-done((bf16[128,1792]{1,0:T(8,128)(2,1)S(1)}, bf16[128,1792]{1,0:T(8,128)(2,1)S(1)}, u32[]{:S(2)}, u32[]{:S(2)}) %collective-permute-start.18) | collective-permute-done | bytes 458784 | tf_op jit(solution)/shard_map/ppermute | solution.py:159
  56.3 2.7 %collective-permute-done.19 = bf16[16,1792]{1,0:T(8,128)(2,1)S(1)} collective-permute-done((bf16[16,1792]{1,0:T(8,128)(2,1)S(1)}, bf16[16,1792]{1,0:T(8,128)(2,1)S(1)}, u32[]{:S(2)}, u32[]{:S(2)}) %collective-permute-start.19) | collective-permute-done | bytes 57376 | tf_op jit(solution)/shard_map/ppermute | solution.py:159
  61.3 2.6 %collective-permute-done.20 = bf16[32,1792]{1,0:T(8,128)(2,1)S(1)} collective-permute-done((bf16[32,1792]{1,0:T(8,128)(2,1)S(1)}, bf16[32,1792]{1,0:T(8,128)(2,1)S(1)}, u32[]{:S(2)}, u32[]{:S(2)}) %collective-permute-start.20) | collective-permute-done | bytes 114720 | tf_op jit(solution)/shard_map/ppermute | solution.py:159
  66.1 2.7 %collective-permute-done.21 = bf16[32,1792]{1,0:T(8,128)(2,1)S(1)} collective-permute-done((bf16[32,1792]{1,0:T(8,128)(2,1)S(1)}, bf16[32,1792]{1,0:T(8,128)(2,1)S(1)}, u32[]{:S(2)}, u32[]{:S(2)}) %collective-permute-start.21) | collective-permute-done | bytes 114720 | tf_op jit(solution)/shard_map/ppermute | solution.py:159
  70.3 2.2 %pad_maximum_fusion = bf16[2,3584,256]{2,1,0:T(8,128)(2,1)} fusion(bf16[1,3584,256]{2,1,0:T(8,128)(2,1)S(1)} %fusion.2, bf16[1,3584,256]{2,1,0:T(8,128)(2,1)S(1)} %fusion.1), kind=kLoop, calls=%fused_computation.16 | loop fusion | flops 1835008 | bytes 7340032 | tf_op jit(solution)/shard_map/stack | solution.py:280
  77.2 2.0 %collective-permute-done.25 = bf16[16,1792]{1,0:T(8,128)(2,1)S(1)} collective-permute-done((bf16[16,1792]{1,0:T(8,128)(2,1)S(1)}, bf16[16,1792]{1,0:T(8,128)(2,1)S(1)}, u32[]{:S(2)}, u32[]{:S(2)}) %collective-permute-start.25) | collective-permute-done | bytes 57376 | tf_op jit(solution)/shard_map/ppermute | solution.py:159
  79.3 1.7 %collective-permute-start.26 = (bf16[32,1792]{1,0:T(8,128)(2,1)S(1)}, bf16[32,1792]{1,0:T(8,128)(2,1)S(1)}, u32[]{:S(2)}, u32[]{:S(2)}) collective-permute-start(bf16[32,1792]{1,0:T(8,128)(2,1)S(1)} %pad_maximum_fusion.7), channel_id=1, source_target_pairs={{1,0},{2,1},{3,2},{11,3},{10,11},{9,10},{8,9},{0,8},{12,4},{4,5},{... | collective-permute-start | bytes 344072 | tf_op jit(solution)/shard_map/ppermute | solution.py:159
  80.9 2.2 %pad_maximum_fusion.1 = bf16[2,3584,256]{2,1,0:T(8,128)(2,1)} fusion(bf16[1,3584,256]{2,1,0:T(8,128)(2,1)S(1)} %fusion.4, bf16[1,3584,256]{2,1,0:T(8,128)(2,1)S(1)} %fusion.3), kind=kLoop, calls=%fused_computation.17 | loop fusion | flops 1835008 | bytes 7340032 | tf_op jit(solution)/shard_map/stack | solution.py:280
  86.6 2.6 %collective-permute-done.27 = bf16[32,1792]{1,0:T(8,128)(2,1)S(1)} collective-permute-done((bf16[32,1792]{1,0:T(8,128)(2,1)S(1)}, bf16[32,1792]{1,0:T(8,128)(2,1)S(1)}, u32[]{:S(2)}, u32[]{:S(2)}) %collective-permute-start.27) | collective-permute-done | bytes 114720 | tf_op jit(solution)/shard_map/ppermute | solution.py:159
  91.5 2.6 %collective-permute-done.28 = bf16[32,1792]{1,0:T(8,128)(2,1)S(1)} collective-permute-done((bf16[32,1792]{1,0:T(8,128)(2,1)S(1)}, bf16[32,1792]{1,0:T(8,128)(2,1)S(1)}, u32[]{:S(2)}, u32[]{:S(2)}) %collective-permute-start.28) | collective-permute-done | bytes 114720 | tf_op jit(solution)/shard_map/ppermute | solution.py:159
  94.1 2.2 %pad_maximum_fusion.2 = bf16[2,256,3584]{2,1,0:T(8,128)(2,1)} fusion(bf16[1,256,3584]{2,1,0:T(8,128)(2,1)S(1)} %fusion.6, bf16[1,256,3584]{2,1,0:T(8,128)(2,1)S(1)} %fusion.5), kind=kLoop, calls=%fused_computation.18 | loop fusion | flops 1835008 | bytes 7340032 | tf_op jit(solution)/shard_map/stack | solution.py:280
  (109 shorter events, 44.4 us)
Async XLA Ops:
  0.6 4.6 %collective-permute-start.9 = (bf16[16,3584]{1,0:T(8,128)(2,1)}, bf16[16,3584]{1,0:T(8,128)(2,1)S(1)}, u32[]{:S(2)}, u32[]{:S(2)}) collective-permute-start(bf16[16,3584]{1,0:T(8,128)(2,1)} %param.8), channel_id=1, source_target_pairs={{0,4},{4,0},{1,5},{5,1},{2,6},{6,2},{3,7},{7,3},{11,15},{15,11},{1... | collective-permute-start | bytes 344072 | tf_op jit(solution)/shard_map/ppermute | solution.py:159
  3.5 5.7 %collective-permute-start = (bf16[16,3712]{1,0:T(8,128)(2,1)S(1)}, bf16[16,3712]{1,0:T(8,128)(2,1)S(1)}, u32[]{:S(2)}, u32[]{:S(2)}) collective-permute-start(bf16[16,3712]{1,0:T(8,128)(2,1)S(1)} %get-tuple-element.16), channel_id=1, source_target_pairs={{0,4},{4,0},{1,5},{5,1},{2,6},{6,2},{3,7},{7,3},{11,15},{15,11},{1... | collective-permute-start | bytes 356360 | tf_op jit(solution)/shard_map/ppermute | solution.py:159
  6.1 7.0 %collective-permute-start.10 = (bf16[32,3584]{1,0:T(8,128)(2,1)S(1)}, bf16[32,3584]{1,0:T(8,128)(2,1)S(1)}, u32[]{:S(2)}, u32[]{:S(2)}) collective-permute-start(bf16[32,3584]{1,0:T(8,128)(2,1)S(1)} %pad_maximum_fusion.4), channel_id=1, source_target_pairs={{0,1},{1,2},{2,3},{3,11},{11,10},{10,9},{9,8},{8,0},{4,12},{5,4},{... | collective-permute-start | bytes 688136 | tf_op jit(solution)/shard_map/ppermute | solution.py:159
  10.1 6.2 %collective-permute-start.1 = (bf16[32,3712]{1,0:T(8,128)(2,1)S(1)}, bf16[32,3712]{1,0:T(8,128)(2,1)S(1)}, u32[]{:S(2)}, u32[]{:S(2)}) collective-permute-start(bf16[32,3712]{1,0:T(8,128)(2,1)S(1)} %pad_maximum_fusion.3), channel_id=1, source_target_pairs={{0,1},{1,2},{2,3},{3,11},{11,10},{10,9},{9,8},{8,0},{4,12},{5,4},{... | collective-permute-start | bytes 712712 | tf_op jit(solution)/shard_map/ppermute | solution.py:159
  13.2 6.0 %collective-permute-start.11 = (bf16[32,3584]{1,0:T(8,128)(2,1)S(1)}, bf16[32,3584]{1,0:T(8,128)(2,1)S(1)}, u32[]{:S(2)}, u32[]{:S(2)}) collective-permute-start(bf16[32,3584]{1,0:T(8,128)(2,1)S(1)} %collective-permute-done.10), channel_id=1, source_target_pairs={{0,1},{1,2},{2,3},{3,11},{11,10},{10,9},{9,8},{8,0},{4,12},{5,4},{... | collective-permute-start | bytes 688136 | tf_op jit(solution)/shard_map/ppermute | solution.py:159
  15.2 19.4 %collective-permute-start.14 = (bf16[32,3584]{1,0:T(8,128)(2,1)S(1)}, bf16[32,3584]{1,0:T(8,128)(2,1)S(1)}, u32[]{:S(2)}, u32[]{:S(2)}) collective-permute-start(bf16[32,3584]{1,0:T(8,128)(2,1)S(1)} %collective-permute-done.10), channel_id=1, source_target_pairs={{0,4},{4,0},{1,5},{5,1},{2,6},{6,2},{3,7},{7,3},{11,15},{15,11},{1... | collective-permute-start | bytes 688136 | tf_op jit(solution)/shard_map/ppermute | solution.py:159
  16.3 6.1 %collective-permute-start.2 = (bf16[32,3712]{1,0:T(8,128)(2,1)S(1)}, bf16[32,3712]{1,0:T(8,128)(2,1)S(1)}, u32[]{:S(2)}, u32[]{:S(2)}) collective-permute-start(bf16[32,3712]{1,0:T(8,128)(2,1)S(1)} %collective-permute-done.1), channel_id=1, source_target_pairs={{0,1},{1,2},{2,3},{3,11},{11,10},{10,9},{9,8},{8,0},{4,12},{5,4},{... | collective-permute-start | bytes 712712 | tf_op jit(solution)/shard_map/ppermute | solution.py:159
  17.9 21.6 %collective-permute-start.5 = (bf16[32,3712]{1,0:T(8,128)(2,1)S(1)}, bf16[32,3712]{1,0:T(8,128)(2,1)S(1)}, u32[]{:S(2)}, u32[]{:S(2)}) collective-permute-start(bf16[32,3712]{1,0:T(8,128)(2,1)S(1)} %collective-permute-done.1), channel_id=1, source_target_pairs={{0,4},{4,0},{1,5},{5,1},{2,6},{6,2},{3,7},{7,3},{11,15},{15,11},{1... | collective-permute-start | bytes 712712 | tf_op jit(solution)/shard_map/ppermute | solution.py:159
  19.2 6.0 %collective-permute-start.12 = (bf16[32,3584]{1,0:T(8,128)(2,1)S(1)}, bf16[32,3584]{1,0:T(8,128)(2,1)S(1)}, u32[]{:S(2)}, u32[]{:S(2)}) collective-permute-start(bf16[32,3584]{1,0:T(8,128)(2,1)S(1)} %collective-permute-done.11), channel_id=1, source_target_pairs={{0,1},{1,2},{2,3},{3,11},{11,10},{10,9},{9,8},{8,0},{4,12},{5,4},{... | collective-permute-start | bytes 688136 | tf_op jit(solution)/shard_map/ppermute | solution.py:159
  21.3 15.7 %collective-permute-start.15 = (bf16[32,3584]{1,0:T(8,128)(2,1)S(1)}, bf16[32,3584]{1,0:T(8,128)(2,1)S(1)}, u32[]{:S(2)}, u32[]{:S(2)}) collective-permute-start(bf16[32,3584]{1,0:T(8,128)(2,1)S(1)} %collective-permute-done.11), channel_id=1, source_target_pairs={{0,4},{4,0},{1,5},{5,1},{2,6},{6,2},{3,7},{7,3},{11,15},{15,11},{1... | collective-permute-start | bytes 688136 | tf_op jit(solution)/shard_map/ppermute | solution.py:159
  22.4 6.1 %collective-permute-start.3 = (bf16[32,3712]{1,0:T(8,128)(2,1)S(1)}, bf16[32,3712]{1,0:T(8,128)(2,1)S(1)}, u32[]{:S(2)}, u32[]{:S(2)}) collective-permute-start(bf16[32,3712]{1,0:T(8,128)(2,1)S(1)} %collective-permute-done.2), channel_id=1, source_target_pairs={{0,1},{1,2},{2,3},{3,11},{11,10},{10,9},{9,8},{8,0},{4,12},{5,4},{... | collective-permute-start | bytes 712712 | tf_op jit(solution)/shard_map/ppermute | solution.py:159
  25.2 14.9 %collective-permute-start.6 = (bf16[32,3712]{1,0:T(8,128)(2,1)S(1)}, bf16[32,3712]{1,0:T(8,128)(2,1)S(1)}, u32[]{:S(2)}, u32[]{:S(2)}) collective-permute-start(bf16[32,3712]{1,0:T(8,128)(2,1)S(1)} %collective-permute-done.2), channel_id=1, source_target_pairs={{0,4},{4,0},{1,5},{5,1},{2,6},{6,2},{3,7},{7,3},{11,15},{15,11},{1... | collective-permute-start | bytes 712712 | tf_op jit(solution)/shard_map/ppermute | solution.py:159
  28.5 4.8 %collective-permute-start.13 = (bf16[16,3584]{1,0:T(8,128)(2,1)S(1)}, bf16[16,3584]{1,0:T(8,128)(2,1)S(1)}, u32[]{:S(2)}, u32[]{:S(2)}) collective-permute-start(bf16[16,3584]{1,0:T(8,128)(2,1)S(1)} %slice.183), channel_id=1, source_target_pairs={{0,1},{1,2},{2,3},{3,11},{11,10},{10,9},{9,8},{8,0},{4,12},{5,4},{... | collective-permute-start | bytes 344072 | tf_op jit(solution)/shard_map/ppermute | solution.py:159
  33.3 6.8 %collective-permute-start.16 = (bf16[32,3584]{1,0:T(8,128)(2,1)S(1)}, bf16[32,3584]{1,0:T(8,128)(2,1)S(1)}, u32[]{:S(2)}, u32[]{:S(2)}) collective-permute-start(bf16[32,3584]{1,0:T(8,128)(2,1)S(1)} %collective-permute-done.12), channel_id=1, source_target_pairs={{0,4},{4,0},{1,5},{5,1},{2,6},{6,2},{3,7},{7,3},{11,15},{15,11},{1... | collective-permute-start | bytes 688136 | tf_op jit(solution)/shard_map/ppermute | solution.py:159
  34.6 4.8 %collective-permute-start.4 = (bf16[16,3712]{1,0:T(8,128)(2,1)S(1)}, bf16[16,3712]{1,0:T(8,128)(2,1)S(1)}, u32[]{:S(2)}, u32[]{:S(2)}) collective-permute-start(bf16[16,3712]{1,0:T(8,128)(2,1)S(1)} %slice.180), channel_id=1, source_target_pairs={{0,1},{1,2},{2,3},{3,11},{11,10},{10,9},{9,8},{8,0},{4,12},{5,4},{... | collective-permute-start | bytes 356360 | tf_op jit(solution)/shard_map/ppermute | solution.py:159
  36.9 10.3 %collective-permute-start.7 = (bf16[32,3712]{1,0:T(8,128)(2,1)S(1)}, bf16[32,3712]{1,0:T(8,128)(2,1)S(1)}, u32[]{:S(2)}, u32[]{:S(2)}) collective-permute-start(bf16[32,3712]{1,0:T(8,128)(2,1)S(1)} %collective-permute-done.3), channel_id=1, source_target_pairs={{0,4},{4,0},{1,5},{5,1},{2,6},{6,2},{3,7},{7,3},{11,15},{15,11},{1... | collective-permute-start | bytes 712712 | tf_op jit(solution)/shard_map/ppermute | solution.py:159
  39.5 7.7 %collective-permute-start.8 = (bf16[16,3712]{1,0:T(8,128)(2,1)S(1)}, bf16[16,3712]{1,0:T(8,128)(2,1)S(1)}, u32[]{:S(2)}, u32[]{:S(2)}) collective-permute-start(bf16[16,3712]{1,0:T(8,128)(2,1)S(1)} %collective-permute-done.4), channel_id=1, source_target_pairs={{0,4},{4,0},{1,5},{5,1},{2,6},{6,2},{3,7},{7,3},{11,15},{15,11},{1... | collective-permute-start | bytes 356360 | tf_op jit(solution)/shard_map/ppermute | solution.py:159
  59.0 4.8 %collective-permute-start.20 = (bf16[32,1792]{1,0:T(8,128)(2,1)S(1)}, bf16[32,1792]{1,0:T(8,128)(2,1)S(1)}, u32[]{:S(2)}, u32[]{:S(2)}) collective-permute-start(bf16[32,1792]{1,0:T(8,128)(2,1)S(1)} %pad_maximum_fusion.6), channel_id=1, source_target_pairs={{1,0},{2,1},{3,2},{11,3},{10,11},{9,10},{8,9},{0,8},{12,4},{4,5},{... | collective-permute-start | bytes 344072 | tf_op jit(solution)/shard_map/ppermute | solution.py:159
  61.2 4.9 %collective-permute-start.24 = (bf16[128,1792]{1,0:T(8,128)(2,1)S(1)}, bf16[128,1792]{1,0:T(8,128)(2,1)S(1)}, u32[]{:S(2)}, u32[]{:S(2)}) collective-permute-start(bf16[128,1792]{1,0:T(8,128)(2,1)S(1)} %get-tuple-element.11), channel_id=1, source_target_pairs={{0,4},{4,0},{1,5},{5,1},{2,6},{6,2},{3,7},{7,3},{11,15},{15,11},{1... | collective-permute-start | bytes 1376264 | tf_op jit(solution)/shard_map/ppermute | solution.py:159
  63.9 4.8 %collective-permute-start.21 = (bf16[32,1792]{1,0:T(8,128)(2,1)S(1)}, bf16[32,1792]{1,0:T(8,128)(2,1)S(1)}, u32[]{:S(2)}, u32[]{:S(2)}) collective-permute-start(bf16[32,1792]{1,0:T(8,128)(2,1)S(1)} %add_convert_fusion.3), channel_id=1, source_target_pairs={{1,0},{2,1},{3,2},{11,3},{10,11},{9,10},{8,9},{0,8},{12,4},{4,5},{... | collective-permute-start | bytes 344072 | tf_op jit(solution)/shard_map/ppermute | solution.py:159
  68.9 4.8 %collective-permute-start.22 = (bf16[32,1792]{1,0:T(8,128)(2,1)S(1)}, bf16[32,1792]{1,0:T(8,128)(2,1)S(1)}, u32[]{:S(2)}, u32[]{:S(2)}) collective-permute-start(bf16[32,1792]{1,0:T(8,128)(2,1)S(1)} %get-tuple-element.8), channel_id=1, source_target_pairs={{1,0},{2,1},{3,2},{11,3},{10,11},{9,10},{8,9},{0,8},{12,4},{4,5},{... | collective-permute-start | bytes 344072 | tf_op jit(solution)/shard_map/ppermute | solution.py:159
  79.3 5.0 %collective-permute-start.26 = (bf16[32,1792]{1,0:T(8,128)(2,1)S(1)}, bf16[32,1792]{1,0:T(8,128)(2,1)S(1)}, u32[]{:S(2)}, u32[]{:S(2)}) collective-permute-start(bf16[32,1792]{1,0:T(8,128)(2,1)S(1)} %pad_maximum_fusion.7), channel_id=1, source_target_pairs={{1,0},{2,1},{3,2},{11,3},{10,11},{9,10},{8,9},{0,8},{12,4},{4,5},{... | collective-permute-start | bytes 344072 | tf_op jit(solution)/shard_map/ppermute | solution.py:159
  84.3 4.8 %collective-permute-start.27 = (bf16[32,1792]{1,0:T(8,128)(2,1)S(1)}, bf16[32,1792]{1,0:T(8,128)(2,1)S(1)}, u32[]{:S(2)}, u32[]{:S(2)}) collective-permute-start(bf16[32,1792]{1,0:T(8,128)(2,1)S(1)} %add_convert_fusion.1), channel_id=1, source_target_pairs={{1,0},{2,1},{3,2},{11,3},{10,11},{9,10},{8,9},{0,8},{12,4},{4,5},{... | collective-permute-start | bytes 344072 | tf_op jit(solution)/shard_map/ppermute | solution.py:159
  89.2 4.8 %collective-permute-start.28 = (bf16[32,1792]{1,0:T(8,128)(2,1)S(1)}, bf16[32,1792]{1,0:T(8,128)(2,1)S(1)}, u32[]{:S(2)}, u32[]{:S(2)}) collective-permute-start(bf16[32,1792]{1,0:T(8,128)(2,1)S(1)} %add_convert_fusion), channel_id=1, source_target_pairs={{1,0},{2,1},{3,2},{11,3},{10,11},{9,10},{8,9},{0,8},{12,4},{4,5},{... | collective-permute-start | bytes 344072 | tf_op jit(solution)/shard_map/ppermute | solution.py:159
  (10 other events, 32.9 us)

commit v2 on v0

--- a/solution.py
+++ b/solution.py
@@ -1,6 +1,10 @@
+import functools
+
 import jax
 import jax.numpy as jnp
 from jax import lax
+from jax.experimental import pallas as pl
+from jax.experimental.pallas import tpu as pltpu
 from jax.sharding import PartitionSpec as P
 
 LIMIT = 4
@@ -14,7 +18,7 @@
     return widened.reshape((groups * local_count,) + source.shape[1:])
 
 
-def per_device(grad_out, saved_input, gate_weight, up_weight, down_weight, expert_ids, gate_num):
+def slots_per_device(grad_out, saved_input, gate_weight, up_weight, down_weight, expert_ids, gate_num):
     tokens_here = grad_out.shape[0]
     model_width = grad_out.shape[1]
     groups = lax.axis_size("node")
@@ -138,7 +142,406 @@
     return (grad_input, jnp.stack(gate_grads), jnp.stack(up_grads), jnp.stack(down_grads))
 
 
+LANES = 128
+STREAMS = 3
+NT = (((1,), (1,)), ((), ()))
+TN = (((0,), (0,)), ((), ()))
+VMEM = pl.BlockSpec(memory_space=pltpu.VMEM)
+ANY = pl.BlockSpec(memory_space=pl.ANY)
+
+
+def ring_moves(local_count):
+    ring_len = 2 * local_count
+
+    def place(core, spot):
+        spot = spot % ring_len
+        if spot < local_count:
+            return core * local_count + spot
+        return (2 + core) * local_count + ring_len - 1 - spot
+
+    spots = range(ring_len)
+    forth = [(place(0, i), place(0, i + 1)) for i in spots]
+    forth += [(place(1, i), place(1, i - 1)) for i in spots]
+    back = [(there, here) for here, there in forth]
+    swap = [(place(core, i), place(1 - core, i)) for i in spots for core in (0, 1)]
+    partner = dict(swap)
+    back_swap = [(here, partner[there]) for here, there in back]
+    return forth, back, swap, back_swap
+
+
+def move(value, pairs):
+    return lax.ppermute(value, ("node", "local"), pairs)
+
+
+def gather_ring(mine, local_count, moves):
+    forth, _, swap, _ = moves
+    rows = mine[0].shape[0]
+    others = [move(value, swap) for value in mine]
+    blocks = [jnp.concatenate(pair, axis=0) for pair in zip(mine, others, strict=True)]
+    near = [[value] for value in mine]
+    for _ in range(local_count - 1):
+        for i, block in enumerate(blocks):
+            blocks[i] = move(block, forth)
+            near[i].append(blocks[i])
+    for i, block in enumerate(blocks):
+        near[i].append(move(block[:rows], forth))
+    near = [jnp.concatenate(parts, axis=0) for parts in near]
+    return [(value, move(value, swap)) for value in near]
+
+
+def reduce_ring(near, far, local_count, moves, beside):
+    _, back, swap, back_swap = moves
+    half = near.shape[0]
+    rows = half // (2 * local_count)
+    wide = jnp.float32
+    made = []
+    from_other = move(far, swap)
+
+    def own(start, count):
+        part = slice(start, start + count)
+        return near[part].astype(wide) + from_other[part].astype(wide)
+
+    def hop(value):
+        moved = move(value, back)
+        if len(made) < len(beside):
+            moved, result = lax.optimization_barrier((moved, beside[len(made)](value)))
+            made.append(result)
+        return moved
+
+    start = half - rows
+    moving = hop(own(start, rows).astype(jnp.bfloat16))
+    for step in range(local_count - 1):
+        start -= 2 * rows
+        held = own(start, 2 * rows)
+        arrived = moving.astype(wide)
+        if step == 0:
+            held = jnp.concatenate([held[:rows] + arrived, held[rows:]], axis=0)
+        else:
+            held = held + arrived
+        held = held.astype(jnp.bfloat16)
+        if step < local_count - 2:
+            moving = hop(held)
+    moving = move(held[:rows], back)
+    crossed = move(held[rows:], back_swap)
+    while len(made) < len(beside):
+        made.append(beside[len(made)](held))
+    total = own(0, rows) + moving.astype(wide) + crossed.astype(wide)
+    return total.astype(jnp.bfloat16), made
+
+
+def cut_columns(total, count):
+    units = total // LANES
+    return [i * units // count * LANES for i in range(count + 1)]
+
+
+def pieces(cuts, start, stop, widest):
+    found = []
+    for stream in range(len(cuts) - 1):
+        low, high = max(start, cuts[stream]), min(stop, cuts[stream + 1])
+        if low >= high:
+            continue
+        count = -(-(high - low) // widest)
+        marks = [low + at for at in cut_columns(high - low, count)]
+        for a, b in zip(marks[:-1], marks[1:], strict=True):
+            found.append((stream, a - cuts[stream], a - start, b - a))
+    return found
+
+
+def joined(refs, piece):
+    stream, at, _, size = piece
+    near, far = refs[2 * stream], refs[2 * stream + 1]
+    return jnp.concatenate([near[:, at : at + size], far[:, at : at + size]], axis=0)
+
+
+def prepare_kernel(cuts, inputs, grads, ids, nums, *rest):
+    count = len(cuts) - 1
+    outs = rest[:count]
+    ids_ref, nums_ref, sem = rest[count:]
+    model_width = grads.shape[1]
+    copies = []
+
+    def start(source, target):
+        copy = pltpu.make_async_copy(source, target, sem.at[len(copies)])
+        copy.start()
+        copies.append(copy)
+
+    start(ids, ids_ref)
+    start(nums, nums_ref)
+    for base, array in ((0, inputs), (model_width, grads)):
+        for stream, at, offset, size in pieces(cuts, base, base + model_width, model_width):
+            start(array.at[:, pl.ds(offset, size)], outs[stream].at[:, pl.ds(at, size)])
+    copies[0].wait()
+    copies[1].wait()
+    picks, tokens_here = ids_ref.shape
+    expert = lax.broadcasted_iota(jnp.int32, (LANES, tokens_here), 0)
+    gates = jnp.zeros((LANES, tokens_here), jnp.float32)
+    for pick in range(picks):
+        value = nums_ref[pick : pick + 1, :].astype(jnp.float32) * gate_scale
+        gates += jnp.where(expert == ids_ref[pick : pick + 1, :], value, 0.0)
+    outs[-1][:, cuts[-1] - cuts[-2] - LANES :] = gates.T.astype(jnp.bfloat16)
+    for copy in copies[2:]:
+        copy.wait()
+
+
+def gate_kernel(parts, *refs):
+    *streams, gate_ref, act_ref = refs
+    experts_here, _, width = gate_ref.shape
+    for expert in range(experts_here):
+        total = None
+        for piece in parts:
+            _, _, at, size = piece
+            term = jnp.dot(
+                joined(streams, piece),
+                gate_ref[expert, at : at + size, :],
+                preferred_element_type=jnp.float32,
+            )
+            total = term if total is None else total + term
+        act_ref[:, expert * width : (expert + 1) * width] = total
+
+
+def up_kernel(parts, *refs):
+    *streams, up_ref, act_ref, hidden_ref, by_gate_ref, by_up_ref = refs
+    experts_here, _, width = up_ref.shape
+    for expert in range(experts_here):
+        cols = slice(expert * width, (expert + 1) * width)
+        up_act = None
+        for piece in parts:
+            _, _, at, size = piece
+            term = jnp.dot(
+                joined(streams, piece),
+                up_ref[expert, at : at + size, :],
+                preferred_element_type=jnp.float32,
+            )
+            up_act = term if up_act is None else up_act + term
+        gate_act = act_ref[:, cols]
+        sigmoid_val = jax.nn.sigmoid(gate_act)
+        silu = gate_act * sigmoid_val
+        hidden_ref[:, cols] = silu * up_act
+        by_gate_ref[:, cols] = up_act * sigmoid_val * (1.0 + gate_act * (1.0 - sigmoid_val))
+        by_up_ref[:, cols] = silu
+
+
+def backward_kernel(parts, gate_part, *refs):
+    *streams, hidden_ref, by_gate_ref, by_up_ref, gate_ref, up_ref, down_ref = refs[:-4]
+    dnear_ref, dfar_ref, acts_ref, hidden_out_ref = refs[-4:]
+    experts_here, model_width, width = gate_ref.shape
+    half = dnear_ref.shape[0]
+    first = lax.axis_index("node") * experts_here
+    gates = joined(streams, gate_part).astype(jnp.float32)
+    column = lax.broadcasted_iota(jnp.int32, gates.shape, 1)
+    for expert in range(experts_here):
+        cols = slice(expert * width, (expert + 1) * width)
+        back_grad = None
+        for piece in parts:
+            _, _, at, size = piece
+            term = lax.dot_general(
+                joined(streams, piece),
+                down_ref[expert, :, at : at + size],
+                NT,
+                preferred_element_type=jnp.float32,
+            )
+            back_grad = term if back_grad is None else back_grad + term
+        gate = jnp.sum(jnp.where(column == first + expert, gates, 0.0), axis=1, keepdims=True)
+        back_grad = gate * back_grad
+        at = 2 * expert * width
+        acts_ref[:, at : at + width] = (back_grad * by_gate_ref[:, cols]).astype(jnp.bfloat16)
+        acts_ref[:, at + width : at + 2 * width] = (back_grad * by_up_ref[:, cols]).astype(
+            jnp.bfloat16
+        )
+        hidden_out_ref[:, cols] = (gate * hidden_ref[:, cols]).astype(jnp.bfloat16)
+    marks = cut_columns(model_width, 7)
+    for low, high in zip(marks[:-1], marks[1:], strict=True):
+        rows = slice(low, high)
+        total = None
+        for expert in range(experts_here):
+            for k, weight in enumerate((gate_ref, up_ref)):
+                at = (2 * expert + k) * width
+                term = lax.dot_general(
+                    acts_ref[:, at : at + width],
+                    weight[expert, rows, :],
+                    NT,
+                    preferred_element_type=jnp.float32,
+                )
+                total = term if total is None else total + term
+        dnear_ref[:, rows] = total[:half]
+        dfar_ref[:, rows] = total[half:].astype(jnp.bfloat16)
+
+
+def input_weight_kernel(k, parts, *refs):
+    *streams, acts_ref, _, out_ref, staged, sem = refs
+    experts_here, _, width = staged.shape
+    copies = []
+    for i, piece in enumerate(parts):
+        _, _, at, size = piece
+        turned = joined(streams, piece).T
+        for expert in range(experts_here):
+            first = (2 * expert + k) * width
+            staged[expert, at : at + size, :] = jnp.dot(
+                turned, acts_ref[:, first : first + width], preferred_element_type=jnp.float32
+            ).astype(jnp.bfloat16)
+            rows = pl.ds(at, size)
+            copy = pltpu.make_async_copy(
+                staged.at[expert, rows, :], out_ref.at[expert, rows, :], sem.at[i, expert]
+            )
+            copy.start()
+            copies.append(copy)
+    for copy in copies:
+        copy.wait()
+
+
+def down_weight_kernel(parts, *refs):
+    *streams, hidden_ref, _, out_ref, staged, sem = refs
+    experts_here, width, _ = staged.shape
+    copies = []
+    turned = [
+        hidden_ref[:, expert * width : (expert + 1) * width].T for expert in range(experts_here)
+    ]
+    for i, piece in enumerate(parts):
+        _, _, at, size = piece
+        grads = joined(streams, piece)
+        for expert in range(experts_here):
+            staged[expert, :, at : at + size] = jnp.dot(
+                turned[expert], grads, preferred_element_type=jnp.float32
+            ).astype(jnp.bfloat16)
+            cols = pl.ds(at, size)
+            copy = pltpu.make_async_copy(
+                staged.at[expert, :, cols], out_ref.at[expert, :, cols], sem.at[i, expert]
+            )
+            copy.start()
+            copies.append(copy)
+    for copy in copies:
+        copy.wait()
+
+
+def call(kernel, name, out_shape, mib, args, matmuls=0, out_specs=None, scratch=(), anys=()):
+    flops = 2 * matmuls * MATMUL_SIZE
+    return pl.pallas_call(
+        kernel,
+        in_specs=[ANY if i in anys else VMEM for i in range(len(args))],
+        out_specs=out_specs or [VMEM] * len(out_shape),
+        out_shape=out_shape,
+        scratch_shapes=list(scratch),
+        compiler_params=pltpu.CompilerParams(vmem_limit_bytes=mib << 20),
+        cost_estimate=pl.CostEstimate(
+            flops=flops, bytes_accessed=matmuls * MATMUL_SIZE // 64, transcendentals=0
+        ),
+        name=name,
+    )(*args)
+
+
+MATMUL_SIZE = 256 * 3584 * 256
+
+
+def ring_per_device(
+    grad_out, saved_input, gate_weight, up_weight, down_weight, expert_ids, gate_num
+):
+    tokens_here, model_width = grad_out.shape
+    local_count = lax.axis_size("local")
+    experts_here, _, width = gate_weight.shape
+    moves = ring_moves(local_count)
+    picks = expert_ids.shape[1]
+    cuts = cut_columns(2 * model_width + LANES, STREAMS)
+
+    def shaped(*shape, dtype=jnp.bfloat16):
+        return jax.ShapeDtypeStruct(shape, dtype)
+
+    mine = call(
+        functools.partial(prepare_kernel, cuts),
+        "prepare",
+        [shaped(tokens_here, b - a) for a, b in zip(cuts[:-1], cuts[1:], strict=True)],
+        4,
+        (saved_input, grad_out, expert_ids.T, gate_num.T),
+        scratch=[
+            pltpu.VMEM((picks, tokens_here), jnp.int32),
+            pltpu.VMEM((picks, tokens_here), jnp.int32),
+            pltpu.SemaphoreType.DMA((2 * STREAMS + 2,)),
+        ],
+        anys=range(4),
+    )
+    gathered = gather_ring(mine, local_count, moves)
+    half = gathered[0][0].shape[0]
+    rows = 2 * half
+    all_width = experts_here * width
+
+    def streams_of(parts):
+        used = sorted({piece[0] for piece in parts})
+        arrays = [value for stream in used for value in gathered[stream]]
+        return arrays, [(used.index(piece[0]), *piece[1:]) for piece in parts]
+
+    wide = shaped(rows, all_width, dtype=jnp.float32)
+    arrays, parts = streams_of(pieces(cuts, 0, model_width, model_width))
+    (gate_act,) = call(
+        functools.partial(gate_kernel, parts),
+        "gate",
+        [wide],
+        10,
+        (*arrays, gate_weight),
+        experts_here,
+    )
+    hidden, by_gate, by_up = call(
+        functools.partial(up_kernel, parts),
+        "up",
+        [wide] * 3,
+        12,
+        (*arrays, up_weight, gate_act),
+        experts_here,
+    )
+    arrays, parts = streams_of(
+        pieces(cuts, model_width, 2 * model_width, model_width)
+        + pieces(cuts, 2 * model_width, 2 * model_width + LANES, LANES)
+    )
+    dnear, dfar, acts, hidden = call(
+        functools.partial(backward_kernel, parts[:-1], parts[-1]),
+        "backward",
+        [
+            shaped(half, model_width, dtype=jnp.float32),
+            shaped(half, model_width),
+            shaped(rows, 2 * all_width),
+            shaped(rows, all_width),
+        ],
+        24,
+        (*arrays, hidden, by_gate, by_up, gate_weight, up_weight, down_weight),
+        3 * experts_here,
+    )
+
+    def weight_grad(kernel, name, start, value, shape, after):
+        arrays, parts = streams_of(pieces(cuts, start, start + model_width, 1280))
+        return call(
+            functools.partial(kernel, parts),
+            name,
+            shaped(*shape),
+            12,
+            (*arrays, value, after),
+            experts_here,
+            out_specs=ANY,
+            scratch=[
+                pltpu.VMEM(shape, jnp.bfloat16),
+                pltpu.SemaphoreType.DMA((len(parts), experts_here)),
+            ],
+            anys=(len(arrays) + 1,),
+        )
+
+    in_shape, out_shape = (experts_here, model_width, width), (experts_here, width, model_width)
+    gate_kernel_grad = functools.partial(input_weight_kernel, 0)
+    up_kernel_grad = functools.partial(input_weight_kernel, 1)
+    grad_input, made = reduce_ring(
+        dnear,
+        dfar,
+        local_count,
+        moves,
+        [
+            lambda after: weight_grad(gate_kernel_grad, "gate_grad", 0, acts, in_shape, after),
+            lambda after: weight_grad(up_kernel_grad, "up_grad", 0, acts, in_shape, after),
+            lambda after: weight_grad(
+                down_weight_kernel, "down_grad", model_width, hidden, out_shape, after
+            ),
+        ],
+    )
+    return (grad_input, *made)
+
+
 def solution(mesh):
+    per_device = ring_per_device if mesh.shape["node"] == LIMIT else slots_per_device
     in_specs = (
         P(("rep", "node", "local"), None),
         P(("rep", "node", "local"), None),

time: 221 us -> 64 us (0.29)
  waiting for transfers between devices: 154 us -> 15.5 us
  matrix products: 16.2 us -> 0 us
  other arithmetic: 15.3 us -> 0.99 us
  Pallas kernels: 0 us -> 12.9 us
  local copies, waits for them, and re-layouts: 13.5 us -> 4.46 us
  starting transfers between devices: 20.3 us -> 29.1 us
    all_to_all x4 -> x0, waiting for transfers between devices: 154 us -> none  [the longest x1 70.8 us: per_device(): lax.all_to_all(partial_value.reshape(groups * local_count, capacity, mode...]
    ppermute x0 -> x24, starting transfers between devices: none -> 29.1 us  [move(): return lax.ppermute(value, ('node', 'local'), pairs)]
    all_to_all x4 -> x0, starting transfers between devices: 20.3 us -> none  [the longest x1 7.39 us: per_device(): lax.all_to_all(spread_rows(send_gate, groups, local_count), ('node', 'loc...]
    dot_general x17 -> x0, matrix products: 16.2 us -> none  [the longest x1 3.65 us: per_device(): lax.dot_general(activations, stacked, contract_cols, preferred_element_ty...]
    ppermute x0 -> x24, waiting for transfers between devices: none -> 15.5 us  [move(): return lax.ppermute(value, ('node', 'local'), pairs)]
    pallas_call x0 -> x7, Pallas kernels: none -> 12.9 us  [call(): pl.pallas_call(kernel, in_specs=[ANY if i in anys else VMEM for i in rang...]
    squeeze x1 -> x0, local copies, waits for them, and re-layouts: 6.31 us -> none  [per_device(): gate_weight[expert]]
    another operation x3 -> x1, other arithmetic: 5.54 us -> 0.02 us  [the longest x1 3.36 us: per_device(): jnp.stack(gate_grads)]
  transfers between devices with their start and end apart: 4 -> 24, of which waited for: 4 -> 17; matrix products, arithmetic and copies ran while one was open for 10% -> 1% of each run, Pallas kernels for 0% -> 15%
where the time goes in v2:
time: 64 us; the launch traced here: 63.8 us
  starting transfers between devices  29.1 us (45%)
  waiting for transfers between devices  15.5 us (24%)
  Pallas kernels  12.9 us (20%)
  local copies, waits for them, and re-layouts  4.46 us (7%)
  other arithmetic  0.99 us (2%)
  between operations  0.87 us (1%)
    ppermute x24, starting transfers between devices, move(): return lax.ppermute(value, ('node', 'local'), pairs)  29.1 us
    ppermute x24, waiting for transfers between devices, move(): return lax.ppermute(value, ('node', 'local'), pairs)  15.5 us
    pallas_call x7, Pallas kernels, call(): pl.pallas_call(kernel, in_specs=[ANY if i in anys else VMEM for i in rang...  12.9 us
    unnamed x25, local copies, waits for them, and re-layouts  4.37 us
  transfers between devices with their start and end apart: 24, of which 17 were waited for; matrix products, arithmetic and copies ran while one was open for 1% of the time, Pallas kernels for 15%

profile of v2, /device:TPU:0, one launch (start us, length us, event | category | flops | bytes accessed | tf_op | source)
XLA Modules:
  0.0 63.8 jit_solution(27096906763051946)
XLA Ops:
  5.8 3.0 %collective-permute-start.1 = (bf16[32,2432]{1,0:T(8,128)(2,1)S(1)}, bf16[32,2432]{1,0:T(8,128)(2,1)S(1)}, u32[]{:S(2)}, u32[]{:S(2)}) collective-permute-start(bf16[32,2432]{1,0:T(8,128)(2,1)S(1)} %pad_maximum_fusion.1), channel_id=1, source_target_pairs={{0,1},{1,2},{2,3},{3,11},{11,10},{10,9},{9,8},{8,0},{4,12},{5,4},{... | collective-permute-start | bytes 466952 | tf_op jit(solution)/shard_map/ppermute | solution.py:173
  8.8 1.6 %collective-permute-start.13 = (bf16[32,2432]{1,0:T(8,128)(2,1)S(1)}, bf16[32,2432]{1,0:T(8,128)(2,1)S(1)}, u32[]{:S(2)}, u32[]{:S(2)}) collective-permute-start(bf16[32,2432]{1,0:T(8,128)(2,1)S(1)} %pad_maximum_fusion.3), channel_id=1, source_target_pairs={{0,1},{1,2},{2,3},{3,11},{11,10},{10,9},{9,8},{8,0},{4,12},{5,4},{... | collective-permute-start | bytes 466952 | tf_op jit(solution)/shard_map/ppermute | solution.py:173
  10.5 1.6 %collective-permute-start.7 = (bf16[32,2432]{1,0:T(8,128)(2,1)S(1)}, bf16[32,2432]{1,0:T(8,128)(2,1)S(1)}, u32[]{:S(2)}, u32[]{:S(2)}) collective-permute-start(bf16[32,2432]{1,0:T(8,128)(2,1)S(1)} %pad_maximum_fusion.2), channel_id=1, source_target_pairs={{0,1},{1,2},{2,3},{3,11},{11,10},{10,9},{9,8},{8,0},{4,12},{5,4},{... | collective-permute-start | bytes 466952 | tf_op jit(solution)/shard_map/ppermute | solution.py:173
  12.1 1.9 %collective-permute-start.2 = (bf16[32,2432]{1,0:T(8,128)(2,1)S(1)}, bf16[32,2432]{1,0:T(8,128)(2,1)S(1)}, u32[]{:S(2)}, u32[]{:S(2)}) collective-permute-start(bf16[32,2432]{1,0:T(8,128)(2,1)S(1)} %collective-permute-done.1), channel_id=1, source_target_pairs={{0,1},{1,2},{2,3},{3,11},{11,10},{10,9},{9,8},{8,0},{4,12},{5,4},{... | collective-permute-start | bytes 466952 | tf_op jit(solution)/shard_map/ppermute | solution.py:173
  14.1 1.6 %collective-permute-start.14 = (bf16[32,2432]{1,0:T(8,128)(2,1)S(1)}, bf16[32,2432]{1,0:T(8,128)(2,1)S(1)}, u32[]{:S(2)}, u32[]{:S(2)}) collective-permute-start(bf16[32,2432]{1,0:T(8,128)(2,1)S(1)} %collective-permute-done.13), channel_id=1, source_target_pairs={{0,1},{1,2},{2,3},{3,11},{11,10},{10,9},{9,8},{8,0},{4,12},{5,4},{... | collective-permute-start | bytes 466952 | tf_op jit(solution)/shard_map/ppermute | solution.py:173
  15.8 1.6 %collective-permute-start.8 = (bf16[32,2432]{1,0:T(8,128)(2,1)S(1)}, bf16[32,2432]{1,0:T(8,128)(2,1)S(1)}, u32[]{:S(2)}, u32[]{:S(2)}) collective-permute-start(bf16[32,2432]{1,0:T(8,128)(2,1)S(1)} %collective-permute-done.7), channel_id=1, source_target_pairs={{0,1},{1,2},{2,3},{3,11},{11,10},{10,9},{9,8},{8,0},{4,12},{5,4},{... | collective-permute-start | bytes 466952 | tf_op jit(solution)/shard_map/ppermute | solution.py:173
  17.4 1.8 %collective-permute-start.3 = (bf16[32,2432]{1,0:T(8,128)(2,1)S(1)}, bf16[32,2432]{1,0:T(8,128)(2,1)S(1)}, u32[]{:S(2)}, u32[]{:S(2)}) collective-permute-start(bf16[32,2432]{1,0:T(8,128)(2,1)S(1)} %collective-permute-done.2), channel_id=1, source_target_pairs={{0,1},{1,2},{2,3},{3,11},{11,10},{10,9},{9,8},{8,0},{4,12},{5,4},{... | collective-permute-start | bytes 466952 | tf_op jit(solution)/shard_map/ppermute | solution.py:173
  19.3 1.6 %collective-permute-start.15 = (bf16[32,2432]{1,0:T(8,128)(2,1)S(1)}, bf16[32,2432]{1,0:T(8,128)(2,1)S(1)}, u32[]{:S(2)}, u32[]{:S(2)}) collective-permute-start(bf16[32,2432]{1,0:T(8,128)(2,1)S(1)} %collective-permute-done.14), channel_id=1, source_target_pairs={{0,1},{1,2},{2,3},{3,11},{11,10},{10,9},{9,8},{8,0},{4,12},{5,4},{... | collective-permute-start | bytes 466952 | tf_op jit(solution)/shard_map/ppermute | solution.py:173
  21.0 1.6 %collective-permute-start.9 = (bf16[32,2432]{1,0:T(8,128)(2,1)S(1)}, bf16[32,2432]{1,0:T(8,128)(2,1)S(1)}, u32[]{:S(2)}, u32[]{:S(2)}) collective-permute-start(bf16[32,2432]{1,0:T(8,128)(2,1)S(1)} %collective-permute-done.8), channel_id=1, source_target_pairs={{0,1},{1,2},{2,3},{3,11},{11,10},{10,9},{9,8},{8,0},{4,12},{5,4},{... | collective-permute-start | bytes 466952 | tf_op jit(solution)/shard_map/ppermute | solution.py:173
  22.7 1.8 %collective-permute-start.4 = (bf16[16,2432]{1,0:T(8,128)(2,1)S(1)}, bf16[16,2432]{1,0:T(8,128)(2,1)S(1)}, u32[]{:S(2)}, u32[]{:S(2)}) collective-permute-start(bf16[16,2432]{1,0:T(8,128)(2,1)S(1)} %slice.69), channel_id=1, source_target_pairs={{0,1},{1,2},{2,3},{3,11},{11,10},{10,9},{9,8},{8,0},{4,12},{5,4},{... | collective-permute-start | bytes 233480 | tf_op jit(solution)/shard_map/ppermute | solution.py:173
  24.6 1.6 %collective-permute-start.16 = (bf16[16,2432]{1,0:T(8,128)(2,1)S(1)}, bf16[16,2432]{1,0:T(8,128)(2,1)S(1)}, u32[]{:S(2)}, u32[]{:S(2)}) collective-permute-start(bf16[16,2432]{1,0:T(8,128)(2,1)S(1)} %slice.71), channel_id=1, source_target_pairs={{0,1},{1,2},{2,3},{3,11},{11,10},{10,9},{9,8},{8,0},{4,12},{5,4},{... | collective-permute-start | bytes 233480 | tf_op jit(solution)/shard_map/ppermute | solution.py:173
  26.2 1.6 %collective-permute-start.10 = (bf16[16,2432]{1,0:T(8,128)(2,1)S(1)}, bf16[16,2432]{1,0:T(8,128)(2,1)S(1)}, u32[]{:S(2)}, u32[]{:S(2)}) collective-permute-start(bf16[16,2432]{1,0:T(8,128)(2,1)S(1)} %slice.70), channel_id=1, source_target_pairs={{0,1},{1,2},{2,3},{3,11},{11,10},{10,9},{9,8},{8,0},{4,12},{5,4},{... | collective-permute-start | bytes 233480 | tf_op jit(solution)/shard_map/ppermute | solution.py:173
  29.1 1.6 %collective-permute-done.10 = bf16[16,2432]{1,0:T(8,128)(2,1)S(1)} collective-permute-done((bf16[16,2432]{1,0:T(8,128)(2,1)S(1)}, bf16[16,2432]{1,0:T(8,128)(2,1)S(1)}, u32[]{:S(2)}, u32[]{:S(2)}) %collective-permute-start.10) | collective-permute-done | bytes 77856 | tf_op jit(solution)/shard_map/ppermute | solution.py:173
  34.4 3.1 %backward.1 = (f32[128,3584]{1,0:T(8,128)S(1)}, bf16[128,3584]{1,0:T(8,128)(2,1)S(1)}, bf16[256,1024]{1,0:T(8,128)(2,1)S(1)}, bf16[256,512]{1,0:T(8,128)(2,1)S(1)}) custom-call(bf16[128,2432]{1,0:T(8,128)(2,1)S(1)} %constant_dynamic-update-slice_fusion.refs_2_.refs_0_, bf16[128,2432]{1,0:T(8,128)(2,1)S(1)} %collective-permute-done.5.refs_3_.refs_1_, ...), custom_call_target="tpu_custom_call" | custom-call | flops 2818572288 | bytes 22020096 | tf_op jit(solution)/shard_map/backward/pallas_call | solution.py:418
  37.7 2.3 %collective-permute-done.18 = bf16[128,3584]{1,0:T(8,128)(2,1)S(1)} collective-permute-done((bf16[128,3584]{1,0:T(8,128)(2,1)S(1)}, bf16[128,3584]{1,0:T(8,128)(2,1)S(1)}, u32[]{:S(2)}, u32[]{:S(2)}) %collective-permute-start.18) | collective-permute-done | bytes 917536 | tf_op jit(solution)/shard_map/ppermute | solution.py:173
  40.1 1.6 %collective-permute-start.19 = (bf16[16,3584]{1,0:T(8,128)(2,1)S(1)}, bf16[16,3584]{1,0:T(8,128)(2,1)S(1)}, u32[]{:S(2)}, u32[]{:S(2)}) collective-permute-start(bf16[16,3584]{1,0:T(8,128)(2,1)S(1)} %add_convert_fusion.3.refs_5_), channel_id=1, source_target_pairs={{1,0},{2,1},{3,2},{11,3},{10,11},{9,10},{8,9},{0,8},{12,4},{4,5},{... | collective-permute-start | bytes 344072 | tf_op jit(solution)/shard_map/ppermute | solution.py:173
  41.7 2.4 %gate_grad.1 = bf16[2,3584,256]{2,1,0:T(8,128)(2,1)} custom-call(bf16[128,2432]{1,0:T(8,128)(2,1)S(1)} %constant_dynamic-update-slice_fusion.10.refs_0_, bf16[128,2432]{1,0:T(8,128)(2,1)S(1)} %collective-permute-done.17.refs_1_, bf16[128,2432]{1,0:T(8,128)(2,1)S(1)} %constant_dynamic-update-slice_fusion.refs_2_.refs_0_, ...), custom_call_target="tpu_custom_call" | custom-call | flops 939524096 | bytes 7340032 | tf_op jit(solution)/shard_map/gate_grad/pallas_call | solution.py:418
  45.0 1.6 %collective-permute-start.20 = (bf16[32,3584]{1,0:T(8,128)(2,1)S(1)}, bf16[32,3584]{1,0:T(8,128)(2,1)S(1)}, u32[]{:S(2)}, u32[]{:S(2)}) collective-permute-start(bf16[32,3584]{1,0:T(8,128)(2,1)S(1)} %pad_maximum_fusion.refs_5_), channel_id=1, source_target_pairs={{1,0},{2,1},{3,2},{11,3},{10,11},{9,10},{8,9},{0,8},{12,4},{4,5},{... | collective-permute-start | bytes 688136 | tf_op jit(solution)/shard_map/ppermute | solution.py:173
  46.5 2.4 %up_grad.1 = bf16[2,3584,256]{2,1,0:T(8,128)(2,1)} custom-call(bf16[128,2432]{1,0:T(8,128)(2,1)S(1)} %constant_dynamic-update-slice_fusion.10.refs_0_, bf16[128,2432]{1,0:T(8,128)(2,1)S(1)} %collective-permute-done.17.refs_1_, bf16[128,2432]{1,0:T(8,128)(2,1)S(1)} %constant_dynamic-update-slice_fusion.refs_2_.refs_0_, ...), custom_call_target="tpu_custom_call" | custom-call | flops 939524096 | bytes 7340032 | tf_op jit(solution)/shard_map/up_grad/pallas_call | solution.py:418
  48.9 2.1 %collective-permute-done.20 = bf16[32,3584]{1,0:T(8,128)(2,1)S(1)} collective-permute-done((bf16[32,3584]{1,0:T(8,128)(2,1)S(1)}, bf16[32,3584]{1,0:T(8,128)(2,1)S(1)}, u32[]{:S(2)}, u32[]{:S(2)}) %collective-permute-start.20) | collective-permute-done | bytes 229408 | tf_op jit(solution)/shard_map/ppermute | solution.py:173
  51.1 1.6 %collective-permute-start.21 = (bf16[32,3584]{1,0:T(8,128)(2,1)S(1)}, bf16[32,3584]{1,0:T(8,128)(2,1)S(1)}, u32[]{:S(2)}, u32[]{:S(2)}) collective-permute-start(bf16[32,3584]{1,0:T(8,128)(2,1)S(1)} %add_convert_fusion.1.refs_5_), channel_id=1, source_target_pairs={{1,0},{2,1},{3,2},{11,3},{10,11},{9,10},{8,9},{0,8},{12,4},{4,5},{... | collective-permute-start | bytes 688136 | tf_op jit(solution)/shard_map/ppermute | solution.py:173
  52.7 2.3 %down_grad.1 = bf16[2,256,3584]{2,1,0:T(8,128)(2,1)} custom-call(bf16[128,2432]{1,0:T(8,128)(2,1)S(1)} %constant_dynamic-update-slice_fusion.refs_2_.refs_0_, bf16[128,2432]{1,0:T(8,128)(2,1)S(1)} %collective-permute-done.5.refs_3_.refs_1_, bf16[128,2432]{1,0:T(8,128)(2,1)S(1)} %constant_dynamic-update-slice_fusion.5.refs_2_, ...), custom_call_target="tpu_custom_call" | custom-call | flops 939524096 | bytes 7340032 | tf_op jit(solution)/shard_map/down_grad/pallas_call | solution.py:418
  54.9 2.2 %collective-permute-done.21 = bf16[32,3584]{1,0:T(8,128)(2,1)S(1)} collective-permute-done((bf16[32,3584]{1,0:T(8,128)(2,1)S(1)}, bf16[32,3584]{1,0:T(8,128)(2,1)S(1)}, u32[]{:S(2)}, u32[]{:S(2)}) %collective-permute-start.21) | collective-permute-done | bytes 229408 | tf_op jit(solution)/shard_map/ppermute | solution.py:173
  58.8 3.3 %collective-permute-done.22 = bf16[16,3584]{1,0:T(8,128)(2,1)S(1)} collective-permute-done((bf16[16,3584]{1,0:T(8,128)(2,1)S(1)}, bf16[16,3584]{1,0:T(8,128)(2,1)S(1)}, u32[]{:S(2)}, u32[]{:S(2)}) %collective-permute-start.22) | collective-permute-done | bytes 114720 | tf_op jit(solution)/shard_map/ppermute | solution.py:173
  (74 shorter events, 15.1 us)
Async XLA Ops:
  4.4 1.4 %collective-permute-start = (bf16[16,2432]{1,0:T(8,128)(2,1)S(1)}, bf16[16,2432]{1,0:T(8,128)(2,1)S(1)}, u32[]{:S(2)}, u32[]{:S(2)}) collective-permute-start(bf16[16,2432]{1,0:T(8,128)(2,1)S(1)} %get-tuple-element.20), channel_id=1, source_target_pairs={{0,4},{4,0},{1,5},{5,1},{2,6},{6,2},{3,7},{7,3},{11,15},{15,11},{1... | collective-permute-start | bytes 233480 | tf_op jit(solution)/shard_map/ppermute | solution.py:173
  4.9 3.9 %collective-permute-start.12 = (bf16[16,2432]{1,0:T(8,128)(2,1)S(1)}, bf16[16,2432]{1,0:T(8,128)(2,1)S(1)}, u32[]{:S(2)}, u32[]{:S(2)}) collective-permute-start(bf16[16,2432]{1,0:T(8,128)(2,1)S(1)} %get-tuple-element.22), channel_id=1, source_target_pairs={{0,4},{4,0},{1,5},{5,1},{2,6},{6,2},{3,7},{7,3},{11,15},{15,11},{1... | collective-permute-start | bytes 233480 | tf_op jit(solution)/shard_map/ppermute | solution.py:173
  5.0 5.5 %collective-permute-start.6 = (bf16[16,2432]{1,0:T(8,128)(2,1)S(1)}, bf16[16,2432]{1,0:T(8,128)(2,1)S(1)}, u32[]{:S(2)}, u32[]{:S(2)}) collective-permute-start(bf16[16,2432]{1,0:T(8,128)(2,1)S(1)} %get-tuple-element.21), channel_id=1, source_target_pairs={{0,4},{4,0},{1,5},{5,1},{2,6},{6,2},{3,7},{7,3},{11,15},{15,11},{1... | collective-permute-start | bytes 233480 | tf_op jit(solution)/shard_map/ppermute | solution.py:173
  5.8 6.3 %collective-permute-start.1 = (bf16[32,2432]{1,0:T(8,128)(2,1)S(1)}, bf16[32,2432]{1,0:T(8,128)(2,1)S(1)}, u32[]{:S(2)}, u32[]{:S(2)}) collective-permute-start(bf16[32,2432]{1,0:T(8,128)(2,1)S(1)} %pad_maximum_fusion.1), channel_id=1, source_target_pairs={{0,1},{1,2},{2,3},{3,11},{11,10},{10,9},{9,8},{8,0},{4,12},{5,4},{... | collective-permute-start | bytes 466952 | tf_op jit(solution)/shard_map/ppermute | solution.py:173
  8.8 5.3 %collective-permute-start.13 = (bf16[32,2432]{1,0:T(8,128)(2,1)S(1)}, bf16[32,2432]{1,0:T(8,128)(2,1)S(1)}, u32[]{:S(2)}, u32[]{:S(2)}) collective-permute-start(bf16[32,2432]{1,0:T(8,128)(2,1)S(1)} %pad_maximum_fusion.3), channel_id=1, source_target_pairs={{0,1},{1,2},{2,3},{3,11},{11,10},{10,9},{9,8},{8,0},{4,12},{5,4},{... | collective-permute-start | bytes 466952 | tf_op jit(solution)/shard_map/ppermute | solution.py:173
  10.5 5.3 %collective-permute-start.7 = (bf16[32,2432]{1,0:T(8,128)(2,1)S(1)}, bf16[32,2432]{1,0:T(8,128)(2,1)S(1)}, u32[]{:S(2)}, u32[]{:S(2)}) collective-permute-start(bf16[32,2432]{1,0:T(8,128)(2,1)S(1)} %pad_maximum_fusion.2), channel_id=1, source_target_pairs={{0,1},{1,2},{2,3},{3,11},{11,10},{10,9},{9,8},{8,0},{4,12},{5,4},{... | collective-permute-start | bytes 466952 | tf_op jit(solution)/shard_map/ppermute | solution.py:173
  12.1 5.3 %collective-permute-start.2 = (bf16[32,2432]{1,0:T(8,128)(2,1)S(1)}, bf16[32,2432]{1,0:T(8,128)(2,1)S(1)}, u32[]{:S(2)}, u32[]{:S(2)}) collective-permute-start(bf16[32,2432]{1,0:T(8,128)(2,1)S(1)} %collective-permute-done.1), channel_id=1, source_target_pairs={{0,1},{1,2},{2,3},{3,11},{11,10},{10,9},{9,8},{8,0},{4,12},{5,4},{... | collective-permute-start | bytes 466952 | tf_op jit(solution)/shard_map/ppermute | solution.py:173
  14.1 5.2 %collective-permute-start.14 = (bf16[32,2432]{1,0:T(8,128)(2,1)S(1)}, bf16[32,2432]{1,0:T(8,128)(2,1)S(1)}, u32[]{:S(2)}, u32[]{:S(2)}) collective-permute-start(bf16[32,2432]{1,0:T(8,128)(2,1)S(1)} %collective-permute-done.13), channel_id=1, source_target_pairs={{0,1},{1,2},{2,3},{3,11},{11,10},{10,9},{9,8},{8,0},{4,12},{5,4},{... | collective-permute-start | bytes 466952 | tf_op jit(solution)/shard_map/ppermute | solution.py:173
  15.8 5.2 %collective-permute-start.8 = (bf16[32,2432]{1,0:T(8,128)(2,1)S(1)}, bf16[32,2432]{1,0:T(8,128)(2,1)S(1)}, u32[]{:S(2)}, u32[]{:S(2)}) collective-permute-start(bf16[32,2432]{1,0:T(8,128)(2,1)S(1)} %collective-permute-done.7), channel_id=1, source_target_pairs={{0,1},{1,2},{2,3},{3,11},{11,10},{10,9},{9,8},{8,0},{4,12},{5,4},{... | collective-permute-start | bytes 466952 | tf_op jit(solution)/shard_map/ppermute | solution.py:173
  17.4 5.2 %collective-permute-start.3 = (bf16[32,2432]{1,0:T(8,128)(2,1)S(1)}, bf16[32,2432]{1,0:T(8,128)(2,1)S(1)}, u32[]{:S(2)}, u32[]{:S(2)}) collective-permute-start(bf16[32,2432]{1,0:T(8,128)(2,1)S(1)} %collective-permute-done.2), channel_id=1, source_target_pairs={{0,1},{1,2},{2,3},{3,11},{11,10},{10,9},{9,8},{8,0},{4,12},{5,4},{... | collective-permute-start | bytes 466952 | tf_op jit(solution)/shard_map/ppermute | solution.py:173
  19.3 5.2 %collective-permute-start.15 = (bf16[32,2432]{1,0:T(8,128)(2,1)S(1)}, bf16[32,2432]{1,0:T(8,128)(2,1)S(1)}, u32[]{:S(2)}, u32[]{:S(2)}) collective-permute-start(bf16[32,2432]{1,0:T(8,128)(2,1)S(1)} %collective-permute-done.14), channel_id=1, source_target_pairs={{0,1},{1,2},{2,3},{3,11},{11,10},{10,9},{9,8},{8,0},{4,12},{5,4},{... | collective-permute-start | bytes 466952 | tf_op jit(solution)/shard_map/ppermute | solution.py:173
  21.0 5.2 %collective-permute-start.9 = (bf16[32,2432]{1,0:T(8,128)(2,1)S(1)}, bf16[32,2432]{1,0:T(8,128)(2,1)S(1)}, u32[]{:S(2)}, u32[]{:S(2)}) collective-permute-start(bf16[32,2432]{1,0:T(8,128)(2,1)S(1)} %collective-permute-done.8), channel_id=1, source_target_pairs={{0,1},{1,2},{2,3},{3,11},{11,10},{10,9},{9,8},{8,0},{4,12},{5,4},{... | collective-permute-start | bytes 466952 | tf_op jit(solution)/shard_map/ppermute | solution.py:173
  22.7 5.3 %collective-permute-start.4 = (bf16[16,2432]{1,0:T(8,128)(2,1)S(1)}, bf16[16,2432]{1,0:T(8,128)(2,1)S(1)}, u32[]{:S(2)}, u32[]{:S(2)}) collective-permute-start(bf16[16,2432]{1,0:T(8,128)(2,1)S(1)} %slice.69), channel_id=1, source_target_pairs={{0,1},{1,2},{2,3},{3,11},{11,10},{10,9},{9,8},{8,0},{4,12},{5,4},{... | collective-permute-start | bytes 233480 | tf_op jit(solution)/shard_map/ppermute | solution.py:173
  24.6 4.4 %collective-permute-start.16 = (bf16[16,2432]{1,0:T(8,128)(2,1)S(1)}, bf16[16,2432]{1,0:T(8,128)(2,1)S(1)}, u32[]{:S(2)}, u32[]{:S(2)}) collective-permute-start(bf16[16,2432]{1,0:T(8,128)(2,1)S(1)} %slice.71), channel_id=1, source_target_pairs={{0,1},{1,2},{2,3},{3,11},{11,10},{10,9},{9,8},{8,0},{4,12},{5,4},{... | collective-permute-start | bytes 233480 | tf_op jit(solution)/shard_map/ppermute | solution.py:173
  26.2 4.4 %collective-permute-start.10 = (bf16[16,2432]{1,0:T(8,128)(2,1)S(1)}, bf16[16,2432]{1,0:T(8,128)(2,1)S(1)}, u32[]{:S(2)}, u32[]{:S(2)}) collective-permute-start(bf16[16,2432]{1,0:T(8,128)(2,1)S(1)} %slice.70), channel_id=1, source_target_pairs={{0,1},{1,2},{2,3},{3,11},{11,10},{10,9},{9,8},{8,0},{4,12},{5,4},{... | collective-permute-start | bytes 233480 | tf_op jit(solution)/shard_map/ppermute | solution.py:173
  28.0 2.8 %collective-permute-start.5 = (bf16[128,2432]{1,0:T(8,128)(2,1)S(1)}, bf16[128,2432]{1,0:T(8,128)(2,1)S(1)}, u32[]{:S(2)}, u32[]{:S(2)}) collective-permute-start(bf16[128,2432]{1,0:T(8,128)(2,1)S(1)} %constant_dynamic-update-slice_fusion.refs_2_.refs_0_), channel_id=1, source_target_pairs={{0,4},{4,0},{1,5},{5,1},{2,6},{6,2},{3,7},{7,3},{11,15},{15,11},{1... | collective-permute-start | bytes 1867784 | tf_op jit(solution)/shard_map/ppermute | solution.py:173
  29.0 2.1 %collective-permute-start.17 = (bf16[128,2432]{1,0:T(8,128)(2,1)S(1)}, bf16[128,2432]{1,0:T(8,128)(2,1)S(1)}, u32[]{:S(2)}, u32[]{:S(2)}) collective-permute-start(bf16[128,2432]{1,0:T(8,128)(2,1)S(1)} %constant_dynamic-update-slice_fusion.10.refs_0_), channel_id=1, source_target_pairs={{0,4},{4,0},{1,5},{5,1},{2,6},{6,2},{3,7},{7,3},{11,15},{15,11},{1... | collective-permute-start | bytes 1867784 | tf_op jit(solution)/shard_map/ppermute | solution.py:173
  30.7 2.9 %collective-permute-start.11 = (bf16[128,2432]{1,0:T(8,128)(2,1)S(1)}, bf16[128,2432]{1,0:T(8,128)(2,1)S(1)}, u32[]{:S(2)}, u32[]{:S(2)}) collective-permute-start(bf16[128,2432]{1,0:T(8,128)(2,1)S(1)} %constant_dynamic-update-slice_fusion.5.refs_2_), channel_id=1, source_target_pairs={{0,4},{4,0},{1,5},{5,1},{2,6},{6,2},{3,7},{7,3},{11,15},{15,11},{1... | collective-permute-start | bytes 1867784 | tf_op jit(solution)/shard_map/ppermute | solution.py:173
  37.5 2.5 %collective-permute-start.18 = (bf16[128,3584]{1,0:T(8,128)(2,1)S(1)}, bf16[128,3584]{1,0:T(8,128)(2,1)S(1)}, u32[]{:S(2)}, u32[]{:S(2)}) collective-permute-start(bf16[128,3584]{1,0:T(8,128)(2,1)S(1)} %get-tuple-element.27), channel_id=1, source_target_pairs={{0,4},{4,0},{1,5},{5,1},{2,6},{6,2},{3,7},{7,3},{11,15},{15,11},{1... | collective-permute-start | bytes 2752520 | tf_op jit(solution)/shard_map/ppermute | solution.py:173
  40.1 4.8 %collective-permute-start.19 = (bf16[16,3584]{1,0:T(8,128)(2,1)S(1)}, bf16[16,3584]{1,0:T(8,128)(2,1)S(1)}, u32[]{:S(2)}, u32[]{:S(2)}) collective-permute-start(bf16[16,3584]{1,0:T(8,128)(2,1)S(1)} %add_convert_fusion.3.refs_5_), channel_id=1, source_target_pairs={{1,0},{2,1},{3,2},{11,3},{10,11},{9,10},{8,9},{0,8},{12,4},{4,5},{... | collective-permute-start | bytes 344072 | tf_op jit(solution)/shard_map/ppermute | solution.py:173
  45.0 6.1 %collective-permute-start.20 = (bf16[32,3584]{1,0:T(8,128)(2,1)S(1)}, bf16[32,3584]{1,0:T(8,128)(2,1)S(1)}, u32[]{:S(2)}, u32[]{:S(2)}) collective-permute-start(bf16[32,3584]{1,0:T(8,128)(2,1)S(1)} %pad_maximum_fusion.refs_5_), channel_id=1, source_target_pairs={{1,0},{2,1},{3,2},{11,3},{10,11},{9,10},{8,9},{0,8},{12,4},{4,5},{... | collective-permute-start | bytes 688136 | tf_op jit(solution)/shard_map/ppermute | solution.py:173
  51.1 6.1 %collective-permute-start.21 = (bf16[32,3584]{1,0:T(8,128)(2,1)S(1)}, bf16[32,3584]{1,0:T(8,128)(2,1)S(1)}, u32[]{:S(2)}, u32[]{:S(2)}) collective-permute-start(bf16[32,3584]{1,0:T(8,128)(2,1)S(1)} %add_convert_fusion.1.refs_5_), channel_id=1, source_target_pairs={{1,0},{2,1},{3,2},{11,3},{10,11},{9,10},{8,9},{0,8},{12,4},{4,5},{... | collective-permute-start | bytes 688136 | tf_op jit(solution)/shard_map/ppermute | solution.py:173
  57.3 4.8 %collective-permute-start.22 = (bf16[16,3584]{1,0:T(8,128)(2,1)S(1)}, bf16[16,3584]{1,0:T(8,128)(2,1)S(1)}, u32[]{:S(2)}, u32[]{:S(2)}) collective-permute-start(bf16[16,3584]{1,0:T(8,128)(2,1)S(1)} %get-tuple-element.36), channel_id=1, source_target_pairs={{1,0},{2,1},{3,2},{11,3},{10,11},{9,10},{8,9},{0,8},{12,4},{4,5},{... | collective-permute-start | bytes 344072 | tf_op jit(solution)/shard_map/ppermute | solution.py:173
  58.8 4.2 %collective-permute-start.23 = (bf16[16,3584]{1,0:T(8,128)(2,1)S(1)}, bf16[16,3584]{1,0:T(8,128)(2,1)S(1)}, u32[]{:S(2)}, u32[]{:S(2)}) collective-permute-start(bf16[16,3584]{1,0:T(8,128)(2,1)S(1)} %get-tuple-element.37), channel_id=1, source_target_pairs={{1,4},{2,5},{3,6},{11,7},{10,15},{9,14},{8,13},{0,12},{12,0},{4,1}... | collective-permute-start | bytes 344072 | tf_op jit(solution)/shard_map/ppermute | solution.py:173
  (7 other events, 40.4 us)

commit v3 on v2

--- a/solution.py
+++ b/solution.py
@@ -147,7 +147,7 @@
 NT = (((1,), (1,)), ((), ()))
 TN = (((0,), (0,)), ((), ()))
 VMEM = pl.BlockSpec(memory_space=pltpu.VMEM)
-ANY = pl.BlockSpec(memory_space=pl.ANY)
+ANY = pl.BlockSpec(memory_space=pltpu.HBM)
 
 
 def ring_moves(local_count):
@@ -166,19 +166,21 @@
     swap = [(place(core, i), place(1 - core, i)) for i in spots for core in (0, 1)]
     partner = dict(swap)
     back_swap = [(here, partner[there]) for here, there in back]
-    return forth, back, swap, back_swap
+    onward = dict(back)
+    back_two = [(here, onward[there]) for here, there in back]
+    return forth, back, swap, back_swap, back_two
 
 
 def move(value, pairs):
     return lax.ppermute(value, ("node", "local"), pairs)
 
 
-def gather_ring(mine, local_count, moves):
-    forth, _, swap, _ = moves
-    rows = mine[0].shape[0]
-    others = [move(value, swap) for value in mine]
-    blocks = [jnp.concatenate(pair, axis=0) for pair in zip(mine, others, strict=True)]
-    near = [[value] for value in mine]
+def gather_ring(mine, cuts, local_count, moves):
+    forth, _, swap, _, _ = moves
+    rows = mine.shape[0]
+    pair = jnp.concatenate([mine, move(mine, swap)], axis=0)
+    blocks = [pair[:, a:b] for a, b in zip(cuts[:-1], cuts[1:], strict=True)]
+    near = [[block[:rows]] for block in blocks]
     for _ in range(local_count - 1):
         for i, block in enumerate(blocks):
             blocks[i] = move(block, forth)
@@ -190,38 +192,43 @@
 
 
 def reduce_ring(near, far, local_count, moves, beside):
-    _, back, swap, back_swap = moves
+    _, back, swap, back_swap, back_two = moves
     half = near.shape[0]
     rows = half // (2 * local_count)
     wide = jnp.float32
     made = []
-    from_other = move(far, swap)
+
+    def with_work(moved, source):
+        if len(made) < len(beside):
+            moved, result = lax.optimization_barrier((moved, beside[len(made)](source)))
+            made.append(result)
+        return moved
+
+    from_other = with_work(move(far, swap), far)
 
     def own(start, count):
         part = slice(start, start + count)
         return near[part].astype(wide) + from_other[part].astype(wide)
 
-    def hop(value):
-        moved = move(value, back)
-        if len(made) < len(beside):
-            moved, result = lax.optimization_barrier((moved, beside[len(made)](value)))
-            made.append(result)
-        return moved
-
     start = half - rows
-    moving = hop(own(start, rows).astype(jnp.bfloat16))
+    skipping = own(start, rows).astype(jnp.bfloat16)
+    held = None
     for step in range(local_count - 1):
         start -= 2 * rows
-        held = own(start, 2 * rows)
-        arrived = moving.astype(wide)
-        if step == 0:
-            held = jnp.concatenate([held[:rows] + arrived, held[rows:]], axis=0)
+        if held is None:
+            held = own(start, 2 * rows)
         else:
-            held = held + arrived
+            held = own(start, 2 * rows) + moving.astype(wide)
+        if step == 1:
+            held = jnp.concatenate([held[:rows] + skipped.astype(wide), held[rows:]], axis=0)
         held = held.astype(jnp.bfloat16)
         if step < local_count - 2:
-            moving = hop(held)
-    moving = move(held[:rows], back)
+            moving = move(held, back)
+            if step > 0:
+                moving = with_work(moving, held)
+        if step == 0:
+            skipped = move(skipping, back_two)
+    moving = with_work(move(held[:rows], back), held)
     crossed = move(held[rows:], back_swap)
     while len(made) < len(beside):
         made.append(beside[len(made)](held))
@@ -251,36 +258,6 @@
     stream, at, _, size = piece
     near, far = refs[2 * stream], refs[2 * stream + 1]
     return jnp.concatenate([near[:, at : at + size], far[:, at : at + size]], axis=0)
-
-
-def prepare_kernel(cuts, inputs, grads, ids, nums, *rest):
-    count = len(cuts) - 1
-    outs = rest[:count]
-    ids_ref, nums_ref, sem = rest[count:]
-    model_width = grads.shape[1]
-    copies = []
-
-    def start(source, target):
-        copy = pltpu.make_async_copy(source, target, sem.at[len(copies)])
-        copy.start()
-        copies.append(copy)
-
-    start(ids, ids_ref)
-    start(nums, nums_ref)
-    for base, array in ((0, inputs), (model_width, grads)):
-        for stream, at, offset, size in pieces(cuts, base, base + model_width, model_width):
-            start(array.at[:, pl.ds(offset, size)], outs[stream].at[:, pl.ds(at, size)])
-    copies[0].wait()
-    copies[1].wait()
-    picks, tokens_here = ids_ref.shape
-    expert = lax.broadcasted_iota(jnp.int32, (LANES, tokens_here), 0)
-    gates = jnp.zeros((LANES, tokens_here), jnp.float32)
-    for pick in range(picks):
-        value = nums_ref[pick : pick + 1, :].astype(jnp.float32) * gate_scale
-        gates += jnp.where(expert == ids_ref[pick : pick + 1, :], value, 0.0)
-    outs[-1][:, cuts[-1] - cuts[-2] - LANES :] = gates.T.astype(jnp.bfloat16)
-    for copy in copies[2:]:
-        copy.wait()
 
 
 def gate_kernel(parts, *refs):
@@ -414,7 +391,7 @@
 
 
 def call(kernel, name, out_shape, mib, args, matmuls=0, out_specs=None, scratch=(), anys=()):
-    flops = 2 * matmuls * MATMUL_SIZE
+    flops = 2 * matmuls * MATMUL_SIZE // 16
     return pl.pallas_call(
         kernel,
         in_specs=[ANY if i in anys else VMEM for i in range(len(args))],
@@ -423,7 +400,7 @@
         scratch_shapes=list(scratch),
         compiler_params=pltpu.CompilerParams(vmem_limit_bytes=mib << 20),
         cost_estimate=pl.CostEstimate(
-            flops=flops, bytes_accessed=matmuls * MATMUL_SIZE // 64, transcendentals=0
+            flops=flops, bytes_accessed=matmuls * MATMUL_SIZE // 2048, transcendentals=0
         ),
         name=name,
     )(*args)
@@ -439,26 +416,17 @@
     local_count = lax.axis_size("local")
     experts_here, _, width = gate_weight.shape
     moves = ring_moves(local_count)
-    picks = expert_ids.shape[1]
     cuts = cut_columns(2 * model_width + LANES, STREAMS)
 
     def shaped(*shape, dtype=jnp.bfloat16):
         return jax.ShapeDtypeStruct(shape, dtype)
 
-    mine = call(
-        functools.partial(prepare_kernel, cuts),
-        "prepare",
-        [shaped(tokens_here, b - a) for a, b in zip(cuts[:-1], cuts[1:], strict=True)],
-        4,
-        (saved_input, grad_out, expert_ids.T, gate_num.T),
-        scratch=[
-            pltpu.VMEM((picks, tokens_here), jnp.int32),
-            pltpu.VMEM((picks, tokens_here), jnp.int32),
-            pltpu.SemaphoreType.DMA((2 * STREAMS + 2,)),
-        ],
-        anys=range(4),
-    )
-    gathered = gather_ring(mine, local_count, moves)
+    expert_hot = expert_ids[:, :, None] == jnp.arange(LANES, dtype=jnp.int32)[None, None, :]
+    gates = jnp.sum(jnp.where(expert_hot, gate_num[:, :, None], 0), axis=1)
+    gates = (gates.astype(jnp.float32) * gate_scale).astype(jnp.bfloat16)
+    mine = jnp.concatenate([saved_input, grad_out, gates], axis=1)
+    mine = lax.optimization_barrier(mine)
+    gathered = gather_ring(mine, cuts, local_count, moves)
     half = gathered[0][0].shape[0]
     rows = 2 * half
     all_width = experts_here * width

time: 64 us -> 60.4 us (0.944)
  local copies, waits for them, and re-layouts: 4.46 us -> 1.05 us
  waiting for transfers between devices: 15.5 us -> 13.1 us
  other arithmetic: 0.99 us -> 3.05 us
    unnamed x25 -> x16, local copies, waits for them, and re-layouts: 4.37 us -> 0.96 us
    ppermute x24 -> x22, waiting for transfers between devices: 15.5 us -> 13.1 us  [move(): return lax.ppermute(value, ('node', 'local'), pairs)]
    concatenate x4 -> x3, other arithmetic: 0.06 us -> 1.19 us  [the longest x1 1.14 us: ring_per_device(): mine = jnp.concatenate([saved_input, grad_out, gates], axis=1)]
    reduce_sum x0 -> x1, other arithmetic: none -> 0.94 us  [ring_per_device(): gates = jnp.sum(jnp.where(expert_hot, gate_num[:, :, None], 0), axis=1)]
    ppermute x24 -> x22, starting transfers between devices: 29.1 us -> 29.4 us  [move(): return lax.ppermute(value, ('node', 'local'), pairs)]
    pallas_call x7 -> x6, Pallas kernels: 12.9 us -> 12.6 us  [call(): pl.pallas_call(kernel, in_specs=[ANY if i in anys else VMEM for i in rang...]
  transfers between devices with their start and end apart: 24 -> 22, of which waited for: 17 -> 16; matrix products, arithmetic and copies ran while one was open for 1% -> 1% of each run, Pallas kernels for 15% -> 16%
where the time goes in v3:
time: 60.4 us; the launch traced here: 60.1 us
  starting transfers between devices  29.4 us (49%)
  waiting for transfers between devices  13.1 us (22%)
  Pallas kernels  12.6 us (21%)
  other arithmetic  3.05 us (5%)
  local copies, waits for them, and re-layouts  1.05 us (2%)
  between operations  0.87 us (1%)
    ppermute x22, starting transfers between devices, move(): return lax.ppermute(value, ('node', 'local'), pairs)  29.4 us
    ppermute x22, waiting for transfers between devices, move(): return lax.ppermute(value, ('node', 'local'), pairs)  13.1 us
    pallas_call x6, Pallas kernels, call(): pl.pallas_call(kernel, in_specs=[ANY if i in anys else VMEM for i in rang...  12.6 us
  transfers between devices with their start and end apart: 22, of which 16 were waited for; matrix products, arithmetic and copies ran while one was open for 1% of the time, Pallas kernels for 16%

profile of v3, /device:TPU:0, one launch (start us, length us, event | category | flops | bytes accessed | tf_op | source)
XLA Modules:
  0.0 60.1 jit_solution(18156827736423266261)
XLA Ops:
  4.4 3.0 %collective-permute-start.1 = (bf16[32,2432]{1,0:T(8,128)(2,1)S(1)}, bf16[32,2432]{1,0:T(8,128)(2,1)S(1)}, u32[]{:S(2)}, u32[]{:S(2)}) collective-permute-start(bf16[32,2432]{1,0:T(8,128)(2,1)S(1)} %get-tuple-element.31), channel_id=1, source_target_pairs={{0,1},{1,2},{2,3},{3,11},{11,10},{10,9},{9,8},{8,0},{4,12},{5,4},{... | collective-permute-start | bytes 466952 | tf_op jit(solution)/shard_map/ppermute | solution.py:175
  7.4 1.6 %collective-permute-start.11 = (bf16[32,2432]{1,0:T(8,128)(2,1)S(1)}, bf16[32,2432]{1,0:T(8,128)(2,1)S(1)}, u32[]{:S(2)}, u32[]{:S(2)}) collective-permute-start(bf16[32,2432]{1,0:T(8,128)(2,1)S(1)} %get-tuple-element.30), channel_id=1, source_target_pairs={{0,1},{1,2},{2,3},{3,11},{11,10},{10,9},{9,8},{8,0},{4,12},{5,4},{... | collective-permute-start | bytes 466952 | tf_op jit(solution)/shard_map/ppermute | solution.py:175
  9.1 1.6 %collective-permute-start.6 = (bf16[32,2432]{1,0:T(8,128)(2,1)S(1)}, bf16[32,2432]{1,0:T(8,128)(2,1)S(1)}, u32[]{:S(2)}, u32[]{:S(2)}) collective-permute-start(bf16[32,2432]{1,0:T(8,128)(2,1)S(1)} %get-tuple-element.32), channel_id=1, source_target_pairs={{0,1},{1,2},{2,3},{3,11},{11,10},{10,9},{9,8},{8,0},{4,12},{5,4},{... | collective-permute-start | bytes 466952 | tf_op jit(solution)/shard_map/ppermute | solution.py:175
  10.6 2.0 %collective-permute-start.2 = (bf16[32,2432]{1,0:T(8,128)(2,1)S(1)}, bf16[32,2432]{1,0:T(8,128)(2,1)S(1)}, u32[]{:S(2)}, u32[]{:S(2)}) collective-permute-start(bf16[32,2432]{1,0:T(8,128)(2,1)S(1)} %collective-permute-done.1), channel_id=1, source_target_pairs={{0,1},{1,2},{2,3},{3,11},{11,10},{10,9},{9,8},{8,0},{4,12},{5,4},{... | collective-permute-start | bytes 466952 | tf_op jit(solution)/shard_map/ppermute | solution.py:175
  12.7 1.6 %collective-permute-start.12 = (bf16[32,2432]{1,0:T(8,128)(2,1)S(1)}, bf16[32,2432]{1,0:T(8,128)(2,1)S(1)}, u32[]{:S(2)}, u32[]{:S(2)}) collective-permute-start(bf16[32,2432]{1,0:T(8,128)(2,1)S(1)} %collective-permute-done.11), channel_id=1, source_target_pairs={{0,1},{1,2},{2,3},{3,11},{11,10},{10,9},{9,8},{8,0},{4,12},{5,4},{... | collective-permute-start | bytes 466952 | tf_op jit(solution)/shard_map/ppermute | solution.py:175
  14.4 1.6 %collective-permute-start.7 = (bf16[32,2432]{1,0:T(8,128)(2,1)S(1)}, bf16[32,2432]{1,0:T(8,128)(2,1)S(1)}, u32[]{:S(2)}, u32[]{:S(2)}) collective-permute-start(bf16[32,2432]{1,0:T(8,128)(2,1)S(1)} %collective-permute-done.6), channel_id=1, source_target_pairs={{0,1},{1,2},{2,3},{3,11},{11,10},{10,9},{9,8},{8,0},{4,12},{5,4},{... | collective-permute-start | bytes 466952 | tf_op jit(solution)/shard_map/ppermute | solution.py:175
  16.1 1.8 %collective-permute-start.3 = (bf16[32,2432]{1,0:T(8,128)(2,1)S(1)}, bf16[32,2432]{1,0:T(8,128)(2,1)S(1)}, u32[]{:S(2)}, u32[]{:S(2)}) collective-permute-start(bf16[32,2432]{1,0:T(8,128)(2,1)S(1)} %collective-permute-done.2), channel_id=1, source_target_pairs={{0,1},{1,2},{2,3},{3,11},{11,10},{10,9},{9,8},{8,0},{4,12},{5,4},{... | collective-permute-start | bytes 466952 | tf_op jit(solution)/shard_map/ppermute | solution.py:175
  18.0 1.6 %collective-permute-start.13 = (bf16[32,2432]{1,0:T(8,128)(2,1)S(1)}, bf16[32,2432]{1,0:T(8,128)(2,1)S(1)}, u32[]{:S(2)}, u32[]{:S(2)}) collective-permute-start(bf16[32,2432]{1,0:T(8,128)(2,1)S(1)} %collective-permute-done.12), channel_id=1, source_target_pairs={{0,1},{1,2},{2,3},{3,11},{11,10},{10,9},{9,8},{8,0},{4,12},{5,4},{... | collective-permute-start | bytes 466952 | tf_op jit(solution)/shard_map/ppermute | solution.py:175
  19.6 1.6 %collective-permute-start.8 = (bf16[32,2432]{1,0:T(8,128)(2,1)S(1)}, bf16[32,2432]{1,0:T(8,128)(2,1)S(1)}, u32[]{:S(2)}, u32[]{:S(2)}) collective-permute-start(bf16[32,2432]{1,0:T(8,128)(2,1)S(1)} %collective-permute-done.7), channel_id=1, source_target_pairs={{0,1},{1,2},{2,3},{3,11},{11,10},{10,9},{9,8},{8,0},{4,12},{5,4},{... | collective-permute-start | bytes 466952 | tf_op jit(solution)/shard_map/ppermute | solution.py:175
  21.3 1.8 %collective-permute-start.4 = (bf16[16,2432]{1,0:T(8,128)(2,1)S(1)}, bf16[16,2432]{1,0:T(8,128)(2,1)S(1)}, u32[]{:S(2)}, u32[]{:S(2)}) collective-permute-start(bf16[16,2432]{1,0:T(8,128)(2,1)S(1)} %slice.102), channel_id=1, source_target_pairs={{0,1},{1,2},{2,3},{3,11},{11,10},{10,9},{9,8},{8,0},{4,12},{5,4},{... | collective-permute-start | bytes 233480 | tf_op jit(solution)/shard_map/ppermute | solution.py:175
  23.2 1.6 %collective-permute-start.14 = (bf16[16,2432]{1,0:T(8,128)(2,1)S(1)}, bf16[16,2432]{1,0:T(8,128)(2,1)S(1)}, u32[]{:S(2)}, u32[]{:S(2)}) collective-permute-start(bf16[16,2432]{1,0:T(8,128)(2,1)S(1)} %slice.108), channel_id=1, source_target_pairs={{0,1},{1,2},{2,3},{3,11},{11,10},{10,9},{9,8},{8,0},{4,12},{5,4},{... | collective-permute-start | bytes 233480 | tf_op jit(solution)/shard_map/ppermute | solution.py:175
  24.9 1.6 %collective-permute-start.9 = (bf16[16,2432]{1,0:T(8,128)(2,1)S(1)}, bf16[16,2432]{1,0:T(8,128)(2,1)S(1)}, u32[]{:S(2)}, u32[]{:S(2)}) collective-permute-start(bf16[16,2432]{1,0:T(8,128)(2,1)S(1)} %slice.106), channel_id=1, source_target_pairs={{0,1},{1,2},{2,3},{3,11},{11,10},{10,9},{9,8},{8,0},{4,12},{5,4},{... | collective-permute-start | bytes 233480 | tf_op jit(solution)/shard_map/ppermute | solution.py:175
  27.7 1.6 %collective-permute-done.9 = bf16[16,2432]{1,0:T(8,128)(2,1)S(1)} collective-permute-done((bf16[16,2432]{1,0:T(8,128)(2,1)S(1)}, bf16[16,2432]{1,0:T(8,128)(2,1)S(1)}, u32[]{:S(2)}, u32[]{:S(2)}) %collective-permute-start.9) | collective-permute-done | bytes 77856 | tf_op jit(solution)/shard_map/ppermute | solution.py:175
  33.0 3.1 %backward.1 = (f32[128,3584]{1,0:T(8,128)S(1)}, bf16[128,3584]{1,0:T(8,128)(2,1)S(1)}, bf16[256,1024]{1,0:T(8,128)(2,1)S(1)}, bf16[256,512]{1,0:T(8,128)(2,1)S(1)}) custom-call(bf16[128,2432]{1,0:T(8,128)(2,1)S(1)} %constant_dynamic-update-slice_fusion.refs_2_.refs_0_, bf16[128,2432]{1,0:T(8,128)(2,1)S(1)} %collective-permute-done.5.refs_3_.refs_1_, ...), custom_call_target="tpu_custom_call" | custom-call | flops 176160768 | bytes 688128 | tf_op jit(solution)/shard_map/backward/pallas_call | solution.py:395
  36.3 2.4 %gate_grad.1 = bf16[2,3584,256]{2,1,0:T(8,128)(2,1)} custom-call(bf16[128,2432]{1,0:T(8,128)(2,1)S(1)} %constant_dynamic-update-slice_fusion.8.refs_0_, bf16[128,2432]{1,0:T(8,128)(2,1)S(1)} %collective-permute-done.15.refs_1_, bf16[128,2432]{1,0:T(8,128)(2,1)S(1)} %constant_dynamic-update-slice_fusion.refs_2_.refs_0_, ...), custom_call_target="tpu_custom_call" | custom-call | flops 58720256 | bytes 229376 | tf_op jit(solution)/shard_map/gate_grad/pallas_call | solution.py:395
  38.8 1.5 %collective-permute-start.17 = (bf16[32,3584]{1,0:T(8,128)(2,1)S(1)}, bf16[32,3584]{1,0:T(8,128)(2,1)S(1)}, u32[]{:S(2)}, u32[]{:S(2)}) collective-permute-start(bf16[32,3584]{1,0:T(8,128)(2,1)S(1)} %add_convert_fusion.1), channel_id=1, source_target_pairs={{1,0},{2,1},{3,2},{11,3},{10,11},{9,10},{8,9},{0,8},{12,4},{4,5},{... | collective-permute-start | bytes 688136 | tf_op jit(solution)/shard_map/ppermute | solution.py:175
  40.4 2.6 %collective-permute-start.18 = (bf16[16,3584]{1,0:T(8,128)(2,1)S(1)}, bf16[16,3584]{1,0:T(8,128)(2,1)S(1)}, u32[]{:S(2)}, u32[]{:S(2)}) collective-permute-start(bf16[16,3584]{1,0:T(8,128)(2,1)S(1)} %add_convert_fusion.3), channel_id=1, source_target_pairs={{1,8},{2,0},{3,1},{11,2},{10,3},{9,11},{8,10},{0,9},{12,5},{4,6},{... | collective-permute-start | bytes 344072 | tf_op jit(solution)/shard_map/ppermute | solution.py:175
  43.0 1.9 %collective-permute-done.17 = bf16[32,3584]{1,0:T(8,128)(2,1)S(1)} collective-permute-done((bf16[32,3584]{1,0:T(8,128)(2,1)S(1)}, bf16[32,3584]{1,0:T(8,128)(2,1)S(1)}, u32[]{:S(2)}, u32[]{:S(2)}) %collective-permute-start.17) | collective-permute-done | bytes 229408 | tf_op jit(solution)/shard_map/ppermute | solution.py:175
  45.0 2.3 %collective-permute-done.18 = bf16[16,3584]{1,0:T(8,128)(2,1)S(1)} collective-permute-done((bf16[16,3584]{1,0:T(8,128)(2,1)S(1)}, bf16[16,3584]{1,0:T(8,128)(2,1)S(1)}, u32[]{:S(2)}, u32[]{:S(2)}) %collective-permute-start.18) | collective-permute-done | bytes 114720 | tf_op jit(solution)/shard_map/ppermute | solution.py:175
  47.3 1.7 %collective-permute-start.19 = (bf16[32,3584]{1,0:T(8,128)(2,1)S(1)}, bf16[32,3584]{1,0:T(8,128)(2,1)S(1)}, u32[]{:S(2)}, u32[]{:S(2)}) collective-permute-start(bf16[32,3584]{1,0:T(8,128)(2,1)S(1)} %pad_maximum_fusion.1.refs_5_), channel_id=1, source_target_pairs={{1,0},{2,1},{3,2},{11,3},{10,11},{9,10},{8,9},{0,8},{12,4},{4,5},{... | collective-permute-start | bytes 688136 | tf_op jit(solution)/shard_map/ppermute | solution.py:175
  49.0 2.4 %up_grad.1 = bf16[2,3584,256]{2,1,0:T(8,128)(2,1)} custom-call(bf16[128,2432]{1,0:T(8,128)(2,1)S(1)} %constant_dynamic-update-slice_fusion.8.refs_0_, bf16[128,2432]{1,0:T(8,128)(2,1)S(1)} %collective-permute-done.15.refs_1_, bf16[128,2432]{1,0:T(8,128)(2,1)S(1)} %constant_dynamic-update-slice_fusion.refs_2_.refs_0_, ...), custom_call_target="tpu_custom_call" | custom-call | flops 58720256 | bytes 229376 | tf_op jit(solution)/shard_map/up_grad/pallas_call | solution.py:395
  51.4 2.6 %collective-permute-done.19 = bf16[32,3584]{1,0:T(8,128)(2,1)S(1)} collective-permute-done((bf16[32,3584]{1,0:T(8,128)(2,1)S(1)}, bf16[32,3584]{1,0:T(8,128)(2,1)S(1)}, u32[]{:S(2)}, u32[]{:S(2)}) %collective-permute-start.19) | collective-permute-done | bytes 229408 | tf_op jit(solution)/shard_map/ppermute | solution.py:175
  55.2 2.3 %down_grad.1 = bf16[2,256,3584]{2,1,0:T(8,128)(2,1)} custom-call(bf16[128,2432]{1,0:T(8,128)(2,1)S(1)} %constant_dynamic-update-slice_fusion.refs_2_.refs_0_, bf16[128,2432]{1,0:T(8,128)(2,1)S(1)} %collective-permute-done.5.refs_3_.refs_1_, bf16[128,2432]{1,0:T(8,128)(2,1)S(1)} %constant_dynamic-update-slice_fusion.4.refs_2_, ...), custom_call_target="tpu_custom_call" | custom-call | flops 58720256 | bytes 229376 | tf_op jit(solution)/shard_map/down_grad/pallas_call | solution.py:395
  57.5 1.5 %collective-permute-done.20 = bf16[16,3584]{1,0:T(8,128)(2,1)S(1)} collective-permute-done((bf16[16,3584]{1,0:T(8,128)(2,1)S(1)}, bf16[16,3584]{1,0:T(8,128)(2,1)S(1)}, u32[]{:S(2)}, u32[]{:S(2)}) %collective-permute-start.20) | collective-permute-done | bytes 114720 | tf_op jit(solution)/shard_map/ppermute | solution.py:175
  (61 shorter events, 11.9 us)
Async XLA Ops:
  0.6 29.1 %copy-start.1 = (bf16[2,3584,256]{2,1,0:T(8,128)(2,1)S(1)}, bf16[2,3584,256]{2,1,0:T(8,128)(2,1)}, u32[]{:S(2)}) copy-start(bf16[2,3584,256]{2,1,0:T(8,128)(2,1)} %refs_7_.1) | copy-start | bytes 11010052
  2.7 1.6 %collective-permute-start = (bf16[16,7296]{1,0:T(8,128)(2,1)S(1)}, bf16[16,7296]{1,0:T(8,128)(2,1)S(1)}, u32[]{:S(2)}, u32[]{:S(2)}) collective-permute-start(bf16[16,7296]{1,0:T(8,128)(2,1)S(1)} %pad_maximum_fusion), channel_id=1, source_target_pairs={{0,4},{4,0},{1,5},{5,1},{2,6},{6,2},{3,7},{7,3},{11,15},{15,11},{1... | collective-permute-start | bytes 700424 | tf_op jit(solution)/shard_map/ppermute | solution.py:175
  4.4 6.2 %collective-permute-start.1 = (bf16[32,2432]{1,0:T(8,128)(2,1)S(1)}, bf16[32,2432]{1,0:T(8,128)(2,1)S(1)}, u32[]{:S(2)}, u32[]{:S(2)}) collective-permute-start(bf16[32,2432]{1,0:T(8,128)(2,1)S(1)} %get-tuple-element.31), channel_id=1, source_target_pairs={{0,1},{1,2},{2,3},{3,11},{11,10},{10,9},{9,8},{8,0},{4,12},{5,4},{... | collective-permute-start | bytes 466952 | tf_op jit(solution)/shard_map/ppermute | solution.py:175
  7.4 5.3 %collective-permute-start.11 = (bf16[32,2432]{1,0:T(8,128)(2,1)S(1)}, bf16[32,2432]{1,0:T(8,128)(2,1)S(1)}, u32[]{:S(2)}, u32[]{:S(2)}) collective-permute-start(bf16[32,2432]{1,0:T(8,128)(2,1)S(1)} %get-tuple-element.30), channel_id=1, source_target_pairs={{0,1},{1,2},{2,3},{3,11},{11,10},{10,9},{9,8},{8,0},{4,12},{5,4},{... | collective-permute-start | bytes 466952 | tf_op jit(solution)/shard_map/ppermute | solution.py:175
  9.1 5.3 %collective-permute-start.6 = (bf16[32,2432]{1,0:T(8,128)(2,1)S(1)}, bf16[32,2432]{1,0:T(8,128)(2,1)S(1)}, u32[]{:S(2)}, u32[]{:S(2)}) collective-permute-start(bf16[32,2432]{1,0:T(8,128)(2,1)S(1)} %get-tuple-element.32), channel_id=1, source_target_pairs={{0,1},{1,2},{2,3},{3,11},{11,10},{10,9},{9,8},{8,0},{4,12},{5,4},{... | collective-permute-start | bytes 466952 | tf_op jit(solution)/shard_map/ppermute | solution.py:175
  10.6 5.4 %collective-permute-start.2 = (bf16[32,2432]{1,0:T(8,128)(2,1)S(1)}, bf16[32,2432]{1,0:T(8,128)(2,1)S(1)}, u32[]{:S(2)}, u32[]{:S(2)}) collective-permute-start(bf16[32,2432]{1,0:T(8,128)(2,1)S(1)} %collective-permute-done.1), channel_id=1, source_target_pairs={{0,1},{1,2},{2,3},{3,11},{11,10},{10,9},{9,8},{8,0},{4,12},{5,4},{... | collective-permute-start | bytes 466952 | tf_op jit(solution)/shard_map/ppermute | solution.py:175
  12.7 5.2 %collective-permute-start.12 = (bf16[32,2432]{1,0:T(8,128)(2,1)S(1)}, bf16[32,2432]{1,0:T(8,128)(2,1)S(1)}, u32[]{:S(2)}, u32[]{:S(2)}) collective-permute-start(bf16[32,2432]{1,0:T(8,128)(2,1)S(1)} %collective-permute-done.11), channel_id=1, source_target_pairs={{0,1},{1,2},{2,3},{3,11},{11,10},{10,9},{9,8},{8,0},{4,12},{5,4},{... | collective-permute-start | bytes 466952 | tf_op jit(solution)/shard_map/ppermute | solution.py:175
  14.4 5.2 %collective-permute-start.7 = (bf16[32,2432]{1,0:T(8,128)(2,1)S(1)}, bf16[32,2432]{1,0:T(8,128)(2,1)S(1)}, u32[]{:S(2)}, u32[]{:S(2)}) collective-permute-start(bf16[32,2432]{1,0:T(8,128)(2,1)S(1)} %collective-permute-done.6), channel_id=1, source_target_pairs={{0,1},{1,2},{2,3},{3,11},{11,10},{10,9},{9,8},{8,0},{4,12},{5,4},{... | collective-permute-start | bytes 466952 | tf_op jit(solution)/shard_map/ppermute | solution.py:175
  16.1 5.2 %collective-permute-start.3 = (bf16[32,2432]{1,0:T(8,128)(2,1)S(1)}, bf16[32,2432]{1,0:T(8,128)(2,1)S(1)}, u32[]{:S(2)}, u32[]{:S(2)}) collective-permute-start(bf16[32,2432]{1,0:T(8,128)(2,1)S(1)} %collective-permute-done.2), channel_id=1, source_target_pairs={{0,1},{1,2},{2,3},{3,11},{11,10},{10,9},{9,8},{8,0},{4,12},{5,4},{... | collective-permute-start | bytes 466952 | tf_op jit(solution)/shard_map/ppermute | solution.py:175
  18.0 5.2 %collective-permute-start.13 = (bf16[32,2432]{1,0:T(8,128)(2,1)S(1)}, bf16[32,2432]{1,0:T(8,128)(2,1)S(1)}, u32[]{:S(2)}, u32[]{:S(2)}) collective-permute-start(bf16[32,2432]{1,0:T(8,128)(2,1)S(1)} %collective-permute-done.12), channel_id=1, source_target_pairs={{0,1},{1,2},{2,3},{3,11},{11,10},{10,9},{9,8},{8,0},{4,12},{5,4},{... | collective-permute-start | bytes 466952 | tf_op jit(solution)/shard_map/ppermute | solution.py:175
  19.6 5.2 %collective-permute-start.8 = (bf16[32,2432]{1,0:T(8,128)(2,1)S(1)}, bf16[32,2432]{1,0:T(8,128)(2,1)S(1)}, u32[]{:S(2)}, u32[]{:S(2)}) collective-permute-start(bf16[32,2432]{1,0:T(8,128)(2,1)S(1)} %collective-permute-done.7), channel_id=1, source_target_pairs={{0,1},{1,2},{2,3},{3,11},{11,10},{10,9},{9,8},{8,0},{4,12},{5,4},{... | collective-permute-start | bytes 466952 | tf_op jit(solution)/shard_map/ppermute | solution.py:175
  21.3 5.3 %collective-permute-start.4 = (bf16[16,2432]{1,0:T(8,128)(2,1)S(1)}, bf16[16,2432]{1,0:T(8,128)(2,1)S(1)}, u32[]{:S(2)}, u32[]{:S(2)}) collective-permute-start(bf16[16,2432]{1,0:T(8,128)(2,1)S(1)} %slice.102), channel_id=1, source_target_pairs={{0,1},{1,2},{2,3},{3,11},{11,10},{10,9},{9,8},{8,0},{4,12},{5,4},{... | collective-permute-start | bytes 233480 | tf_op jit(solution)/shard_map/ppermute | solution.py:175
  23.2 4.4 %collective-permute-start.14 = (bf16[16,2432]{1,0:T(8,128)(2,1)S(1)}, bf16[16,2432]{1,0:T(8,128)(2,1)S(1)}, u32[]{:S(2)}, u32[]{:S(2)}) collective-permute-start(bf16[16,2432]{1,0:T(8,128)(2,1)S(1)} %slice.108), channel_id=1, source_target_pairs={{0,1},{1,2},{2,3},{3,11},{11,10},{10,9},{9,8},{8,0},{4,12},{5,4},{... | collective-permute-start | bytes 233480 | tf_op jit(solution)/shard_map/ppermute | solution.py:175
  24.9 4.4 %collective-permute-start.9 = (bf16[16,2432]{1,0:T(8,128)(2,1)S(1)}, bf16[16,2432]{1,0:T(8,128)(2,1)S(1)}, u32[]{:S(2)}, u32[]{:S(2)}) collective-permute-start(bf16[16,2432]{1,0:T(8,128)(2,1)S(1)} %slice.106), channel_id=1, source_target_pairs={{0,1},{1,2},{2,3},{3,11},{11,10},{10,9},{9,8},{8,0},{4,12},{5,4},{... | collective-permute-start | bytes 233480 | tf_op jit(solution)/shard_map/ppermute | solution.py:175
  26.5 4.4 %copy-start = (bf16[2,3584,256]{2,1,0:T(8,128)(2,1)S(1)}, bf16[2,3584,256]{2,1,0:T(8,128)(2,1)}, u32[]{:S(2)}) copy-start(bf16[2,3584,256]{2,1,0:T(8,128)(2,1)} %refs_8_.1) | copy-start | bytes 11010052
  26.6 2.8 %collective-permute-start.5 = (bf16[128,2432]{1,0:T(8,128)(2,1)S(1)}, bf16[128,2432]{1,0:T(8,128)(2,1)S(1)}, u32[]{:S(2)}, u32[]{:S(2)}) collective-permute-start(bf16[128,2432]{1,0:T(8,128)(2,1)S(1)} %constant_dynamic-update-slice_fusion.refs_2_.refs_0_), channel_id=1, source_target_pairs={{0,4},{4,0},{1,5},{5,1},{2,6},{6,2},{3,7},{7,3},{11,15},{15,11},{1... | collective-permute-start | bytes 1867784 | tf_op jit(solution)/shard_map/ppermute | solution.py:175
  27.6 2.1 %collective-permute-start.15 = (bf16[128,2432]{1,0:T(8,128)(2,1)S(1)}, bf16[128,2432]{1,0:T(8,128)(2,1)S(1)}, u32[]{:S(2)}, u32[]{:S(2)}) collective-permute-start(bf16[128,2432]{1,0:T(8,128)(2,1)S(1)} %constant_dynamic-update-slice_fusion.8.refs_0_), channel_id=1, source_target_pairs={{0,4},{4,0},{1,5},{5,1},{2,6},{6,2},{3,7},{7,3},{11,15},{15,11},{1... | collective-permute-start | bytes 1867784 | tf_op jit(solution)/shard_map/ppermute | solution.py:175
  29.3 2.9 %collective-permute-start.10 = (bf16[128,2432]{1,0:T(8,128)(2,1)S(1)}, bf16[128,2432]{1,0:T(8,128)(2,1)S(1)}, u32[]{:S(2)}, u32[]{:S(2)}) collective-permute-start(bf16[128,2432]{1,0:T(8,128)(2,1)S(1)} %constant_dynamic-update-slice_fusion.4.refs_2_), channel_id=1, source_target_pairs={{0,4},{4,0},{1,5},{5,1},{2,6},{6,2},{3,7},{7,3},{11,15},{15,11},{1... | collective-permute-start | bytes 1867784 | tf_op jit(solution)/shard_map/ppermute | solution.py:175
  36.1 2.6 %collective-permute-start.16 = (bf16[128,3584]{1,0:T(8,128)(2,1)S(1)}, bf16[128,3584]{1,0:T(8,128)(2,1)S(1)}, u32[]{:S(2)}, u32[]{:S(2)}) collective-permute-start(bf16[128,3584]{1,0:T(8,128)(2,1)S(1)} %get-tuple-element.21.refs_5_), channel_id=1, source_target_pairs={{0,4},{4,0},{1,5},{5,1},{2,6},{6,2},{3,7},{7,3},{11,15},{15,11},{1... | collective-permute-start | bytes 2752520 | tf_op jit(solution)/shard_map/ppermute | solution.py:175
  38.8 6.1 %collective-permute-start.17 = (bf16[32,3584]{1,0:T(8,128)(2,1)S(1)}, bf16[32,3584]{1,0:T(8,128)(2,1)S(1)}, u32[]{:S(2)}, u32[]{:S(2)}) collective-permute-start(bf16[32,3584]{1,0:T(8,128)(2,1)S(1)} %add_convert_fusion.1), channel_id=1, source_target_pairs={{1,0},{2,1},{3,2},{11,3},{10,11},{9,10},{8,9},{0,8},{12,4},{4,5},{... | collective-permute-start | bytes 688136 | tf_op jit(solution)/shard_map/ppermute | solution.py:175
  40.4 6.9 %collective-permute-start.18 = (bf16[16,3584]{1,0:T(8,128)(2,1)S(1)}, bf16[16,3584]{1,0:T(8,128)(2,1)S(1)}, u32[]{:S(2)}, u32[]{:S(2)}) collective-permute-start(bf16[16,3584]{1,0:T(8,128)(2,1)S(1)} %add_convert_fusion.3), channel_id=1, source_target_pairs={{1,8},{2,0},{3,1},{11,2},{10,3},{9,11},{8,10},{0,9},{12,5},{4,6},{... | collective-permute-start | bytes 344072 | tf_op jit(solution)/shard_map/ppermute | solution.py:175
  47.3 6.8 %collective-permute-start.19 = (bf16[32,3584]{1,0:T(8,128)(2,1)S(1)}, bf16[32,3584]{1,0:T(8,128)(2,1)S(1)}, u32[]{:S(2)}, u32[]{:S(2)}) collective-permute-start(bf16[32,3584]{1,0:T(8,128)(2,1)S(1)} %pad_maximum_fusion.1.refs_5_), channel_id=1, source_target_pairs={{1,0},{2,1},{3,2},{11,3},{10,11},{9,10},{8,9},{0,8},{12,4},{4,5},{... | collective-permute-start | bytes 688136 | tf_op jit(solution)/shard_map/ppermute | solution.py:175
  54.1 4.8 %collective-permute-start.20 = (bf16[16,3584]{1,0:T(8,128)(2,1)S(1)}, bf16[16,3584]{1,0:T(8,128)(2,1)S(1)}, u32[]{:S(2)}, u32[]{:S(2)}) collective-permute-start(bf16[16,3584]{1,0:T(8,128)(2,1)S(1)} %get-tuple-element.36), channel_id=1, source_target_pairs={{1,0},{2,1},{3,2},{11,3},{10,11},{9,10},{8,9},{0,8},{12,4},{4,5},{... | collective-permute-start | bytes 344072 | tf_op jit(solution)/shard_map/ppermute | solution.py:175
  55.2 4.2 %collective-permute-start.21 = (bf16[16,3584]{1,0:T(8,128)(2,1)S(1)}, bf16[16,3584]{1,0:T(8,128)(2,1)S(1)}, u32[]{:S(2)}, u32[]{:S(2)}) collective-permute-start(bf16[16,3584]{1,0:T(8,128)(2,1)S(1)} %get-tuple-element.37), channel_id=1, source_target_pairs={{1,4},{2,5},{3,6},{11,7},{10,15},{9,14},{8,13},{0,12},{12,0},{4,1}... | collective-permute-start | bytes 344072 | tf_op jit(solution)/shard_map/ppermute | solution.py:175
  (1 other events, 2.0 us)

commit v4 on v3

--- a/solution.py
+++ b/solution.py
@@ -166,20 +166,24 @@
     swap = [(place(core, i), place(1 - core, i)) for i in spots for core in (0, 1)]
     partner = dict(swap)
     back_swap = [(here, partner[there]) for here, there in back]
-    onward = dict(back)
-    back_two = [(here, onward[there]) for here, there in back]
-    return forth, back, swap, back_swap, back_two
+    backs = [
+        [(place(core, i), place(core, i + (2 * core - 1) * hops)) for i in spots for core in (0, 1)]
+        for hops in range(local_count)
+    ]
+    return forth, backs, swap, back_swap
 
 
 def move(value, pairs):
     return lax.ppermute(value, ("node", "local"), pairs)
 
 
-def gather_ring(mine, cuts, local_count, moves):
-    forth, _, swap, _, _ = moves
+def gather_ring(mine, gates, cuts, local_count, moves):
+    forth, _, swap, _ = moves
     rows = mine.shape[0]
     pair = jnp.concatenate([mine, move(mine, swap)], axis=0)
+    gates = jnp.concatenate([gates, move(gates, swap)], axis=0)
     blocks = [pair[:, a:b] for a, b in zip(cuts[:-1], cuts[1:], strict=True)]
+    blocks[-1] = jnp.concatenate([blocks[-1], gates], axis=1)
     near = [[block[:rows]] for block in blocks]
     for _ in range(local_count - 1):
         for i, block in enumerate(blocks):
@@ -192,8 +196,8 @@
 
 
 def reduce_ring(near, far, local_count, moves, beside):
-    _, back, swap, back_swap, back_two = moves
-    half = near.shape[0]
+    _, backs, swap, back_swap = moves
+    half = near[0].shape[0]
     rows = half // (2 * local_count)
     wide = jnp.float32
     made = []
@@ -204,31 +208,37 @@
             made.append(result)
         return moved
 
-    from_other = with_work(move(far, swap), far)
+    from_other = [move(value, swap) for value in far]
+
+    def part(column, start, count):
+        rows_here = slice(start, start + count)
+        return near[column][rows_here].astype(wide) + from_other[column][rows_here].astype(wide)
 
     def own(start, count):
-        part = slice(start, start + count)
-        return near[part].astype(wide) + from_other[part].astype(wide)
-
-    start = half - rows
-    skipping = own(start, rows).astype(jnp.bfloat16)
-    held = None
-    for step in range(local_count - 1):
-        start -= 2 * rows
-        if held is None:
-            held = own(start, 2 * rows)
-        else:
-            held = own(start, 2 * rows) + moving.astype(wide)
-        if step == 1:
-            held = jnp.concatenate([held[:rows] + skipped.astype(wide), held[rows:]], axis=0)
-        held = held.astype(jnp.bfloat16)
-        if step < local_count - 2:
-            moving = move(held, back)
-            if step > 0:
-                moving = with_work(moving, held)
-        if step == 0:
-            skipped = move(skipping, back_two)
-    moving = with_work(move(held[:rows], back), held)
+        return jnp.concatenate([part(i, start, count) for i in range(len(near))], axis=1)
+
+    blocks = [own((2 * hops - 1) * rows, 2 * rows) for hops in range(1, local_count)]
+    blocks.append(own(half - rows, rows))
+    sent = [block.astype(jnp.bfloat16) for block in blocks]
+    moved = []
+    for hops, value in enumerate(sent):
+        if hops == 2:
+            early = [
+                part(i, (2 * hops + 1) * rows, 2 * rows).astype(jnp.bfloat16)
+                for i in range(len(near))
+            ]
+            value = jnp.concatenate([move(piece, backs[hops]) for piece in early], axis=1)
+            moved.append(value)
+        elif hops:
+            moved.append(move(value, backs[hops]))
+    for i in range(min(2, len(moved))):
+        moved[i] = with_work(moved[i], sent[1])
+    held = blocks[0]
+    for value in moved[:-1]:
+        held = held + value.astype(wide)
+    held = jnp.concatenate([held[:rows] + moved[-1].astype(wide), held[rows:]], axis=0)
+    held = held.astype(jnp.bfloat16)
+    moving = with_work(move(held[:rows], backs[1]), held)
     crossed = move(held[rows:], back_swap)
     while len(made) < len(beside):
         made.append(beside[len(made)](held))
@@ -260,37 +270,35 @@
     return jnp.concatenate([near[:, at : at + size], far[:, at : at + size]], axis=0)
 
 
-def gate_kernel(parts, *refs):
-    *streams, gate_ref, act_ref = refs
+def products(parts, streams, weight_ref, expert):
+    total = None
+    for piece in parts:
+        _, _, at, size = piece
+        term = jnp.dot(
+            joined(streams, piece),
+            weight_ref[expert, at : at + size, :],
+            preferred_element_type=jnp.float32,
+        )
+        total = term if total is None else total + term
+    return total
+
+
+def begin_kernel(parts, *refs):
+    *streams, gate_ref, gate_sum_ref = refs
     experts_here, _, width = gate_ref.shape
     for expert in range(experts_here):
-        total = None
-        for piece in parts:
-            _, _, at, size = piece
-            term = jnp.dot(
-                joined(streams, piece),
-                gate_ref[expert, at : at + size, :],
-                preferred_element_type=jnp.float32,
-            )
-            total = term if total is None else total + term
-        act_ref[:, expert * width : (expert + 1) * width] = total
-
-
-def up_kernel(parts, *refs):
-    *streams, up_ref, act_ref, hidden_ref, by_gate_ref, by_up_ref = refs
+        cols = slice(expert * width, (expert + 1) * width)
+        gate_sum_ref[:, cols] = products(parts, streams, gate_ref, expert)
+
+
+def finish_kernel(parts, count, *refs):
+    *streams, gate_ref, up_ref, gate_sum_ref = refs[:-3]
+    hidden_ref, by_gate_ref, by_up_ref = refs[-3:]
     experts_here, _, width = up_ref.shape
     for expert in range(experts_here):
         cols = slice(expert * width, (expert + 1) * width)
-        up_act = None
-        for piece in parts:
-            _, _, at, size = piece
-            term = jnp.dot(
-                joined(streams, piece),
-                up_ref[expert, at : at + size, :],
-                preferred_element_type=jnp.float32,
-            )
-            up_act = term if up_act is None else up_act + term
-        gate_act = act_ref[:, cols]
+        gate_act = gate_sum_ref[:, cols] + products(parts[count:], streams, gate_ref, expert)
+        up_act = products(parts, streams, up_ref, expert)
         sigmoid_val = jax.nn.sigmoid(gate_act)
         silu = gate_act * sigmoid_val
         hidden_ref[:, cols] = silu * up_act
@@ -301,8 +309,7 @@
 def backward_kernel(parts, gate_part, *refs):
     *streams, hidden_ref, by_gate_ref, by_up_ref, gate_ref, up_ref, down_ref = refs[:-4]
     dnear_ref, dfar_ref, acts_ref, hidden_out_ref = refs[-4:]
-    experts_here, model_width, width = gate_ref.shape
-    half = dnear_ref.shape[0]
+    experts_here, _, width = gate_ref.shape
     first = lax.axis_index("node") * experts_here
     gates = joined(streams, gate_part).astype(jnp.float32)
     column = lax.broadcasted_iota(jnp.int32, gates.shape, 1)
@@ -326,22 +333,31 @@
             jnp.bfloat16
         )
         hidden_out_ref[:, cols] = (gate * hidden_ref[:, cols]).astype(jnp.bfloat16)
-    marks = cut_columns(model_width, 7)
+    spread(acts_ref, gate_ref, up_ref, dnear_ref, dfar_ref, 0)
+
+
+def spread(acts_ref, gate_ref, up_ref, dnear_ref, dfar_ref, first):
+    experts_here, _, width = gate_ref.shape
+    half, span = dnear_ref.shape
+    marks = cut_columns(span, -(-span // 512))
     for low, high in zip(marks[:-1], marks[1:], strict=True):
-        rows = slice(low, high)
         total = None
         for expert in range(experts_here):
             for k, weight in enumerate((gate_ref, up_ref)):
                 at = (2 * expert + k) * width
                 term = lax.dot_general(
                     acts_ref[:, at : at + width],
-                    weight[expert, rows, :],
+                    weight[expert, first + low : first + high, :],
                     NT,
                     preferred_element_type=jnp.float32,
                 )
                 total = term if total is None else total + term
-        dnear_ref[:, rows] = total[:half]
-        dfar_ref[:, rows] = total[half:].astype(jnp.bfloat16)
+        dnear_ref[:, low:high] = total[:half]
+        dfar_ref[:, low:high] = total[half:].astype(jnp.bfloat16)
+
+
+def spread_kernel(first, acts_ref, gate_ref, up_ref, dnear_ref, dfar_ref):
+    spread(acts_ref, gate_ref, up_ref, dnear_ref, dfar_ref, first)
 
 
 def input_weight_kernel(k, parts, *refs):
@@ -391,7 +407,7 @@
 
 
 def call(kernel, name, out_shape, mib, args, matmuls=0, out_specs=None, scratch=(), anys=()):
-    flops = 2 * matmuls * MATMUL_SIZE // 16
+    flops = 2 * matmuls * MATMUL_SIZE
     return pl.pallas_call(
         kernel,
         in_specs=[ANY if i in anys else VMEM for i in range(len(args))],
@@ -400,7 +416,7 @@
         scratch_shapes=list(scratch),
         compiler_params=pltpu.CompilerParams(vmem_limit_bytes=mib << 20),
         cost_estimate=pl.CostEstimate(
-            flops=flops, bytes_accessed=matmuls * MATMUL_SIZE // 2048, transcendentals=0
+            flops=flops, bytes_accessed=matmuls * MATMUL_SIZE // 128, transcendentals=0
         ),
         name=name,
     )(*args)
@@ -421,12 +437,12 @@
     def shaped(*shape, dtype=jnp.bfloat16):
         return jax.ShapeDtypeStruct(shape, dtype)
 
+    mine = lax.optimization_barrier(jnp.concatenate([saved_input, grad_out], axis=1))
+    _, expert_ids = lax.optimization_barrier((mine, expert_ids))
     expert_hot = expert_ids[:, :, None] == jnp.arange(LANES, dtype=jnp.int32)[None, None, :]
     gates = jnp.sum(jnp.where(expert_hot, gate_num[:, :, None], 0), axis=1)
     gates = (gates.astype(jnp.float32) * gate_scale).astype(jnp.bfloat16)
-    mine = jnp.concatenate([saved_input, grad_out, gates], axis=1)
-    mine = lax.optimization_barrier(mine)
-    gathered = gather_ring(mine, cuts, local_count, moves)
+    gathered = gather_ring(mine, gates, cuts, local_count, moves)
     half = gathered[0][0].shape[0]
     rows = 2 * half
     all_width = experts_here * width
@@ -437,39 +453,53 @@
         return arrays, [(used.index(piece[0]), *piece[1:]) for piece in parts]
 
     wide = shaped(rows, all_width, dtype=jnp.float32)
-    arrays, parts = streams_of(pieces(cuts, 0, model_width, model_width))
-    (gate_act,) = call(
-        functools.partial(gate_kernel, parts),
-        "gate",
+    in_parts = pieces(cuts, 0, model_width, model_width)
+    arrays, parts = streams_of(in_parts[:1])
+    sums = call(
+        functools.partial(begin_kernel, parts),
+        "begin",
         [wide],
-        10,
+        14,
         (*arrays, gate_weight),
         experts_here,
     )
+    arrays, parts = streams_of(in_parts)
     hidden, by_gate, by_up = call(
-        functools.partial(up_kernel, parts),
-        "up",
+        functools.partial(finish_kernel, parts, 1),
+        "finish",
         [wide] * 3,
-        12,
-        (*arrays, up_weight, gate_act),
-        experts_here,
+        16,
+        (*arrays, gate_weight, up_weight, *sums),
+        3 * experts_here,
     )
     arrays, parts = streams_of(
         pieces(cuts, model_width, 2 * model_width, model_width)
         + pieces(cuts, 2 * model_width, 2 * model_width + LANES, LANES)
     )
+    span = cut_columns(model_width, 2)[1]
     dnear, dfar, acts, hidden = call(
         functools.partial(backward_kernel, parts[:-1], parts[-1]),
         "backward",
         [
-            shaped(half, model_width, dtype=jnp.float32),
-            shaped(half, model_width),
+            shaped(half, span, dtype=jnp.float32),
+            shaped(half, span),
             shaped(rows, 2 * all_width),
             shaped(rows, all_width),
         ],
         24,
         (*arrays, hidden, by_gate, by_up, gate_weight, up_weight, down_weight),
-        3 * experts_here,
+        2 * experts_here,
+    )
+    more_near, more_far = call(
+        functools.partial(spread_kernel, span),
+        "spread",
+        [
+            shaped(half, model_width - span, dtype=jnp.float32),
+            shaped(half, model_width - span),
+        ],
+        16,
+        (acts, gate_weight, up_weight),
+        experts_here,
     )
 
     def weight_grad(kernel, name, start, value, shape, after):
@@ -493,8 +523,8 @@
     gate_kernel_grad = functools.partial(input_weight_kernel, 0)
     up_kernel_grad = functools.partial(input_weight_kernel, 1)
     grad_input, made = reduce_ring(
-        dnear,
-        dfar,
+        (dnear, more_near),
+        (dfar, more_far),
         local_count,
         moves,
         [

time: 60.4 us -> 58 us (0.960)
  waiting for transfers between devices: 13.1 us -> 9.65 us
  starting transfers between devices: 29.4 us -> 30.5 us
    ppermute x22 -> x25, waiting for transfers between devices: 13.1 us -> 9.65 us  [move(): return lax.ppermute(value, ('node', 'local'), pairs)]
    ppermute x22 -> x25, starting transfers between devices: 29.4 us -> 30.5 us  [move(): return lax.ppermute(value, ('node', 'local'), pairs)]
    pallas_call x6 -> x7, Pallas kernels: 12.6 us -> 13 us  [call(): pl.pallas_call(kernel, in_specs=[ANY if i in anys else VMEM for i in rang...]
  transfers between devices with their start and end apart: 22 -> 25, of which waited for: 16 -> 7; matrix products, arithmetic and copies ran while one was open for 1% -> 2% of each run, Pallas kernels for 16% -> 18%
where the time goes in v4:
time: 58 us; the launch traced here: 57.8 us
  starting transfers between devices  30.5 us (53%)
  Pallas kernels  13 us (22%)
  waiting for transfers between devices  9.65 us (17%)
  other arithmetic  2.94 us (5%)
  between operations  0.97 us (2%)
  local copies, waits for them, and re-layouts  0.74 us (1%)
    ppermute x25, starting transfers between devices, move(): return lax.ppermute(value, ('node', 'local'), pairs)  30.5 us
    pallas_call x7, Pallas kernels, call(): pl.pallas_call(kernel, in_specs=[ANY if i in anys else VMEM for i in rang...  13 us
    ppermute x25, waiting for transfers between devices, move(): return lax.ppermute(value, ('node', 'local'), pairs)  9.65 us
  transfers between devices with their start and end apart: 25, of which 7 were waited for; matrix products, arithmetic and copies ran while one was open for 2% of the time, Pallas kernels for 18%

profile of v4, /device:TPU:0, one launch (start us, length us, event | category | flops | bytes accessed | tf_op | source)
XLA Modules:
  0.0 57.8 jit_solution(11149050192599462856)
XLA Ops:
  3.4 3.0 %collective-permute-start.12 = (bf16[32,2432]{1,0:T(8,128)(2,1)S(1)}, bf16[32,2432]{1,0:T(8,128)(2,1)S(1)}, u32[]{:S(2)}, u32[]{:S(2)}) collective-permute-start(bf16[32,2432]{1,0:T(8,128)(2,1)S(1)} %get-tuple-element.46), channel_id=1, source_target_pairs={{0,1},{1,2},{2,3},{3,11},{11,10},{10,9},{9,8},{8,0},{4,12},{5,4},{... | collective-permute-start | bytes 466952 | tf_op jit(solution)/shard_map/ppermute | solution.py:177
  6.4 1.6 %collective-permute-start.1 = (bf16[32,2432]{1,0:T(8,128)(2,1)S(1)}, bf16[32,2432]{1,0:T(8,128)(2,1)S(1)}, u32[]{:S(2)}, u32[]{:S(2)}) collective-permute-start(bf16[32,2432]{1,0:T(8,128)(2,1)S(1)} %get-tuple-element.47), channel_id=1, source_target_pairs={{0,1},{1,2},{2,3},{3,11},{11,10},{10,9},{9,8},{8,0},{4,12},{5,4},{... | collective-permute-start | bytes 466952 | tf_op jit(solution)/shard_map/ppermute | solution.py:177
  8.0 1.6 %collective-permute-start.7 = (bf16[32,2432]{1,0:T(8,128)(2,1)S(1)}, bf16[32,2432]{1,0:T(8,128)(2,1)S(1)}, u32[]{:S(2)}, u32[]{:S(2)}) collective-permute-start(bf16[32,2432]{1,0:T(8,128)(2,1)S(1)} %maximum_maximum_fusion), channel_id=1, source_target_pairs={{0,1},{1,2},{2,3},{3,11},{11,10},{10,9},{9,8},{8,0},{4,12},{5,4},{... | collective-permute-start | bytes 466952 | tf_op jit(solution)/shard_map/ppermute | solution.py:177
  9.7 2.0 %collective-permute-start.13 = (bf16[32,2432]{1,0:T(8,128)(2,1)S(1)}, bf16[32,2432]{1,0:T(8,128)(2,1)S(1)}, u32[]{:S(2)}, u32[]{:S(2)}) collective-permute-start(bf16[32,2432]{1,0:T(8,128)(2,1)S(1)} %collective-permute-done.12), channel_id=1, source_target_pairs={{0,1},{1,2},{2,3},{3,11},{11,10},{10,9},{9,8},{8,0},{4,12},{5,4},{... | collective-permute-start | bytes 466952 | tf_op jit(solution)/shard_map/ppermute | solution.py:177
  11.7 1.7 %collective-permute-start.2 = (bf16[32,2432]{1,0:T(8,128)(2,1)S(1)}, bf16[32,2432]{1,0:T(8,128)(2,1)S(1)}, u32[]{:S(2)}, u32[]{:S(2)}) collective-permute-start(bf16[32,2432]{1,0:T(8,128)(2,1)S(1)} %collective-permute-done.1), channel_id=1, source_target_pairs={{0,1},{1,2},{2,3},{3,11},{11,10},{10,9},{9,8},{8,0},{4,12},{5,4},{... | collective-permute-start | bytes 466952 | tf_op jit(solution)/shard_map/ppermute | solution.py:177
  13.3 1.7 %collective-permute-start.8 = (bf16[32,2432]{1,0:T(8,128)(2,1)S(1)}, bf16[32,2432]{1,0:T(8,128)(2,1)S(1)}, u32[]{:S(2)}, u32[]{:S(2)}) collective-permute-start(bf16[32,2432]{1,0:T(8,128)(2,1)S(1)} %collective-permute-done.7), channel_id=1, source_target_pairs={{0,1},{1,2},{2,3},{3,11},{11,10},{10,9},{9,8},{8,0},{4,12},{5,4},{... | collective-permute-start | bytes 466952 | tf_op jit(solution)/shard_map/ppermute | solution.py:177
  15.1 1.8 %collective-permute-start.14 = (bf16[32,2432]{1,0:T(8,128)(2,1)S(1)}, bf16[32,2432]{1,0:T(8,128)(2,1)S(1)}, u32[]{:S(2)}, u32[]{:S(2)}) collective-permute-start(bf16[32,2432]{1,0:T(8,128)(2,1)S(1)} %collective-permute-done.13), channel_id=1, source_target_pairs={{0,1},{1,2},{2,3},{3,11},{11,10},{10,9},{9,8},{8,0},{4,12},{5,4},{... | collective-permute-start | bytes 466952 | tf_op jit(solution)/shard_map/ppermute | solution.py:177
  16.9 1.7 %collective-permute-start.3 = (bf16[32,2432]{1,0:T(8,128)(2,1)S(1)}, bf16[32,2432]{1,0:T(8,128)(2,1)S(1)}, u32[]{:S(2)}, u32[]{:S(2)}) collective-permute-start(bf16[32,2432]{1,0:T(8,128)(2,1)S(1)} %collective-permute-done.2), channel_id=1, source_target_pairs={{0,1},{1,2},{2,3},{3,11},{11,10},{10,9},{9,8},{8,0},{4,12},{5,4},{... | collective-permute-start | bytes 466952 | tf_op jit(solution)/shard_map/ppermute | solution.py:177
  18.6 1.7 %collective-permute-start.9 = (bf16[32,2432]{1,0:T(8,128)(2,1)S(1)}, bf16[32,2432]{1,0:T(8,128)(2,1)S(1)}, u32[]{:S(2)}, u32[]{:S(2)}) collective-permute-start(bf16[32,2432]{1,0:T(8,128)(2,1)S(1)} %collective-permute-done.8), channel_id=1, source_target_pairs={{0,1},{1,2},{2,3},{3,11},{11,10},{10,9},{9,8},{8,0},{4,12},{5,4},{... | collective-permute-start | bytes 466952 | tf_op jit(solution)/shard_map/ppermute | solution.py:177
  20.4 1.8 %collective-permute-start.15 = (bf16[16,2432]{1,0:T(8,128)(2,1)S(1)}, bf16[16,2432]{1,0:T(8,128)(2,1)S(1)}, u32[]{:S(2)}, u32[]{:S(2)}) collective-permute-start(bf16[16,2432]{1,0:T(8,128)(2,1)S(1)} %slice.143), channel_id=1, source_target_pairs={{0,1},{1,2},{2,3},{3,11},{11,10},{10,9},{9,8},{8,0},{4,12},{5,4},{... | collective-permute-start | bytes 233480 | tf_op jit(solution)/shard_map/ppermute | solution.py:177
  22.1 1.7 %collective-permute-start.4 = (bf16[16,2432]{1,0:T(8,128)(2,1)S(1)}, bf16[16,2432]{1,0:T(8,128)(2,1)S(1)}, u32[]{:S(2)}, u32[]{:S(2)}) collective-permute-start(bf16[16,2432]{1,0:T(8,128)(2,1)S(1)} %slice.137), channel_id=1, source_target_pairs={{0,1},{1,2},{2,3},{3,11},{11,10},{10,9},{9,8},{8,0},{4,12},{5,4},{... | collective-permute-start | bytes 233480 | tf_op jit(solution)/shard_map/ppermute | solution.py:177
  23.8 1.7 %collective-permute-start.10 = (bf16[16,2432]{1,0:T(8,128)(2,1)S(1)}, bf16[16,2432]{1,0:T(8,128)(2,1)S(1)}, u32[]{:S(2)}, u32[]{:S(2)}) collective-permute-start(bf16[16,2432]{1,0:T(8,128)(2,1)S(1)} %slice.141), channel_id=1, source_target_pairs={{0,1},{1,2},{2,3},{3,11},{11,10},{10,9},{9,8},{8,0},{4,12},{5,4},{... | collective-permute-start | bytes 233480 | tf_op jit(solution)/shard_map/ppermute | solution.py:177
  26.7 1.6 %collective-permute-done.10 = bf16[16,2432]{1,0:T(8,128)(2,1)S(1)} collective-permute-done((bf16[16,2432]{1,0:T(8,128)(2,1)S(1)}, bf16[16,2432]{1,0:T(8,128)(2,1)S(1)}, u32[]{:S(2)}, u32[]{:S(2)}) %collective-permute-start.10) | collective-permute-done | bytes 77856 | tf_op jit(solution)/shard_map/ppermute | solution.py:177
  29.3 1.5 %finish.1 = (f32[256,512]{1,0:T(8,128)S(1)}, f32[256,512]{1,0:T(8,128)S(1)}, f32[256,512]{1,0:T(8,128)S(1)}) custom-call(bf16[128,2432]{1,0:T(8,128)(2,1)S(1)} %constant_dynamic-update-slice_fusion.8.refs_0_, bf16[128,2432]{1,0:T(8,128)(2,1)S(1)} %collective-permute-done.16.refs_1_, bf16[128,2432]{1,0:T(8,128)(2,1)S(1)} %constant_dynamic-update-slice_fusion.refs_2_.refs_0_, ...), custom_call_target="tpu_custom_call" | custom-call | flops 2818572288 | bytes 11010048 | tf_op jit(solution)/shard_map/finish/pallas_call | solution.py:411
  31.3 2.3 %backward.1 = (f32[128,1792]{1,0:T(8,128)S(1)}, bf16[128,1792]{1,0:T(8,128)(2,1)S(1)}, bf16[256,1024]{1,0:T(8,128)(2,1)S(1)}, bf16[256,512]{1,0:T(8,128)(2,1)S(1)}) custom-call(bf16[128,2432]{1,0:T(8,128)(2,1)S(1)} %constant_dynamic-update-slice_fusion.refs_2_.refs_0_, bf16[128,2432]{1,0:T(8,128)(2,1)S(1)} %collective-permute-done.5.refs_3_.refs_1_, ...), custom_call_target="tpu_custom_call" | custom-call | flops 1879048192 | bytes 7340032 | tf_op jit(solution)/shard_map/backward/pallas_call | solution.py:411
  35.6 2.6 %collective-permute-start.20 = (bf16[32,1792]{1,0:T(8,128)(2,1)S(1)}, bf16[32,1792]{1,0:T(8,128)(2,1)S(1)}, u32[]{:S(2)}, u32[]{:S(2)}) collective-permute-start(bf16[32,1792]{1,0:T(8,128)(2,1)S(1)} %get-tuple-element.41), channel_id=1, source_target_pairs={{0,9},{4,6},{1,8},{5,7},{2,0},{6,15},{3,1},{7,14},{11,2},{15,13},{... | collective-permute-start | bytes 344072 | tf_op jit(solution)/shard_map/ppermute | solution.py:177
  38.3 2.6 %collective-permute-start.22 = (bf16[16,3584]{1,0:T(8,128)(2,1)S(1)}, bf16[16,3584]{1,0:T(8,128)(2,1)S(1)}, u32[]{:S(2)}, u32[]{:S(2)}) collective-permute-start(bf16[16,3584]{1,0:T(8,128)(2,1)S(1)} %pad_maximum_fusion.5), channel_id=1, source_target_pairs={{0,10},{4,7},{1,9},{5,15},{2,8},{6,14},{3,0},{7,13},{11,1},{15,12}... | collective-permute-start | bytes 344072 | tf_op jit(solution)/shard_map/ppermute | solution.py:177
  41.0 1.6 %collective-permute-start.21 = (bf16[32,1792]{1,0:T(8,128)(2,1)S(1)}, bf16[32,1792]{1,0:T(8,128)(2,1)S(1)}, u32[]{:S(2)}, u32[]{:S(2)}) collective-permute-start(bf16[32,1792]{1,0:T(8,128)(2,1)S(1)} %get-tuple-element.44), channel_id=1, source_target_pairs={{0,9},{4,6},{1,8},{5,7},{2,0},{6,15},{3,1},{7,14},{11,2},{15,13},{... | collective-permute-start | bytes 344072 | tf_op jit(solution)/shard_map/ppermute | solution.py:177
  42.7 2.4 %up_grad.1 = bf16[2,3584,256]{2,1,0:T(8,128)(2,1)} custom-call(bf16[128,2432]{1,0:T(8,128)(2,1)S(1)} %constant_dynamic-update-slice_fusion.8.refs_0_, bf16[128,2432]{1,0:T(8,128)(2,1)S(1)} %collective-permute-done.16.refs_1_, bf16[128,2432]{1,0:T(8,128)(2,1)S(1)} %constant_dynamic-update-slice_fusion.refs_2_.refs_0_, ...), custom_call_target="tpu_custom_call" | custom-call | flops 939524096 | bytes 3670016 | tf_op jit(solution)/shard_map/up_grad/pallas_call | solution.py:411
  45.1 2.4 %gate_grad.1 = bf16[2,3584,256]{2,1,0:T(8,128)(2,1)} custom-call(bf16[128,2432]{1,0:T(8,128)(2,1)S(1)} %constant_dynamic-update-slice_fusion.8.refs_0_, bf16[128,2432]{1,0:T(8,128)(2,1)S(1)} %collective-permute-done.16.refs_1_, bf16[128,2432]{1,0:T(8,128)(2,1)S(1)} %constant_dynamic-update-slice_fusion.refs_2_.refs_0_, ...), custom_call_target="tpu_custom_call" | custom-call | flops 939524096 | bytes 3670016 | tf_op jit(solution)/shard_map/gate_grad/pallas_call | solution.py:411
  47.5 2.4 %collective-permute-done.21 = bf16[32,1792]{1,0:T(8,128)(2,1)S(1)} collective-permute-done((bf16[32,1792]{1,0:T(8,128)(2,1)S(1)}, bf16[32,1792]{1,0:T(8,128)(2,1)S(1)}, u32[]{:S(2)}, u32[]{:S(2)}) %collective-permute-start.21) | collective-permute-done | bytes 114720 | tf_op jit(solution)/shard_map/ppermute | solution.py:177
  49.9 2.2 %collective-permute-done.19 = bf16[32,3584]{1,0:T(8,128)(2,1)S(1)} collective-permute-done((bf16[32,3584]{1,0:T(8,128)(2,1)S(1)}, bf16[32,3584]{1,0:T(8,128)(2,1)S(1)}, u32[]{:S(2)}, u32[]{:S(2)}) %collective-permute-start.19) | collective-permute-done | bytes 229408 | tf_op jit(solution)/shard_map/ppermute | solution.py:177
  52.6 2.3 %down_grad.1 = bf16[2,256,3584]{2,1,0:T(8,128)(2,1)} custom-call(bf16[128,2432]{1,0:T(8,128)(2,1)S(1)} %constant_dynamic-update-slice_fusion.refs_2_.refs_0_, bf16[128,2432]{1,0:T(8,128)(2,1)S(1)} %collective-permute-done.5.refs_3_.refs_1_, bf16[128,2432]{1,0:T(8,128)(2,1)S(1)} %constant_dynamic-update-slice_fusion.4.refs_2_, ...), custom_call_target="tpu_custom_call" | custom-call | flops 939524096 | bytes 3670016 | tf_op jit(solution)/shard_map/down_grad/pallas_call | solution.py:411
  54.9 2.2 %collective-permute-done.23 = bf16[16,3584]{1,0:T(8,128)(2,1)S(1)} collective-permute-done((bf16[16,3584]{1,0:T(8,128)(2,1)S(1)}, bf16[16,3584]{1,0:T(8,128)(2,1)S(1)}, u32[]{:S(2)}, u32[]{:S(2)}) %collective-permute-start.23) | collective-permute-done | bytes 114720 | tf_op jit(solution)/shard_map/ppermute | solution.py:177
  (74 shorter events, 9.1 us)
Async XLA Ops:
  3.1 4.9 %collective-permute-start.6 = (bf16[16,128]{1,0:T(8,128)(2,1)S(1)}, bf16[16,128]{1,0:T(8,128)(2,1)S(1)}, u32[]{:S(2)}, u32[]{:S(2)}) collective-permute-start(bf16[16,128]{1,0:T(8,128)(2,1)S(1)} %multiply_convert_fusion), channel_id=1, source_target_pairs={{0,4},{4,0},{1,5},{5,1},{2,6},{6,2},{3,7},{7,3},{11,15},{15,11},{1... | collective-permute-start | bytes 12296 | tf_op jit(solution)/shard_map/ppermute | solution.py:177
  3.4 6.3 %collective-permute-start.12 = (bf16[32,2432]{1,0:T(8,128)(2,1)S(1)}, bf16[32,2432]{1,0:T(8,128)(2,1)S(1)}, u32[]{:S(2)}, u32[]{:S(2)}) collective-permute-start(bf16[32,2432]{1,0:T(8,128)(2,1)S(1)} %get-tuple-element.46), channel_id=1, source_target_pairs={{0,1},{1,2},{2,3},{3,11},{11,10},{10,9},{9,8},{8,0},{4,12},{5,4},{... | collective-permute-start | bytes 466952 | tf_op jit(solution)/shard_map/ppermute | solution.py:177
  6.4 5.2 %collective-permute-start.1 = (bf16[32,2432]{1,0:T(8,128)(2,1)S(1)}, bf16[32,2432]{1,0:T(8,128)(2,1)S(1)}, u32[]{:S(2)}, u32[]{:S(2)}) collective-permute-start(bf16[32,2432]{1,0:T(8,128)(2,1)S(1)} %get-tuple-element.47), channel_id=1, source_target_pairs={{0,1},{1,2},{2,3},{3,11},{11,10},{10,9},{9,8},{8,0},{4,12},{5,4},{... | collective-permute-start | bytes 466952 | tf_op jit(solution)/shard_map/ppermute | solution.py:177
  8.0 5.3 %collective-permute-start.7 = (bf16[32,2432]{1,0:T(8,128)(2,1)S(1)}, bf16[32,2432]{1,0:T(8,128)(2,1)S(1)}, u32[]{:S(2)}, u32[]{:S(2)}) collective-permute-start(bf16[32,2432]{1,0:T(8,128)(2,1)S(1)} %maximum_maximum_fusion), channel_id=1, source_target_pairs={{0,1},{1,2},{2,3},{3,11},{11,10},{10,9},{9,8},{8,0},{4,12},{5,4},{... | collective-permute-start | bytes 466952 | tf_op jit(solution)/shard_map/ppermute | solution.py:177
  9.7 5.4 %collective-permute-start.13 = (bf16[32,2432]{1,0:T(8,128)(2,1)S(1)}, bf16[32,2432]{1,0:T(8,128)(2,1)S(1)}, u32[]{:S(2)}, u32[]{:S(2)}) collective-permute-start(bf16[32,2432]{1,0:T(8,128)(2,1)S(1)} %collective-permute-done.12), channel_id=1, source_target_pairs={{0,1},{1,2},{2,3},{3,11},{11,10},{10,9},{9,8},{8,0},{4,12},{5,4},{... | collective-permute-start | bytes 466952 | tf_op jit(solution)/shard_map/ppermute | solution.py:177
  11.7 5.2 %collective-permute-start.2 = (bf16[32,2432]{1,0:T(8,128)(2,1)S(1)}, bf16[32,2432]{1,0:T(8,128)(2,1)S(1)}, u32[]{:S(2)}, u32[]{:S(2)}) collective-permute-start(bf16[32,2432]{1,0:T(8,128)(2,1)S(1)} %collective-permute-done.1), channel_id=1, source_target_pairs={{0,1},{1,2},{2,3},{3,11},{11,10},{10,9},{9,8},{8,0},{4,12},{5,4},{... | collective-permute-start | bytes 466952 | tf_op jit(solution)/shard_map/ppermute | solution.py:177
  13.3 5.2 %collective-permute-start.8 = (bf16[32,2432]{1,0:T(8,128)(2,1)S(1)}, bf16[32,2432]{1,0:T(8,128)(2,1)S(1)}, u32[]{:S(2)}, u32[]{:S(2)}) collective-permute-start(bf16[32,2432]{1,0:T(8,128)(2,1)S(1)} %collective-permute-done.7), channel_id=1, source_target_pairs={{0,1},{1,2},{2,3},{3,11},{11,10},{10,9},{9,8},{8,0},{4,12},{5,4},{... | collective-permute-start | bytes 466952 | tf_op jit(solution)/shard_map/ppermute | solution.py:177
  15.1 5.3 %collective-permute-start.14 = (bf16[32,2432]{1,0:T(8,128)(2,1)S(1)}, bf16[32,2432]{1,0:T(8,128)(2,1)S(1)}, u32[]{:S(2)}, u32[]{:S(2)}) collective-permute-start(bf16[32,2432]{1,0:T(8,128)(2,1)S(1)} %collective-permute-done.13), channel_id=1, source_target_pairs={{0,1},{1,2},{2,3},{3,11},{11,10},{10,9},{9,8},{8,0},{4,12},{5,4},{... | collective-permute-start | bytes 466952 | tf_op jit(solution)/shard_map/ppermute | solution.py:177
  16.9 5.2 %collective-permute-start.3 = (bf16[32,2432]{1,0:T(8,128)(2,1)S(1)}, bf16[32,2432]{1,0:T(8,128)(2,1)S(1)}, u32[]{:S(2)}, u32[]{:S(2)}) collective-permute-start(bf16[32,2432]{1,0:T(8,128)(2,1)S(1)} %collective-permute-done.2), channel_id=1, source_target_pairs={{0,1},{1,2},{2,3},{3,11},{11,10},{10,9},{9,8},{8,0},{4,12},{5,4},{... | collective-permute-start | bytes 466952 | tf_op jit(solution)/shard_map/ppermute | solution.py:177
  18.6 5.3 %collective-permute-start.9 = (bf16[32,2432]{1,0:T(8,128)(2,1)S(1)}, bf16[32,2432]{1,0:T(8,128)(2,1)S(1)}, u32[]{:S(2)}, u32[]{:S(2)}) collective-permute-start(bf16[32,2432]{1,0:T(8,128)(2,1)S(1)} %collective-permute-done.8), channel_id=1, source_target_pairs={{0,1},{1,2},{2,3},{3,11},{11,10},{10,9},{9,8},{8,0},{4,12},{5,4},{... | collective-permute-start | bytes 466952 | tf_op jit(solution)/shard_map/ppermute | solution.py:177
  20.4 5.2 %collective-permute-start.15 = (bf16[16,2432]{1,0:T(8,128)(2,1)S(1)}, bf16[16,2432]{1,0:T(8,128)(2,1)S(1)}, u32[]{:S(2)}, u32[]{:S(2)}) collective-permute-start(bf16[16,2432]{1,0:T(8,128)(2,1)S(1)} %slice.143), channel_id=1, source_target_pairs={{0,1},{1,2},{2,3},{3,11},{11,10},{10,9},{9,8},{8,0},{4,12},{5,4},{... | collective-permute-start | bytes 233480 | tf_op jit(solution)/shard_map/ppermute | solution.py:177
  22.1 4.4 %collective-permute-start.4 = (bf16[16,2432]{1,0:T(8,128)(2,1)S(1)}, bf16[16,2432]{1,0:T(8,128)(2,1)S(1)}, u32[]{:S(2)}, u32[]{:S(2)}) collective-permute-start(bf16[16,2432]{1,0:T(8,128)(2,1)S(1)} %slice.137), channel_id=1, source_target_pairs={{0,1},{1,2},{2,3},{3,11},{11,10},{10,9},{9,8},{8,0},{4,12},{5,4},{... | collective-permute-start | bytes 233480 | tf_op jit(solution)/shard_map/ppermute | solution.py:177
  23.8 4.4 %collective-permute-start.10 = (bf16[16,2432]{1,0:T(8,128)(2,1)S(1)}, bf16[16,2432]{1,0:T(8,128)(2,1)S(1)}, u32[]{:S(2)}, u32[]{:S(2)}) collective-permute-start(bf16[16,2432]{1,0:T(8,128)(2,1)S(1)} %slice.141), channel_id=1, source_target_pairs={{0,1},{1,2},{2,3},{3,11},{11,10},{10,9},{9,8},{8,0},{4,12},{5,4},{... | collective-permute-start | bytes 233480 | tf_op jit(solution)/shard_map/ppermute | solution.py:177
  25.6 2.8 %collective-permute-start.16 = (bf16[128,2432]{1,0:T(8,128)(2,1)S(1)}, bf16[128,2432]{1,0:T(8,128)(2,1)S(1)}, u32[]{:S(2)}, u32[]{:S(2)}) collective-permute-start(bf16[128,2432]{1,0:T(8,128)(2,1)S(1)} %constant_dynamic-update-slice_fusion.8.refs_0_), channel_id=1, source_target_pairs={{0,4},{4,0},{1,5},{5,1},{2,6},{6,2},{3,7},{7,3},{11,15},{15,11},{1... | collective-permute-start | bytes 1867784 | tf_op jit(solution)/shard_map/ppermute | solution.py:177
  26.6 2.7 %collective-permute-start.5 = (bf16[128,2432]{1,0:T(8,128)(2,1)S(1)}, bf16[128,2432]{1,0:T(8,128)(2,1)S(1)}, u32[]{:S(2)}, u32[]{:S(2)}) collective-permute-start(bf16[128,2432]{1,0:T(8,128)(2,1)S(1)} %constant_dynamic-update-slice_fusion.refs_2_.refs_0_), channel_id=1, source_target_pairs={{0,4},{4,0},{1,5},{5,1},{2,6},{6,2},{3,7},{7,3},{11,15},{15,11},{1... | collective-permute-start | bytes 1867784 | tf_op jit(solution)/shard_map/ppermute | solution.py:177
  28.3 2.5 %collective-permute-start.11 = (bf16[128,2432]{1,0:T(8,128)(2,1)S(1)}, bf16[128,2432]{1,0:T(8,128)(2,1)S(1)}, u32[]{:S(2)}, u32[]{:S(2)}) collective-permute-start(bf16[128,2432]{1,0:T(8,128)(2,1)S(1)} %constant_dynamic-update-slice_fusion.4.refs_2_), channel_id=1, source_target_pairs={{0,4},{4,0},{1,5},{5,1},{2,6},{6,2},{3,7},{7,3},{11,15},{15,11},{1... | collective-permute-start | bytes 1867784 | tf_op jit(solution)/shard_map/ppermute | solution.py:177
  33.6 2.0 %collective-permute-start.17 = (bf16[128,1792]{1,0:T(8,128)(2,1)S(1)}, bf16[128,1792]{1,0:T(8,128)(2,1)S(1)}, u32[]{:S(2)}, u32[]{:S(2)}) collective-permute-start(bf16[128,1792]{1,0:T(8,128)(2,1)S(1)} %get-tuple-element.25), channel_id=1, source_target_pairs={{0,4},{4,0},{1,5},{5,1},{2,6},{6,2},{3,7},{7,3},{11,15},{15,11},{1... | collective-permute-start | bytes 1376264 | tf_op jit(solution)/shard_map/ppermute | solution.py:177
  35.4 2.9 %collective-permute-start.18 = (bf16[128,1792]{1,0:T(8,128)(2,1)S(1)}, bf16[128,1792]{1,0:T(8,128)(2,1)S(1)}, u32[]{:S(2)}, u32[]{:S(2)}) collective-permute-start(bf16[128,1792]{1,0:T(8,128)(2,1)S(1)} %get-tuple-element.28), channel_id=1, source_target_pairs={{0,4},{4,0},{1,5},{5,1},{2,6},{6,2},{3,7},{7,3},{11,15},{15,11},{1... | collective-permute-start | bytes 1376264 | tf_op jit(solution)/shard_map/ppermute | solution.py:177
  35.6 11.9 %collective-permute-start.20 = (bf16[32,1792]{1,0:T(8,128)(2,1)S(1)}, bf16[32,1792]{1,0:T(8,128)(2,1)S(1)}, u32[]{:S(2)}, u32[]{:S(2)}) collective-permute-start(bf16[32,1792]{1,0:T(8,128)(2,1)S(1)} %get-tuple-element.41), channel_id=1, source_target_pairs={{0,9},{4,6},{1,8},{5,7},{2,0},{6,15},{3,1},{7,14},{11,2},{15,13},{... | collective-permute-start | bytes 344072 | tf_op jit(solution)/shard_map/ppermute | solution.py:177
  38.3 13.9 %collective-permute-start.22 = (bf16[16,3584]{1,0:T(8,128)(2,1)S(1)}, bf16[16,3584]{1,0:T(8,128)(2,1)S(1)}, u32[]{:S(2)}, u32[]{:S(2)}) collective-permute-start(bf16[16,3584]{1,0:T(8,128)(2,1)S(1)} %pad_maximum_fusion.5), channel_id=1, source_target_pairs={{0,10},{4,7},{1,9},{5,15},{2,8},{6,14},{3,0},{7,13},{11,1},{15,12}... | collective-permute-start | bytes 344072 | tf_op jit(solution)/shard_map/ppermute | solution.py:177
  41.0 8.9 %collective-permute-start.21 = (bf16[32,1792]{1,0:T(8,128)(2,1)S(1)}, bf16[32,1792]{1,0:T(8,128)(2,1)S(1)}, u32[]{:S(2)}, u32[]{:S(2)}) collective-permute-start(bf16[32,1792]{1,0:T(8,128)(2,1)S(1)} %get-tuple-element.44), channel_id=1, source_target_pairs={{0,9},{4,6},{1,8},{5,7},{2,0},{6,15},{3,1},{7,14},{11,2},{15,13},{... | collective-permute-start | bytes 344072 | tf_op jit(solution)/shard_map/ppermute | solution.py:177
  42.6 9.5 %collective-permute-start.19 = (bf16[32,3584]{1,0:T(8,128)(2,1)S(1)}, bf16[32,3584]{1,0:T(8,128)(2,1)S(1)}, u32[]{:S(2)}, u32[]{:S(2)}) collective-permute-start(bf16[32,3584]{1,0:T(8,128)(2,1)S(1)} %pad_maximum_fusion.1.refs_5_), channel_id=1, source_target_pairs={{0,8},{4,5},{1,0},{5,6},{2,1},{6,7},{3,2},{7,15},{11,3},{15,14},{1... | collective-permute-start | bytes 688136 | tf_op jit(solution)/shard_map/ppermute | solution.py:177
  52.2 5.0 %collective-permute-start.24 = (bf16[16,3584]{1,0:T(8,128)(2,1)S(1)}, bf16[16,3584]{1,0:T(8,128)(2,1)S(1)}, u32[]{:S(2)}, u32[]{:S(2)}) collective-permute-start(bf16[16,3584]{1,0:T(8,128)(2,1)S(1)} %slice.196), channel_id=1, source_target_pairs={{1,4},{2,5},{3,6},{11,7},{10,15},{9,14},{8,13},{0,12},{12,0},{4,1}... | collective-permute-start | bytes 344072 | tf_op jit(solution)/shard_map/ppermute | solution.py:177
  52.3 4.8 %collective-permute-start.23 = (bf16[16,3584]{1,0:T(8,128)(2,1)S(1)}, bf16[16,3584]{1,0:T(8,128)(2,1)S(1)}, u32[]{:S(2)}, u32[]{:S(2)}) collective-permute-start(bf16[16,3584]{1,0:T(8,128)(2,1)S(1)} %fusion.1), channel_id=1, source_target_pairs={{0,8},{4,5},{1,0},{5,6},{2,1},{6,7},{3,2},{7,15},{11,3},{15,14},{1... | collective-permute-start | bytes 344072 | tf_op jit(solution)/shard_map/ppermute | solution.py:177
  (4 other events, 40.4 us)

commit v5 on v4

--- a/solution.py
+++ b/solution.py
@@ -162,10 +162,9 @@
     spots = range(ring_len)
     forth = [(place(0, i), place(0, i + 1)) for i in spots]
     forth += [(place(1, i), place(1, i - 1)) for i in spots]
-    back = [(there, here) for here, there in forth]
     swap = [(place(core, i), place(1 - core, i)) for i in spots for core in (0, 1)]
     partner = dict(swap)
-    back_swap = [(here, partner[there]) for here, there in back]
+    back_swap = [(there, partner[here]) for here, there in forth]
     backs = [
         [(place(core, i), place(core, i + (2 * core - 1) * hops)) for i in spots for core in (0, 1)]
         for hops in range(local_count)
@@ -231,8 +230,7 @@
             moved.append(value)
         elif hops:
             moved.append(move(value, backs[hops]))
-    for i in range(min(2, len(moved))):
-        moved[i] = with_work(moved[i], sent[1])
+    moved[0] = with_work(moved[0], sent[1])
     held = blocks[0]
     for value in moved[:-1]:
         held = held + value.astype(wide)
@@ -360,24 +358,25 @@
     spread(acts_ref, gate_ref, up_ref, dnear_ref, dfar_ref, first)
 
 
-def input_weight_kernel(k, parts, *refs):
-    *streams, acts_ref, _, out_ref, staged, sem = refs
-    experts_here, _, width = staged.shape
+def input_weight_kernel(parts, *refs):
+    *streams, acts_ref, _, gate_out_ref, up_out_ref, staged, sem = refs
+    _, experts_here, _, width = staged.shape
     copies = []
     for i, piece in enumerate(parts):
         _, _, at, size = piece
         turned = joined(streams, piece).T
         for expert in range(experts_here):
-            first = (2 * expert + k) * width
-            staged[expert, at : at + size, :] = jnp.dot(
-                turned, acts_ref[:, first : first + width], preferred_element_type=jnp.float32
-            ).astype(jnp.bfloat16)
-            rows = pl.ds(at, size)
-            copy = pltpu.make_async_copy(
-                staged.at[expert, rows, :], out_ref.at[expert, rows, :], sem.at[i, expert]
-            )
-            copy.start()
-            copies.append(copy)
+            for k, out_ref in enumerate((gate_out_ref, up_out_ref)):
+                first = (2 * expert + k) * width
+                staged[k, expert, at : at + size, :] = jnp.dot(
+                    turned, acts_ref[:, first : first + width], preferred_element_type=jnp.float32
+                ).astype(jnp.bfloat16)
+                rows = pl.ds(at, size)
+                copy = pltpu.make_async_copy(
+                    staged.at[k, expert, rows, :], out_ref.at[expert, rows, :], sem.at[i, expert, k]
+                )
+                copy.start()
+                copies.append(copy)
     for copy in copies:
         copy.wait()
 
@@ -398,7 +397,7 @@
             ).astype(jnp.bfloat16)
             cols = pl.ds(at, size)
             copy = pltpu.make_async_copy(
-                staged.at[expert, :, cols], out_ref.at[expert, :, cols], sem.at[i, expert]
+                staged.at[expert, :, cols], out_ref.at[expert, :, cols], sem.at[i, expert, 0]
             )
             copy.start()
             copies.append(copy)
@@ -406,8 +405,7 @@
         copy.wait()
 
 
-def call(kernel, name, out_shape, mib, args, matmuls=0, out_specs=None, scratch=(), anys=()):
-    flops = 2 * matmuls * MATMUL_SIZE
+def call(kernel, name, out_shape, mib, args, work, out_specs=None, scratch=(), anys=()):
     return pl.pallas_call(
         kernel,
         in_specs=[ANY if i in anys else VMEM for i in range(len(args))],
@@ -416,13 +414,10 @@
         scratch_shapes=list(scratch),
         compiler_params=pltpu.CompilerParams(vmem_limit_bytes=mib << 20),
         cost_estimate=pl.CostEstimate(
-            flops=flops, bytes_accessed=matmuls * MATMUL_SIZE // 128, transcendentals=0
+            flops=2 * work, bytes_accessed=work // LANES, transcendentals=0
         ),
         name=name,
     )(*args)
-
-
-MATMUL_SIZE = 256 * 3584 * 256
 
 
 def ring_per_device(
@@ -446,6 +441,7 @@
     half = gathered[0][0].shape[0]
     rows = 2 * half
     all_width = experts_here * width
+    work = experts_here * rows * model_width * width
 
     def streams_of(parts):
         used = sorted({piece[0] for piece in parts})
@@ -461,7 +457,7 @@
         [wide],
         14,
         (*arrays, gate_weight),
-        experts_here,
+        work,
     )
     arrays, parts = streams_of(in_parts)
     hidden, by_gate, by_up = call(
@@ -470,7 +466,7 @@
         [wide] * 3,
         16,
         (*arrays, gate_weight, up_weight, *sums),
-        3 * experts_here,
+        3 * work,
     )
     arrays, parts = streams_of(
         pieces(cuts, model_width, 2 * model_width, model_width)
@@ -488,7 +484,7 @@
         ],
         24,
         (*arrays, hidden, by_gate, by_up, gate_weight, up_weight, down_weight),
-        2 * experts_here,
+        2 * work,
     )
     more_near, more_far = call(
         functools.partial(spread_kernel, span),
@@ -499,42 +495,42 @@
         ],
         16,
         (acts, gate_weight, up_weight),
-        experts_here,
-    )
-
-    def weight_grad(kernel, name, start, value, shape, after):
+        work,
+    )
+
+    def weight_grad(kernel, name, start, value, after, outs, staged):
         arrays, parts = streams_of(pieces(cuts, start, start + model_width, 1280))
         return call(
             functools.partial(kernel, parts),
             name,
-            shaped(*shape),
-            12,
+            [shaped(*shape) for shape in outs],
+            20,
             (*arrays, value, after),
-            experts_here,
-            out_specs=ANY,
+            len(outs) * work,
+            out_specs=[ANY] * len(outs),
             scratch=[
-                pltpu.VMEM(shape, jnp.bfloat16),
-                pltpu.SemaphoreType.DMA((len(parts), experts_here)),
+                pltpu.VMEM(staged, jnp.bfloat16),
+                pltpu.SemaphoreType.DMA((len(parts), experts_here, len(outs))),
             ],
             anys=(len(arrays) + 1,),
         )
 
     in_shape, out_shape = (experts_here, model_width, width), (experts_here, width, model_width)
-    gate_kernel_grad = functools.partial(input_weight_kernel, 0)
-    up_kernel_grad = functools.partial(input_weight_kernel, 1)
     grad_input, made = reduce_ring(
         (dnear, more_near),
         (dfar, more_far),
         local_count,
         moves,
         [
-            lambda after: weight_grad(gate_kernel_grad, "gate_grad", 0, acts, in_shape, after),
-            lambda after: weight_grad(up_kernel_grad, "up_grad", 0, acts, in_shape, after),
             lambda after: weight_grad(
-                down_weight_kernel, "down_grad", model_width, hidden, out_shape, after
+                input_weight_kernel, "input_grads", 0, acts, after, [in_shape] * 2, (2, *in_shape)
+            ),
+            lambda after: weight_grad(
+                down_weight_kernel, "down_grad", model_width, hidden, after, [out_shape], out_shape
             ),
         ],
     )
+    made = [value for values in made for value in values]
     return (grad_input, *made)
 
 

time: 58 us -> 57.9 us (level)
  starting transfers between devices: 30.5 us -> 31.8 us
  Pallas kernels: 13 us -> 11.8 us
    ppermute x25, starting transfers between devices: 30.5 us -> 31.8 us  [move(): return lax.ppermute(value, ('node', 'local'), pairs)]
    pallas_call x7 -> x6, Pallas kernels: 13 us -> 11.8 us  [call(): pl.pallas_call(kernel, in_specs=[ANY if i in anys else VMEM for i in rang...]
  transfers between devices with their start and end apart: 25 -> 25, of which waited for: 7 -> 6; matrix products, arithmetic and copies ran while one was open for 2% -> 2% of each run, Pallas kernels for 18% -> 16%
where the time goes in v5:
time: 57.9 us; the launch traced here: 57.6 us
  starting transfers between devices  31.8 us (55%)
  Pallas kernels  11.8 us (20%)
  waiting for transfers between devices  9.49 us (16%)
  other arithmetic  2.93 us (5%)
  between operations  0.95 us (2%)
  local copies, waits for them, and re-layouts  0.74 us (1%)
    ppermute x25, starting transfers between devices, move(): return lax.ppermute(value, ('node', 'local'), pairs)  31.8 us
    pallas_call x6, Pallas kernels, call(): pl.pallas_call(kernel, in_specs=[ANY if i in anys else VMEM for i in rang...  11.8 us
    ppermute x25, waiting for transfers between devices, move(): return lax.ppermute(value, ('node', 'local'), pairs)  9.49 us
  transfers between devices with their start and end apart: 25, of which 6 were waited for; matrix products, arithmetic and copies ran while one was open for 2% of the time, Pallas kernels for 16%

profile of v5, /device:TPU:0, one launch (start us, length us, event | category | flops | bytes accessed | tf_op | source)
XLA Modules:
  0.0 57.6 jit_solution(8390288162749413444)
XLA Ops:
  0.6 1.1 %pad_maximum_fusion = bf16[16,7168]{1,0:T(8,128)(2,1)S(1)} fusion(bf16[16,3584]{1,0:T(8,128)(2,1)} %param.7, bf16[16,3584]{1,0:T(8,128)(2,1)} %param.8), kind=kLoop, calls=%fused_computation.9 | loop fusion | flops 458752 | bytes 458752 | tf_op jit(solution)/shard_map/concatenate | solution.py:435
  3.4 3.0 %collective-permute-start.12 = (bf16[32,2432]{1,0:T(8,128)(2,1)S(1)}, bf16[32,2432]{1,0:T(8,128)(2,1)S(1)}, u32[]{:S(2)}, u32[]{:S(2)}) collective-permute-start(bf16[32,2432]{1,0:T(8,128)(2,1)S(1)} %get-tuple-element.48), channel_id=1, source_target_pairs={{0,1},{1,2},{2,3},{3,11},{11,10},{10,9},{9,8},{8,0},{4,12},{5,4},{... | collective-permute-start | bytes 466952 | tf_op jit(solution)/shard_map/ppermute | solution.py:176
  6.4 1.6 %collective-permute-start.1 = (bf16[32,2432]{1,0:T(8,128)(2,1)S(1)}, bf16[32,2432]{1,0:T(8,128)(2,1)S(1)}, u32[]{:S(2)}, u32[]{:S(2)}) collective-permute-start(bf16[32,2432]{1,0:T(8,128)(2,1)S(1)} %get-tuple-element.49), channel_id=1, source_target_pairs={{0,1},{1,2},{2,3},{3,11},{11,10},{10,9},{9,8},{8,0},{4,12},{5,4},{... | collective-permute-start | bytes 466952 | tf_op jit(solution)/shard_map/ppermute | solution.py:176
  8.0 1.6 %collective-permute-start.7 = (bf16[32,2432]{1,0:T(8,128)(2,1)S(1)}, bf16[32,2432]{1,0:T(8,128)(2,1)S(1)}, u32[]{:S(2)}, u32[]{:S(2)}) collective-permute-start(bf16[32,2432]{1,0:T(8,128)(2,1)S(1)} %maximum_maximum_fusion), channel_id=1, source_target_pairs={{0,1},{1,2},{2,3},{3,11},{11,10},{10,9},{9,8},{8,0},{4,12},{5,4},{... | collective-permute-start | bytes 466952 | tf_op jit(solution)/shard_map/ppermute | solution.py:176
  9.7 2.0 %collective-permute-start.13 = (bf16[32,2432]{1,0:T(8,128)(2,1)S(1)}, bf16[32,2432]{1,0:T(8,128)(2,1)S(1)}, u32[]{:S(2)}, u32[]{:S(2)}) collective-permute-start(bf16[32,2432]{1,0:T(8,128)(2,1)S(1)} %collective-permute-done.12), channel_id=1, source_target_pairs={{0,1},{1,2},{2,3},{3,11},{11,10},{10,9},{9,8},{8,0},{4,12},{5,4},{... | collective-permute-start | bytes 466952 | tf_op jit(solution)/shard_map/ppermute | solution.py:176
  11.7 1.7 %collective-permute-start.2 = (bf16[32,2432]{1,0:T(8,128)(2,1)S(1)}, bf16[32,2432]{1,0:T(8,128)(2,1)S(1)}, u32[]{:S(2)}, u32[]{:S(2)}) collective-permute-start(bf16[32,2432]{1,0:T(8,128)(2,1)S(1)} %collective-permute-done.1), channel_id=1, source_target_pairs={{0,1},{1,2},{2,3},{3,11},{11,10},{10,9},{9,8},{8,0},{4,12},{5,4},{... | collective-permute-start | bytes 466952 | tf_op jit(solution)/shard_map/ppermute | solution.py:176
  13.3 1.7 %collective-permute-start.8 = (bf16[32,2432]{1,0:T(8,128)(2,1)S(1)}, bf16[32,2432]{1,0:T(8,128)(2,1)S(1)}, u32[]{:S(2)}, u32[]{:S(2)}) collective-permute-start(bf16[32,2432]{1,0:T(8,128)(2,1)S(1)} %collective-permute-done.7), channel_id=1, source_target_pairs={{0,1},{1,2},{2,3},{3,11},{11,10},{10,9},{9,8},{8,0},{4,12},{5,4},{... | collective-permute-start | bytes 466952 | tf_op jit(solution)/shard_map/ppermute | solution.py:176
  15.1 1.8 %collective-permute-start.14 = (bf16[32,2432]{1,0:T(8,128)(2,1)S(1)}, bf16[32,2432]{1,0:T(8,128)(2,1)S(1)}, u32[]{:S(2)}, u32[]{:S(2)}) collective-permute-start(bf16[32,2432]{1,0:T(8,128)(2,1)S(1)} %collective-permute-done.13), channel_id=1, source_target_pairs={{0,1},{1,2},{2,3},{3,11},{11,10},{10,9},{9,8},{8,0},{4,12},{5,4},{... | collective-permute-start | bytes 466952 | tf_op jit(solution)/shard_map/ppermute | solution.py:176
  16.9 1.7 %collective-permute-start.3 = (bf16[32,2432]{1,0:T(8,128)(2,1)S(1)}, bf16[32,2432]{1,0:T(8,128)(2,1)S(1)}, u32[]{:S(2)}, u32[]{:S(2)}) collective-permute-start(bf16[32,2432]{1,0:T(8,128)(2,1)S(1)} %collective-permute-done.2), channel_id=1, source_target_pairs={{0,1},{1,2},{2,3},{3,11},{11,10},{10,9},{9,8},{8,0},{4,12},{5,4},{... | collective-permute-start | bytes 466952 | tf_op jit(solution)/shard_map/ppermute | solution.py:176
  18.6 1.7 %collective-permute-start.9 = (bf16[32,2432]{1,0:T(8,128)(2,1)S(1)}, bf16[32,2432]{1,0:T(8,128)(2,1)S(1)}, u32[]{:S(2)}, u32[]{:S(2)}) collective-permute-start(bf16[32,2432]{1,0:T(8,128)(2,1)S(1)} %collective-permute-done.8), channel_id=1, source_target_pairs={{0,1},{1,2},{2,3},{3,11},{11,10},{10,9},{9,8},{8,0},{4,12},{5,4},{... | collective-permute-start | bytes 466952 | tf_op jit(solution)/shard_map/ppermute | solution.py:176
  20.4 1.8 %collective-permute-start.15 = (bf16[16,2432]{1,0:T(8,128)(2,1)S(1)}, bf16[16,2432]{1,0:T(8,128)(2,1)S(1)}, u32[]{:S(2)}, u32[]{:S(2)}) collective-permute-start(bf16[16,2432]{1,0:T(8,128)(2,1)S(1)} %slice.143), channel_id=1, source_target_pairs={{0,1},{1,2},{2,3},{3,11},{11,10},{10,9},{9,8},{8,0},{4,12},{5,4},{... | collective-permute-start | bytes 233480 | tf_op jit(solution)/shard_map/ppermute | solution.py:176
  22.1 1.7 %collective-permute-start.4 = (bf16[16,2432]{1,0:T(8,128)(2,1)S(1)}, bf16[16,2432]{1,0:T(8,128)(2,1)S(1)}, u32[]{:S(2)}, u32[]{:S(2)}) collective-permute-start(bf16[16,2432]{1,0:T(8,128)(2,1)S(1)} %slice.137), channel_id=1, source_target_pairs={{0,1},{1,2},{2,3},{3,11},{11,10},{10,9},{9,8},{8,0},{4,12},{5,4},{... | collective-permute-start | bytes 233480 | tf_op jit(solution)/shard_map/ppermute | solution.py:176
  23.8 1.7 %collective-permute-start.10 = (bf16[16,2432]{1,0:T(8,128)(2,1)S(1)}, bf16[16,2432]{1,0:T(8,128)(2,1)S(1)}, u32[]{:S(2)}, u32[]{:S(2)}) collective-permute-start(bf16[16,2432]{1,0:T(8,128)(2,1)S(1)} %slice.141), channel_id=1, source_target_pairs={{0,1},{1,2},{2,3},{3,11},{11,10},{10,9},{9,8},{8,0},{4,12},{5,4},{... | collective-permute-start | bytes 233480 | tf_op jit(solution)/shard_map/ppermute | solution.py:176
  26.7 1.6 %collective-permute-done.10 = bf16[16,2432]{1,0:T(8,128)(2,1)S(1)} collective-permute-done((bf16[16,2432]{1,0:T(8,128)(2,1)S(1)}, bf16[16,2432]{1,0:T(8,128)(2,1)S(1)}, u32[]{:S(2)}, u32[]{:S(2)}) %collective-permute-start.10) | collective-permute-done | bytes 77856 | tf_op jit(solution)/shard_map/ppermute | solution.py:176
  29.3 1.5 %finish.1 = (f32[256,512]{1,0:T(8,128)S(1)}, f32[256,512]{1,0:T(8,128)S(1)}, f32[256,512]{1,0:T(8,128)S(1)}) custom-call(bf16[128,2432]{1,0:T(8,128)(2,1)S(1)} %constant_dynamic-update-slice_fusion.8.refs_0_, bf16[128,2432]{1,0:T(8,128)(2,1)S(1)} %collective-permute-done.16.refs_1_, bf16[128,2432]{1,0:T(8,128)(2,1)S(1)} %constant_dynamic-update-slice_fusion.refs_2_.refs_0_, ...), custom_call_target="tpu_custom_call" | custom-call | flops 2818572288 | bytes 11010048 | tf_op jit(solution)/shard_map/finish/pallas_call | solution.py:409
  31.3 2.3 %backward.1 = (f32[128,1792]{1,0:T(8,128)S(1)}, bf16[128,1792]{1,0:T(8,128)(2,1)S(1)}, bf16[256,1024]{1,0:T(8,128)(2,1)S(1)}, bf16[256,512]{1,0:T(8,128)(2,1)S(1)}) custom-call(bf16[128,2432]{1,0:T(8,128)(2,1)S(1)} %constant_dynamic-update-slice_fusion.refs_2_.refs_0_, bf16[128,2432]{1,0:T(8,128)(2,1)S(1)} %collective-permute-done.5.refs_3_.refs_1_, ...), custom_call_target="tpu_custom_call" | custom-call | flops 1879048192 | bytes 7340032 | tf_op jit(solution)/shard_map/backward/pallas_call | solution.py:409
  34.1 1.2 %spread.1 = (f32[128,1792]{1,0:T(8,128)S(1)}, bf16[128,1792]{1,0:T(8,128)(2,1)S(1)}) custom-call(bf16[256,1024]{1,0:T(8,128)(2,1)S(1)} %get-tuple-element.27.acts_ref.refs_4_, bf16[2,3584,256]{2,1,0:T(8,128)(2,1)S(1)} %copy-done, bf16[2,3584,256]{2,1,0:T(8,128)(2,1)S(1)} %copy-done.1), custom_call_target="tpu_custom_call" | custom-call | flops 939524096 | bytes 3670016 | tf_op jit(solution)/shard_map/spread/pallas_call | solution.py:409
  35.6 2.6 %collective-permute-start.20 = (bf16[32,1792]{1,0:T(8,128)(2,1)S(1)}, bf16[32,1792]{1,0:T(8,128)(2,1)S(1)}, u32[]{:S(2)}, u32[]{:S(2)}) collective-permute-start(bf16[32,1792]{1,0:T(8,128)(2,1)S(1)} %get-tuple-element.42), channel_id=1, source_target_pairs={{0,9},{4,6},{1,8},{5,7},{2,0},{6,15},{3,1},{7,14},{11,2},{15,13},{... | collective-permute-start | bytes 344072 | tf_op jit(solution)/shard_map/ppermute | solution.py:176
  38.3 1.6 %collective-permute-start.19 = (bf16[32,3584]{1,0:T(8,128)(2,1)S(1)}, bf16[32,3584]{1,0:T(8,128)(2,1)S(1)}, u32[]{:S(2)}, u32[]{:S(2)}) collective-permute-start(bf16[32,3584]{1,0:T(8,128)(2,1)S(1)} %pad_maximum_fusion.1.refs_5_), channel_id=1, source_target_pairs={{0,8},{4,5},{1,0},{5,6},{2,1},{6,7},{3,2},{7,15},{11,3},{15,14},{1... | collective-permute-start | bytes 688136 | tf_op jit(solution)/shard_map/ppermute | solution.py:176
  40.0 2.6 %collective-permute-start.22 = (bf16[16,3584]{1,0:T(8,128)(2,1)S(1)}, bf16[16,3584]{1,0:T(8,128)(2,1)S(1)}, u32[]{:S(2)}, u32[]{:S(2)}) collective-permute-start(bf16[16,3584]{1,0:T(8,128)(2,1)S(1)} %pad_maximum_fusion.4), channel_id=1, source_target_pairs={{0,10},{4,7},{1,9},{5,15},{2,8},{6,14},{3,0},{7,13},{11,1},{15,12}... | collective-permute-start | bytes 344072 | tf_op jit(solution)/shard_map/ppermute | solution.py:176
  43.1 3.6 %input_grads.1 = (bf16[2,3584,256]{2,1,0:T(8,128)(2,1)}, bf16[2,3584,256]{2,1,0:T(8,128)(2,1)}) custom-call(bf16[128,2432]{1,0:T(8,128)(2,1)S(1)} %constant_dynamic-update-slice_fusion.8.refs_0_, bf16[128,2432]{1,0:T(8,128)(2,1)S(1)} %collective-permute-done.16.refs_1_, bf16[128,2432]{1,0:T(8,128)(2,1)S(1)} %constant_dynamic-update-slice_fusion.refs_2_.refs_0_, ...), custom_call_target="tpu_custom_call" | custom-call | flops 1879048192 | bytes 7340032 | tf_op jit(solution)/shard_map/input_grads/pallas_call | solution.py:409
  46.7 4.6 %collective-permute-done.21 = bf16[32,1792]{1,0:T(8,128)(2,1)S(1)} collective-permute-done((bf16[32,1792]{1,0:T(8,128)(2,1)S(1)}, bf16[32,1792]{1,0:T(8,128)(2,1)S(1)}, u32[]{:S(2)}, u32[]{:S(2)}) %collective-permute-start.21) | collective-permute-done | bytes 114720 | tf_op jit(solution)/shard_map/ppermute | solution.py:176
  52.7 2.3 %down_grad.1 = bf16[2,256,3584]{2,1,0:T(8,128)(2,1)} custom-call(bf16[128,2432]{1,0:T(8,128)(2,1)S(1)} %constant_dynamic-update-slice_fusion.refs_2_.refs_0_, bf16[128,2432]{1,0:T(8,128)(2,1)S(1)} %collective-permute-done.5.refs_3_.refs_1_, bf16[128,2432]{1,0:T(8,128)(2,1)S(1)} %constant_dynamic-update-slice_fusion.4.refs_2_, ...), custom_call_target="tpu_custom_call" | custom-call | flops 939524096 | bytes 3670016 | tf_op jit(solution)/shard_map/down_grad/pallas_call | solution.py:409
  55.0 2.0 %collective-permute-done.23 = bf16[16,3584]{1,0:T(8,128)(2,1)S(1)} collective-permute-done((bf16[16,3584]{1,0:T(8,128)(2,1)S(1)}, bf16[16,3584]{1,0:T(8,128)(2,1)S(1)}, u32[]{:S(2)}, u32[]{:S(2)}) %collective-permute-start.23) | collective-permute-done | bytes 114720 | tf_op jit(solution)/shard_map/ppermute | solution.py:176
  (72 shorter events, 7.8 us)
Async XLA Ops:
  3.1 4.9 %collective-permute-start.6 = (bf16[16,128]{1,0:T(8,128)(2,1)S(1)}, bf16[16,128]{1,0:T(8,128)(2,1)S(1)}, u32[]{:S(2)}, u32[]{:S(2)}) collective-permute-start(bf16[16,128]{1,0:T(8,128)(2,1)S(1)} %multiply_convert_fusion), channel_id=1, source_target_pairs={{0,4},{4,0},{1,5},{5,1},{2,6},{6,2},{3,7},{7,3},{11,15},{15,11},{1... | collective-permute-start | bytes 12296 | tf_op jit(solution)/shard_map/ppermute | solution.py:176
  3.4 6.3 %collective-permute-start.12 = (bf16[32,2432]{1,0:T(8,128)(2,1)S(1)}, bf16[32,2432]{1,0:T(8,128)(2,1)S(1)}, u32[]{:S(2)}, u32[]{:S(2)}) collective-permute-start(bf16[32,2432]{1,0:T(8,128)(2,1)S(1)} %get-tuple-element.48), channel_id=1, source_target_pairs={{0,1},{1,2},{2,3},{3,11},{11,10},{10,9},{9,8},{8,0},{4,12},{5,4},{... | collective-permute-start | bytes 466952 | tf_op jit(solution)/shard_map/ppermute | solution.py:176
  6.4 5.2 %collective-permute-start.1 = (bf16[32,2432]{1,0:T(8,128)(2,1)S(1)}, bf16[32,2432]{1,0:T(8,128)(2,1)S(1)}, u32[]{:S(2)}, u32[]{:S(2)}) collective-permute-start(bf16[32,2432]{1,0:T(8,128)(2,1)S(1)} %get-tuple-element.49), channel_id=1, source_target_pairs={{0,1},{1,2},{2,3},{3,11},{11,10},{10,9},{9,8},{8,0},{4,12},{5,4},{... | collective-permute-start | bytes 466952 | tf_op jit(solution)/shard_map/ppermute | solution.py:176
  8.0 5.3 %collective-permute-start.7 = (bf16[32,2432]{1,0:T(8,128)(2,1)S(1)}, bf16[32,2432]{1,0:T(8,128)(2,1)S(1)}, u32[]{:S(2)}, u32[]{:S(2)}) collective-permute-start(bf16[32,2432]{1,0:T(8,128)(2,1)S(1)} %maximum_maximum_fusion), channel_id=1, source_target_pairs={{0,1},{1,2},{2,3},{3,11},{11,10},{10,9},{9,8},{8,0},{4,12},{5,4},{... | collective-permute-start | bytes 466952 | tf_op jit(solution)/shard_map/ppermute | solution.py:176
  9.7 5.4 %collective-permute-start.13 = (bf16[32,2432]{1,0:T(8,128)(2,1)S(1)}, bf16[32,2432]{1,0:T(8,128)(2,1)S(1)}, u32[]{:S(2)}, u32[]{:S(2)}) collective-permute-start(bf16[32,2432]{1,0:T(8,128)(2,1)S(1)} %collective-permute-done.12), channel_id=1, source_target_pairs={{0,1},{1,2},{2,3},{3,11},{11,10},{10,9},{9,8},{8,0},{4,12},{5,4},{... | collective-permute-start | bytes 466952 | tf_op jit(solution)/shard_map/ppermute | solution.py:176
  11.7 5.2 %collective-permute-start.2 = (bf16[32,2432]{1,0:T(8,128)(2,1)S(1)}, bf16[32,2432]{1,0:T(8,128)(2,1)S(1)}, u32[]{:S(2)}, u32[]{:S(2)}) collective-permute-start(bf16[32,2432]{1,0:T(8,128)(2,1)S(1)} %collective-permute-done.1), channel_id=1, source_target_pairs={{0,1},{1,2},{2,3},{3,11},{11,10},{10,9},{9,8},{8,0},{4,12},{5,4},{... | collective-permute-start | bytes 466952 | tf_op jit(solution)/shard_map/ppermute | solution.py:176
  13.3 5.2 %collective-permute-start.8 = (bf16[32,2432]{1,0:T(8,128)(2,1)S(1)}, bf16[32,2432]{1,0:T(8,128)(2,1)S(1)}, u32[]{:S(2)}, u32[]{:S(2)}) collective-permute-start(bf16[32,2432]{1,0:T(8,128)(2,1)S(1)} %collective-permute-done.7), channel_id=1, source_target_pairs={{0,1},{1,2},{2,3},{3,11},{11,10},{10,9},{9,8},{8,0},{4,12},{5,4},{... | collective-permute-start | bytes 466952 | tf_op jit(solution)/shard_map/ppermute | solution.py:176
  15.1 5.3 %collective-permute-start.14 = (bf16[32,2432]{1,0:T(8,128)(2,1)S(1)}, bf16[32,2432]{1,0:T(8,128)(2,1)S(1)}, u32[]{:S(2)}, u32[]{:S(2)}) collective-permute-start(bf16[32,2432]{1,0:T(8,128)(2,1)S(1)} %collective-permute-done.13), channel_id=1, source_target_pairs={{0,1},{1,2},{2,3},{3,11},{11,10},{10,9},{9,8},{8,0},{4,12},{5,4},{... | collective-permute-start | bytes 466952 | tf_op jit(solution)/shard_map/ppermute | solution.py:176
  16.9 5.2 %collective-permute-start.3 = (bf16[32,2432]{1,0:T(8,128)(2,1)S(1)}, bf16[32,2432]{1,0:T(8,128)(2,1)S(1)}, u32[]{:S(2)}, u32[]{:S(2)}) collective-permute-start(bf16[32,2432]{1,0:T(8,128)(2,1)S(1)} %collective-permute-done.2), channel_id=1, source_target_pairs={{0,1},{1,2},{2,3},{3,11},{11,10},{10,9},{9,8},{8,0},{4,12},{5,4},{... | collective-permute-start | bytes 466952 | tf_op jit(solution)/shard_map/ppermute | solution.py:176
  18.6 5.3 %collective-permute-start.9 = (bf16[32,2432]{1,0:T(8,128)(2,1)S(1)}, bf16[32,2432]{1,0:T(8,128)(2,1)S(1)}, u32[]{:S(2)}, u32[]{:S(2)}) collective-permute-start(bf16[32,2432]{1,0:T(8,128)(2,1)S(1)} %collective-permute-done.8), channel_id=1, source_target_pairs={{0,1},{1,2},{2,3},{3,11},{11,10},{10,9},{9,8},{8,0},{4,12},{5,4},{... | collective-permute-start | bytes 466952 | tf_op jit(solution)/shard_map/ppermute | solution.py:176
  20.4 5.2 %collective-permute-start.15 = (bf16[16,2432]{1,0:T(8,128)(2,1)S(1)}, bf16[16,2432]{1,0:T(8,128)(2,1)S(1)}, u32[]{:S(2)}, u32[]{:S(2)}) collective-permute-start(bf16[16,2432]{1,0:T(8,128)(2,1)S(1)} %slice.143), channel_id=1, source_target_pairs={{0,1},{1,2},{2,3},{3,11},{11,10},{10,9},{9,8},{8,0},{4,12},{5,4},{... | collective-permute-start | bytes 233480 | tf_op jit(solution)/shard_map/ppermute | solution.py:176
  22.1 4.4 %collective-permute-start.4 = (bf16[16,2432]{1,0:T(8,128)(2,1)S(1)}, bf16[16,2432]{1,0:T(8,128)(2,1)S(1)}, u32[]{:S(2)}, u32[]{:S(2)}) collective-permute-start(bf16[16,2432]{1,0:T(8,128)(2,1)S(1)} %slice.137), channel_id=1, source_target_pairs={{0,1},{1,2},{2,3},{3,11},{11,10},{10,9},{9,8},{8,0},{4,12},{5,4},{... | collective-permute-start | bytes 233480 | tf_op jit(solution)/shard_map/ppermute | solution.py:176
  23.8 4.4 %collective-permute-start.10 = (bf16[16,2432]{1,0:T(8,128)(2,1)S(1)}, bf16[16,2432]{1,0:T(8,128)(2,1)S(1)}, u32[]{:S(2)}, u32[]{:S(2)}) collective-permute-start(bf16[16,2432]{1,0:T(8,128)(2,1)S(1)} %slice.141), channel_id=1, source_target_pairs={{0,1},{1,2},{2,3},{3,11},{11,10},{10,9},{9,8},{8,0},{4,12},{5,4},{... | collective-permute-start | bytes 233480 | tf_op jit(solution)/shard_map/ppermute | solution.py:176
  25.6 2.8 %collective-permute-start.16 = (bf16[128,2432]{1,0:T(8,128)(2,1)S(1)}, bf16[128,2432]{1,0:T(8,128)(2,1)S(1)}, u32[]{:S(2)}, u32[]{:S(2)}) collective-permute-start(bf16[128,2432]{1,0:T(8,128)(2,1)S(1)} %constant_dynamic-update-slice_fusion.8.refs_0_), channel_id=1, source_target_pairs={{0,4},{4,0},{1,5},{5,1},{2,6},{6,2},{3,7},{7,3},{11,15},{15,11},{1... | collective-permute-start | bytes 1867784 | tf_op jit(solution)/shard_map/ppermute | solution.py:176
  26.6 2.7 %collective-permute-start.5 = (bf16[128,2432]{1,0:T(8,128)(2,1)S(1)}, bf16[128,2432]{1,0:T(8,128)(2,1)S(1)}, u32[]{:S(2)}, u32[]{:S(2)}) collective-permute-start(bf16[128,2432]{1,0:T(8,128)(2,1)S(1)} %constant_dynamic-update-slice_fusion.refs_2_.refs_0_), channel_id=1, source_target_pairs={{0,4},{4,0},{1,5},{5,1},{2,6},{6,2},{3,7},{7,3},{11,15},{15,11},{1... | collective-permute-start | bytes 1867784 | tf_op jit(solution)/shard_map/ppermute | solution.py:176
  28.3 2.5 %collective-permute-start.11 = (bf16[128,2432]{1,0:T(8,128)(2,1)S(1)}, bf16[128,2432]{1,0:T(8,128)(2,1)S(1)}, u32[]{:S(2)}, u32[]{:S(2)}) collective-permute-start(bf16[128,2432]{1,0:T(8,128)(2,1)S(1)} %constant_dynamic-update-slice_fusion.4.refs_2_), channel_id=1, source_target_pairs={{0,4},{4,0},{1,5},{5,1},{2,6},{6,2},{3,7},{7,3},{11,15},{15,11},{1... | collective-permute-start | bytes 1867784 | tf_op jit(solution)/shard_map/ppermute | solution.py:176
  33.6 2.0 %collective-permute-start.17 = (bf16[128,1792]{1,0:T(8,128)(2,1)S(1)}, bf16[128,1792]{1,0:T(8,128)(2,1)S(1)}, u32[]{:S(2)}, u32[]{:S(2)}) collective-permute-start(bf16[128,1792]{1,0:T(8,128)(2,1)S(1)} %get-tuple-element.26), channel_id=1, source_target_pairs={{0,4},{4,0},{1,5},{5,1},{2,6},{6,2},{3,7},{7,3},{11,15},{15,11},{1... | collective-permute-start | bytes 1376264 | tf_op jit(solution)/shard_map/ppermute | solution.py:176
  35.4 2.8 %collective-permute-start.18 = (bf16[128,1792]{1,0:T(8,128)(2,1)S(1)}, bf16[128,1792]{1,0:T(8,128)(2,1)S(1)}, u32[]{:S(2)}, u32[]{:S(2)}) collective-permute-start(bf16[128,1792]{1,0:T(8,128)(2,1)S(1)} %get-tuple-element.29), channel_id=1, source_target_pairs={{0,4},{4,0},{1,5},{5,1},{2,6},{6,2},{3,7},{7,3},{11,15},{15,11},{1... | collective-permute-start | bytes 1376264 | tf_op jit(solution)/shard_map/ppermute | solution.py:176
  35.6 11.1 %collective-permute-start.20 = (bf16[32,1792]{1,0:T(8,128)(2,1)S(1)}, bf16[32,1792]{1,0:T(8,128)(2,1)S(1)}, u32[]{:S(2)}, u32[]{:S(2)}) collective-permute-start(bf16[32,1792]{1,0:T(8,128)(2,1)S(1)} %get-tuple-element.42), channel_id=1, source_target_pairs={{0,9},{4,6},{1,8},{5,7},{2,0},{6,15},{3,1},{7,14},{11,2},{15,13},{... | collective-permute-start | bytes 344072 | tf_op jit(solution)/shard_map/ppermute | solution.py:176
  38.3 8.4 %collective-permute-start.19 = (bf16[32,3584]{1,0:T(8,128)(2,1)S(1)}, bf16[32,3584]{1,0:T(8,128)(2,1)S(1)}, u32[]{:S(2)}, u32[]{:S(2)}) collective-permute-start(bf16[32,3584]{1,0:T(8,128)(2,1)S(1)} %pad_maximum_fusion.1.refs_5_), channel_id=1, source_target_pairs={{0,8},{4,5},{1,0},{5,6},{2,1},{6,7},{3,2},{7,15},{11,3},{15,14},{1... | collective-permute-start | bytes 688136 | tf_op jit(solution)/shard_map/ppermute | solution.py:176
  40.0 12.1 %collective-permute-start.22 = (bf16[16,3584]{1,0:T(8,128)(2,1)S(1)}, bf16[16,3584]{1,0:T(8,128)(2,1)S(1)}, u32[]{:S(2)}, u32[]{:S(2)}) collective-permute-start(bf16[16,3584]{1,0:T(8,128)(2,1)S(1)} %pad_maximum_fusion.4), channel_id=1, source_target_pairs={{0,10},{4,7},{1,9},{5,15},{2,8},{6,14},{3,0},{7,13},{11,1},{15,12}... | collective-permute-start | bytes 344072 | tf_op jit(solution)/shard_map/ppermute | solution.py:176
  42.7 8.6 %collective-permute-start.21 = (bf16[32,1792]{1,0:T(8,128)(2,1)S(1)}, bf16[32,1792]{1,0:T(8,128)(2,1)S(1)}, u32[]{:S(2)}, u32[]{:S(2)}) collective-permute-start(bf16[32,1792]{1,0:T(8,128)(2,1)S(1)} %get-tuple-element.45), channel_id=1, source_target_pairs={{0,9},{4,6},{1,8},{5,7},{2,0},{6,15},{3,1},{7,14},{11,2},{15,13},{... | collective-permute-start | bytes 344072 | tf_op jit(solution)/shard_map/ppermute | solution.py:176
  51.4 5.6 %collective-permute-start.24 = (bf16[16,3584]{1,0:T(8,128)(2,1)S(1)}, bf16[16,3584]{1,0:T(8,128)(2,1)S(1)}, u32[]{:S(2)}, u32[]{:S(2)}) collective-permute-start(bf16[16,3584]{1,0:T(8,128)(2,1)S(1)} %slice.196), channel_id=1, source_target_pairs={{1,4},{2,5},{3,6},{11,7},{10,15},{9,14},{8,13},{0,12},{12,0},{4,1}... | collective-permute-start | bytes 344072 | tf_op jit(solution)/shard_map/ppermute | solution.py:176
  52.1 4.8 %collective-permute-start.23 = (bf16[16,3584]{1,0:T(8,128)(2,1)S(1)}, bf16[16,3584]{1,0:T(8,128)(2,1)S(1)}, u32[]{:S(2)}, u32[]{:S(2)}) collective-permute-start(bf16[16,3584]{1,0:T(8,128)(2,1)S(1)} %fusion.1), channel_id=1, source_target_pairs={{0,8},{4,5},{1,0},{5,6},{2,1},{6,7},{3,2},{7,15},{11,3},{15,14},{1... | collective-permute-start | bytes 344072 | tf_op jit(solution)/shard_map/ppermute | solution.py:176
  (4 other events, 40.4 us)

commit v6 on v5

--- a/solution.py
+++ b/solution.py
@@ -216,25 +216,29 @@
     def own(start, count):
         return jnp.concatenate([part(i, start, count) for i in range(len(near))], axis=1)
 
-    blocks = [own((2 * hops - 1) * rows, 2 * rows) for hops in range(1, local_count)]
-    blocks.append(own(half - rows, rows))
-    sent = [block.astype(jnp.bfloat16) for block in blocks]
-    moved = []
-    for hops, value in enumerate(sent):
-        if hops == 2:
-            early = [
-                part(i, (2 * hops + 1) * rows, 2 * rows).astype(jnp.bfloat16)
-                for i in range(len(near))
-            ]
-            value = jnp.concatenate([move(piece, backs[hops]) for piece in early], axis=1)
-            moved.append(value)
-        elif hops:
-            moved.append(move(value, backs[hops]))
-    moved[0] = with_work(moved[0], sent[1])
-    held = blocks[0]
-    for value in moved[:-1]:
-        held = held + value.astype(wide)
-    held = jnp.concatenate([held[:rows] + moved[-1].astype(wide), held[rows:]], axis=0)
+    far_block = jnp.concatenate(
+        [
+            move(part(i, half - rows, rows).astype(jnp.bfloat16), backs[local_count - 1])
+            for i in range(2)
+        ],
+        axis=1,
+    )
+    straight, passed = [], None
+    for hops in reversed(range(1, local_count - 1)):
+        at = (2 * hops + 1) * rows
+        value = part(0, at, 2 * rows)
+        if passed is not None:
+            value = value + passed.astype(wide)
+        value = value.astype(jnp.bfloat16)
+        passed = move(value, backs[1])
+        straight.append(move(part(1, at, 2 * rows).astype(jnp.bfloat16), backs[hops]))
+    straight[-1] = with_work(straight[-1], value)
+    held = [part(i, rows, 2 * rows) for i in range(2)]
+    held[0] = held[0] + passed.astype(wide)
+    for value in straight:
+        held[1] = held[1] + value.astype(wide)
+    held = jnp.concatenate(held, axis=1)
+    held = jnp.concatenate([held[:rows] + far_block.astype(wide), held[rows:]], axis=0)
     held = held.astype(jnp.bfloat16)
     moving = with_work(move(held[:rows], backs[1]), held)
     crossed = move(held[rows:], back_swap)
@@ -535,7 +539,8 @@
 
 
 def solution(mesh):
-    per_device = ring_per_device if mesh.shape["node"] == LIMIT else slots_per_device
+    every_group = mesh.shape["node"] == LIMIT and mesh.shape["local"] > 2
+    per_device = ring_per_device if every_group else slots_per_device
     in_specs = (
         P(("rep", "node", "local"), None),
         P(("rep", "node", "local"), None),

time: 57.9 us -> 57.4 us (level)
  waiting for transfers between devices: 9.49 us -> 7.23 us
  starting transfers between devices: 31.8 us -> 33.6 us
    ppermute x25 -> x27, waiting for transfers between devices: 9.49 us -> 7.23 us  [move(): return lax.ppermute(value, ('node', 'local'), pairs)]
    ppermute x25 -> x27, starting transfers between devices: 31.8 us -> 33.6 us  [move(): return lax.ppermute(value, ('node', 'local'), pairs)]
  transfers between devices with their start and end apart: 25 -> 27, of which waited for: 6 -> 7; matrix products, arithmetic and copies ran while one was open for 2% -> 2% of each run, Pallas kernels for 16% -> 17%
where the time goes in v6:
time: 57.4 us; the launch traced here: 57.2 us
  starting transfers between devices  33.6 us (59%)
  Pallas kernels  11.8 us (21%)
  waiting for transfers between devices  7.23 us (13%)
  other arithmetic  2.92 us (5%)
  between operations  0.95 us (2%)
  local copies, waits for them, and re-layouts  0.72 us (1%)
    ppermute x27, starting transfers between devices, move(): return lax.ppermute(value, ('node', 'local'), pairs)  33.6 us
    pallas_call x6, Pallas kernels, call(): pl.pallas_call(kernel, in_specs=[ANY if i in anys else VMEM for i in rang...  11.8 us
    ppermute x27, waiting for transfers between devices, move(): return lax.ppermute(value, ('node', 'local'), pairs)  7.23 us
  transfers between devices with their start and end apart: 27, of which 7 were waited for; matrix products, arithmetic and copies ran while one was open for 2% of the time, Pallas kernels for 17%

profile of v6, /device:TPU:0, one launch (start us, length us, event | category | flops | bytes accessed | tf_op | source)
XLA Modules:
  0.0 57.2 jit_solution(14951917483263610216)
XLA Ops:
  3.4 3.0 %collective-permute-start.12 = (bf16[32,2432]{1,0:T(8,128)(2,1)S(1)}, bf16[32,2432]{1,0:T(8,128)(2,1)S(1)}, u32[]{:S(2)}, u32[]{:S(2)}) collective-permute-start(bf16[32,2432]{1,0:T(8,128)(2,1)S(1)} %get-tuple-element.44), channel_id=1, source_target_pairs={{0,1},{1,2},{2,3},{3,11},{11,10},{10,9},{9,8},{8,0},{4,12},{5,4},{... | collective-permute-start | bytes 466952 | tf_op jit(solution)/shard_map/ppermute | solution.py:176
  6.4 1.6 %collective-permute-start.1 = (bf16[32,2432]{1,0:T(8,128)(2,1)S(1)}, bf16[32,2432]{1,0:T(8,128)(2,1)S(1)}, u32[]{:S(2)}, u32[]{:S(2)}) collective-permute-start(bf16[32,2432]{1,0:T(8,128)(2,1)S(1)} %get-tuple-element.45), channel_id=1, source_target_pairs={{0,1},{1,2},{2,3},{3,11},{11,10},{10,9},{9,8},{8,0},{4,12},{5,4},{... | collective-permute-start | bytes 466952 | tf_op jit(solution)/shard_map/ppermute | solution.py:176
  8.0 1.6 %collective-permute-start.7 = (bf16[32,2432]{1,0:T(8,128)(2,1)S(1)}, bf16[32,2432]{1,0:T(8,128)(2,1)S(1)}, u32[]{:S(2)}, u32[]{:S(2)}) collective-permute-start(bf16[32,2432]{1,0:T(8,128)(2,1)S(1)} %maximum_maximum_fusion), channel_id=1, source_target_pairs={{0,1},{1,2},{2,3},{3,11},{11,10},{10,9},{9,8},{8,0},{4,12},{5,4},{... | collective-permute-start | bytes 466952 | tf_op jit(solution)/shard_map/ppermute | solution.py:176
  9.7 2.0 %collective-permute-start.13 = (bf16[32,2432]{1,0:T(8,128)(2,1)S(1)}, bf16[32,2432]{1,0:T(8,128)(2,1)S(1)}, u32[]{:S(2)}, u32[]{:S(2)}) collective-permute-start(bf16[32,2432]{1,0:T(8,128)(2,1)S(1)} %collective-permute-done.12), channel_id=1, source_target_pairs={{0,1},{1,2},{2,3},{3,11},{11,10},{10,9},{9,8},{8,0},{4,12},{5,4},{... | collective-permute-start | bytes 466952 | tf_op jit(solution)/shard_map/ppermute | solution.py:176
  11.7 1.7 %collective-permute-start.2 = (bf16[32,2432]{1,0:T(8,128)(2,1)S(1)}, bf16[32,2432]{1,0:T(8,128)(2,1)S(1)}, u32[]{:S(2)}, u32[]{:S(2)}) collective-permute-start(bf16[32,2432]{1,0:T(8,128)(2,1)S(1)} %collective-permute-done.1), channel_id=1, source_target_pairs={{0,1},{1,2},{2,3},{3,11},{11,10},{10,9},{9,8},{8,0},{4,12},{5,4},{... | collective-permute-start | bytes 466952 | tf_op jit(solution)/shard_map/ppermute | solution.py:176
  13.3 1.7 %collective-permute-start.8 = (bf16[32,2432]{1,0:T(8,128)(2,1)S(1)}, bf16[32,2432]{1,0:T(8,128)(2,1)S(1)}, u32[]{:S(2)}, u32[]{:S(2)}) collective-permute-start(bf16[32,2432]{1,0:T(8,128)(2,1)S(1)} %collective-permute-done.7), channel_id=1, source_target_pairs={{0,1},{1,2},{2,3},{3,11},{11,10},{10,9},{9,8},{8,0},{4,12},{5,4},{... | collective-permute-start | bytes 466952 | tf_op jit(solution)/shard_map/ppermute | solution.py:176
  15.1 1.8 %collective-permute-start.14 = (bf16[32,2432]{1,0:T(8,128)(2,1)S(1)}, bf16[32,2432]{1,0:T(8,128)(2,1)S(1)}, u32[]{:S(2)}, u32[]{:S(2)}) collective-permute-start(bf16[32,2432]{1,0:T(8,128)(2,1)S(1)} %collective-permute-done.13), channel_id=1, source_target_pairs={{0,1},{1,2},{2,3},{3,11},{11,10},{10,9},{9,8},{8,0},{4,12},{5,4},{... | collective-permute-start | bytes 466952 | tf_op jit(solution)/shard_map/ppermute | solution.py:176
  16.9 1.7 %collective-permute-start.3 = (bf16[32,2432]{1,0:T(8,128)(2,1)S(1)}, bf16[32,2432]{1,0:T(8,128)(2,1)S(1)}, u32[]{:S(2)}, u32[]{:S(2)}) collective-permute-start(bf16[32,2432]{1,0:T(8,128)(2,1)S(1)} %collective-permute-done.2), channel_id=1, source_target_pairs={{0,1},{1,2},{2,3},{3,11},{11,10},{10,9},{9,8},{8,0},{4,12},{5,4},{... | collective-permute-start | bytes 466952 | tf_op jit(solution)/shard_map/ppermute | solution.py:176
  18.6 1.7 %collective-permute-start.9 = (bf16[32,2432]{1,0:T(8,128)(2,1)S(1)}, bf16[32,2432]{1,0:T(8,128)(2,1)S(1)}, u32[]{:S(2)}, u32[]{:S(2)}) collective-permute-start(bf16[32,2432]{1,0:T(8,128)(2,1)S(1)} %collective-permute-done.8), channel_id=1, source_target_pairs={{0,1},{1,2},{2,3},{3,11},{11,10},{10,9},{9,8},{8,0},{4,12},{5,4},{... | collective-permute-start | bytes 466952 | tf_op jit(solution)/shard_map/ppermute | solution.py:176
  20.4 1.8 %collective-permute-start.15 = (bf16[16,2432]{1,0:T(8,128)(2,1)S(1)}, bf16[16,2432]{1,0:T(8,128)(2,1)S(1)}, u32[]{:S(2)}, u32[]{:S(2)}) collective-permute-start(bf16[16,2432]{1,0:T(8,128)(2,1)S(1)} %slice.143), channel_id=1, source_target_pairs={{0,1},{1,2},{2,3},{3,11},{11,10},{10,9},{9,8},{8,0},{4,12},{5,4},{... | collective-permute-start | bytes 233480 | tf_op jit(solution)/shard_map/ppermute | solution.py:176
  22.1 1.7 %collective-permute-start.4 = (bf16[16,2432]{1,0:T(8,128)(2,1)S(1)}, bf16[16,2432]{1,0:T(8,128)(2,1)S(1)}, u32[]{:S(2)}, u32[]{:S(2)}) collective-permute-start(bf16[16,2432]{1,0:T(8,128)(2,1)S(1)} %slice.137), channel_id=1, source_target_pairs={{0,1},{1,2},{2,3},{3,11},{11,10},{10,9},{9,8},{8,0},{4,12},{5,4},{... | collective-permute-start | bytes 233480 | tf_op jit(solution)/shard_map/ppermute | solution.py:176
  23.8 1.7 %collective-permute-start.10 = (bf16[16,2432]{1,0:T(8,128)(2,1)S(1)}, bf16[16,2432]{1,0:T(8,128)(2,1)S(1)}, u32[]{:S(2)}, u32[]{:S(2)}) collective-permute-start(bf16[16,2432]{1,0:T(8,128)(2,1)S(1)} %slice.141), channel_id=1, source_target_pairs={{0,1},{1,2},{2,3},{3,11},{11,10},{10,9},{9,8},{8,0},{4,12},{5,4},{... | collective-permute-start | bytes 233480 | tf_op jit(solution)/shard_map/ppermute | solution.py:176
  26.7 1.6 %collective-permute-done.10 = bf16[16,2432]{1,0:T(8,128)(2,1)S(1)} collective-permute-done((bf16[16,2432]{1,0:T(8,128)(2,1)S(1)}, bf16[16,2432]{1,0:T(8,128)(2,1)S(1)}, u32[]{:S(2)}, u32[]{:S(2)}) %collective-permute-start.10) | collective-permute-done | bytes 77856 | tf_op jit(solution)/shard_map/ppermute | solution.py:176
  29.3 1.5 %finish.1 = (f32[256,512]{1,0:T(8,128)S(1)}, f32[256,512]{1,0:T(8,128)S(1)}, f32[256,512]{1,0:T(8,128)S(1)}) custom-call(bf16[128,2432]{1,0:T(8,128)(2,1)S(1)} %constant_dynamic-update-slice_fusion.8.refs_0_, bf16[128,2432]{1,0:T(8,128)(2,1)S(1)} %collective-permute-done.16.refs_1_, bf16[128,2432]{1,0:T(8,128)(2,1)S(1)} %constant_dynamic-update-slice_fusion.refs_2_.refs_0_, ...), custom_call_target="tpu_custom_call" | custom-call | flops 2818572288 | bytes 11010048 | tf_op jit(solution)/shard_map/finish/pallas_call | solution.py:413
  31.3 2.3 %backward.1 = (f32[128,1792]{1,0:T(8,128)S(1)}, bf16[128,1792]{1,0:T(8,128)(2,1)S(1)}, bf16[256,1024]{1,0:T(8,128)(2,1)S(1)}, bf16[256,512]{1,0:T(8,128)(2,1)S(1)}) custom-call(bf16[128,2432]{1,0:T(8,128)(2,1)S(1)} %constant_dynamic-update-slice_fusion.refs_2_.refs_0_, bf16[128,2432]{1,0:T(8,128)(2,1)S(1)} %collective-permute-done.5.refs_3_.refs_1_, ...), custom_call_target="tpu_custom_call" | custom-call | flops 1879048192 | bytes 7340032 | tf_op jit(solution)/shard_map/backward/pallas_call | solution.py:413
  34.1 1.2 %spread.1 = (f32[128,1792]{1,0:T(8,128)S(1)}, bf16[128,1792]{1,0:T(8,128)(2,1)S(1)}) custom-call(bf16[256,1024]{1,0:T(8,128)(2,1)S(1)} %get-tuple-element.27.acts_ref.refs_4_, bf16[2,3584,256]{2,1,0:T(8,128)(2,1)S(1)} %copy-done, bf16[2,3584,256]{2,1,0:T(8,128)(2,1)S(1)} %copy-done.1), custom_call_target="tpu_custom_call" | custom-call | flops 939524096 | bytes 3670016 | tf_op jit(solution)/shard_map/spread/pallas_call | solution.py:413
  35.6 1.6 %collective-permute-start.19 = (bf16[32,1792]{1,0:T(8,128)(2,1)S(1)}, bf16[32,1792]{1,0:T(8,128)(2,1)S(1)}, u32[]{:S(2)}, u32[]{:S(2)}) collective-permute-start(bf16[32,1792]{1,0:T(8,128)(2,1)S(1)} %add_convert_fusion.3), channel_id=1, source_target_pairs={{0,8},{4,5},{1,0},{5,6},{2,1},{6,7},{3,2},{7,15},{11,3},{15,14},{1... | collective-permute-start | bytes 344072 | tf_op jit(solution)/shard_map/ppermute | solution.py:176
  37.2 3.7 %collective-permute-start.23 = (bf16[16,1792]{1,0:T(8,128)(2,1)S(1)}, bf16[16,1792]{1,0:T(8,128)(2,1)S(1)}, u32[]{:S(2)}, u32[]{:S(2)}) collective-permute-start(bf16[16,1792]{1,0:T(8,128)(2,1)S(1)} %get-tuple-element.38), channel_id=1, source_target_pairs={{0,10},{4,7},{1,9},{5,15},{2,8},{6,14},{3,0},{7,13},{11,1},{15,12}... | collective-permute-start | bytes 172040 | tf_op jit(solution)/shard_map/ppermute | solution.py:176
  41.0 1.7 %collective-permute-start.21 = (bf16[32,1792]{1,0:T(8,128)(2,1)S(1)}, bf16[32,1792]{1,0:T(8,128)(2,1)S(1)}, u32[]{:S(2)}, u32[]{:S(2)}) collective-permute-start(bf16[32,1792]{1,0:T(8,128)(2,1)S(1)} %get-tuple-element.42), channel_id=1, source_target_pairs={{0,9},{4,6},{1,8},{5,7},{2,0},{6,15},{3,1},{7,14},{11,2},{15,13},{... | collective-permute-start | bytes 344072 | tf_op jit(solution)/shard_map/ppermute | solution.py:176
  43.4 1.6 %collective-permute-start.20 = (bf16[32,1792]{1,0:T(8,128)(2,1)S(1)}, bf16[32,1792]{1,0:T(8,128)(2,1)S(1)}, u32[]{:S(2)}, u32[]{:S(2)}) collective-permute-start(bf16[32,1792]{1,0:T(8,128)(2,1)S(1)} %add_convert_fusion.2.refs_5_), channel_id=1, source_target_pairs={{0,8},{4,5},{1,0},{5,6},{2,1},{6,7},{3,2},{7,15},{11,3},{15,14},{1... | collective-permute-start | bytes 344072 | tf_op jit(solution)/shard_map/ppermute | solution.py:176
  45.1 3.6 %input_grads.1 = (bf16[2,3584,256]{2,1,0:T(8,128)(2,1)}, bf16[2,3584,256]{2,1,0:T(8,128)(2,1)}) custom-call(bf16[128,2432]{1,0:T(8,128)(2,1)S(1)} %constant_dynamic-update-slice_fusion.8.refs_0_, bf16[128,2432]{1,0:T(8,128)(2,1)S(1)} %collective-permute-done.16.refs_1_, bf16[128,2432]{1,0:T(8,128)(2,1)S(1)} %constant_dynamic-update-slice_fusion.refs_2_.refs_0_, ...), custom_call_target="tpu_custom_call" | custom-call | flops 1879048192 | bytes 7340032 | tf_op jit(solution)/shard_map/input_grads/pallas_call | solution.py:413
  48.7 1.6 %collective-permute-done.22 = bf16[32,1792]{1,0:T(8,128)(2,1)S(1)} collective-permute-done((bf16[32,1792]{1,0:T(8,128)(2,1)S(1)}, bf16[32,1792]{1,0:T(8,128)(2,1)S(1)}, u32[]{:S(2)}, u32[]{:S(2)}) %collective-permute-start.22) | collective-permute-done | bytes 114720 | tf_op jit(solution)/shard_map/ppermute | solution.py:176
  52.7 2.3 %down_grad.1 = bf16[2,256,3584]{2,1,0:T(8,128)(2,1)} custom-call(bf16[128,2432]{1,0:T(8,128)(2,1)S(1)} %constant_dynamic-update-slice_fusion.refs_2_.refs_0_, bf16[128,2432]{1,0:T(8,128)(2,1)S(1)} %collective-permute-done.5.refs_3_.refs_1_, bf16[128,2432]{1,0:T(8,128)(2,1)S(1)} %constant_dynamic-update-slice_fusion.4.refs_2_, ...), custom_call_target="tpu_custom_call" | custom-call | flops 939524096 | bytes 3670016 | tf_op jit(solution)/shard_map/down_grad/pallas_call | solution.py:413
  55.0 1.5 %collective-permute-done.25 = bf16[16,3584]{1,0:T(8,128)(2,1)S(1)} collective-permute-done((bf16[16,3584]{1,0:T(8,128)(2,1)S(1)}, bf16[16,3584]{1,0:T(8,128)(2,1)S(1)}, u32[]{:S(2)}, u32[]{:S(2)}) %collective-permute-start.25) | collective-permute-done | bytes 114720 | tf_op jit(solution)/shard_map/ppermute | solution.py:176
  (76 shorter events, 10.3 us)
Async XLA Ops:
  3.1 4.9 %collective-permute-start.6 = (bf16[16,128]{1,0:T(8,128)(2,1)S(1)}, bf16[16,128]{1,0:T(8,128)(2,1)S(1)}, u32[]{:S(2)}, u32[]{:S(2)}) collective-permute-start(bf16[16,128]{1,0:T(8,128)(2,1)S(1)} %multiply_convert_fusion), channel_id=1, source_target_pairs={{0,4},{4,0},{1,5},{5,1},{2,6},{6,2},{3,7},{7,3},{11,15},{15,11},{1... | collective-permute-start | bytes 12296 | tf_op jit(solution)/shard_map/ppermute | solution.py:176
  3.4 6.3 %collective-permute-start.12 = (bf16[32,2432]{1,0:T(8,128)(2,1)S(1)}, bf16[32,2432]{1,0:T(8,128)(2,1)S(1)}, u32[]{:S(2)}, u32[]{:S(2)}) collective-permute-start(bf16[32,2432]{1,0:T(8,128)(2,1)S(1)} %get-tuple-element.44), channel_id=1, source_target_pairs={{0,1},{1,2},{2,3},{3,11},{11,10},{10,9},{9,8},{8,0},{4,12},{5,4},{... | collective-permute-start | bytes 466952 | tf_op jit(solution)/shard_map/ppermute | solution.py:176
  6.4 5.2 %collective-permute-start.1 = (bf16[32,2432]{1,0:T(8,128)(2,1)S(1)}, bf16[32,2432]{1,0:T(8,128)(2,1)S(1)}, u32[]{:S(2)}, u32[]{:S(2)}) collective-permute-start(bf16[32,2432]{1,0:T(8,128)(2,1)S(1)} %get-tuple-element.45), channel_id=1, source_target_pairs={{0,1},{1,2},{2,3},{3,11},{11,10},{10,9},{9,8},{8,0},{4,12},{5,4},{... | collective-permute-start | bytes 466952 | tf_op jit(solution)/shard_map/ppermute | solution.py:176
  8.0 5.3 %collective-permute-start.7 = (bf16[32,2432]{1,0:T(8,128)(2,1)S(1)}, bf16[32,2432]{1,0:T(8,128)(2,1)S(1)}, u32[]{:S(2)}, u32[]{:S(2)}) collective-permute-start(bf16[32,2432]{1,0:T(8,128)(2,1)S(1)} %maximum_maximum_fusion), channel_id=1, source_target_pairs={{0,1},{1,2},{2,3},{3,11},{11,10},{10,9},{9,8},{8,0},{4,12},{5,4},{... | collective-permute-start | bytes 466952 | tf_op jit(solution)/shard_map/ppermute | solution.py:176
  9.7 5.4 %collective-permute-start.13 = (bf16[32,2432]{1,0:T(8,128)(2,1)S(1)}, bf16[32,2432]{1,0:T(8,128)(2,1)S(1)}, u32[]{:S(2)}, u32[]{:S(2)}) collective-permute-start(bf16[32,2432]{1,0:T(8,128)(2,1)S(1)} %collective-permute-done.12), channel_id=1, source_target_pairs={{0,1},{1,2},{2,3},{3,11},{11,10},{10,9},{9,8},{8,0},{4,12},{5,4},{... | collective-permute-start | bytes 466952 | tf_op jit(solution)/shard_map/ppermute | solution.py:176
  11.7 5.2 %collective-permute-start.2 = (bf16[32,2432]{1,0:T(8,128)(2,1)S(1)}, bf16[32,2432]{1,0:T(8,128)(2,1)S(1)}, u32[]{:S(2)}, u32[]{:S(2)}) collective-permute-start(bf16[32,2432]{1,0:T(8,128)(2,1)S(1)} %collective-permute-done.1), channel_id=1, source_target_pairs={{0,1},{1,2},{2,3},{3,11},{11,10},{10,9},{9,8},{8,0},{4,12},{5,4},{... | collective-permute-start | bytes 466952 | tf_op jit(solution)/shard_map/ppermute | solution.py:176
  13.3 5.2 %collective-permute-start.8 = (bf16[32,2432]{1,0:T(8,128)(2,1)S(1)}, bf16[32,2432]{1,0:T(8,128)(2,1)S(1)}, u32[]{:S(2)}, u32[]{:S(2)}) collective-permute-start(bf16[32,2432]{1,0:T(8,128)(2,1)S(1)} %collective-permute-done.7), channel_id=1, source_target_pairs={{0,1},{1,2},{2,3},{3,11},{11,10},{10,9},{9,8},{8,0},{4,12},{5,4},{... | collective-permute-start | bytes 466952 | tf_op jit(solution)/shard_map/ppermute | solution.py:176
  15.1 5.3 %collective-permute-start.14 = (bf16[32,2432]{1,0:T(8,128)(2,1)S(1)}, bf16[32,2432]{1,0:T(8,128)(2,1)S(1)}, u32[]{:S(2)}, u32[]{:S(2)}) collective-permute-start(bf16[32,2432]{1,0:T(8,128)(2,1)S(1)} %collective-permute-done.13), channel_id=1, source_target_pairs={{0,1},{1,2},{2,3},{3,11},{11,10},{10,9},{9,8},{8,0},{4,12},{5,4},{... | collective-permute-start | bytes 466952 | tf_op jit(solution)/shard_map/ppermute | solution.py:176
  16.9 5.2 %collective-permute-start.3 = (bf16[32,2432]{1,0:T(8,128)(2,1)S(1)}, bf16[32,2432]{1,0:T(8,128)(2,1)S(1)}, u32[]{:S(2)}, u32[]{:S(2)}) collective-permute-start(bf16[32,2432]{1,0:T(8,128)(2,1)S(1)} %collective-permute-done.2), channel_id=1, source_target_pairs={{0,1},{1,2},{2,3},{3,11},{11,10},{10,9},{9,8},{8,0},{4,12},{5,4},{... | collective-permute-start | bytes 466952 | tf_op jit(solution)/shard_map/ppermute | solution.py:176
  18.6 5.3 %collective-permute-start.9 = (bf16[32,2432]{1,0:T(8,128)(2,1)S(1)}, bf16[32,2432]{1,0:T(8,128)(2,1)S(1)}, u32[]{:S(2)}, u32[]{:S(2)}) collective-permute-start(bf16[32,2432]{1,0:T(8,128)(2,1)S(1)} %collective-permute-done.8), channel_id=1, source_target_pairs={{0,1},{1,2},{2,3},{3,11},{11,10},{10,9},{9,8},{8,0},{4,12},{5,4},{... | collective-permute-start | bytes 466952 | tf_op jit(solution)/shard_map/ppermute | solution.py:176
  20.4 5.2 %collective-permute-start.15 = (bf16[16,2432]{1,0:T(8,128)(2,1)S(1)}, bf16[16,2432]{1,0:T(8,128)(2,1)S(1)}, u32[]{:S(2)}, u32[]{:S(2)}) collective-permute-start(bf16[16,2432]{1,0:T(8,128)(2,1)S(1)} %slice.143), channel_id=1, source_target_pairs={{0,1},{1,2},{2,3},{3,11},{11,10},{10,9},{9,8},{8,0},{4,12},{5,4},{... | collective-permute-start | bytes 233480 | tf_op jit(solution)/shard_map/ppermute | solution.py:176
  22.1 4.4 %collective-permute-start.4 = (bf16[16,2432]{1,0:T(8,128)(2,1)S(1)}, bf16[16,2432]{1,0:T(8,128)(2,1)S(1)}, u32[]{:S(2)}, u32[]{:S(2)}) collective-permute-start(bf16[16,2432]{1,0:T(8,128)(2,1)S(1)} %slice.137), channel_id=1, source_target_pairs={{0,1},{1,2},{2,3},{3,11},{11,10},{10,9},{9,8},{8,0},{4,12},{5,4},{... | collective-permute-start | bytes 233480 | tf_op jit(solution)/shard_map/ppermute | solution.py:176
  23.8 4.4 %collective-permute-start.10 = (bf16[16,2432]{1,0:T(8,128)(2,1)S(1)}, bf16[16,2432]{1,0:T(8,128)(2,1)S(1)}, u32[]{:S(2)}, u32[]{:S(2)}) collective-permute-start(bf16[16,2432]{1,0:T(8,128)(2,1)S(1)} %slice.141), channel_id=1, source_target_pairs={{0,1},{1,2},{2,3},{3,11},{11,10},{10,9},{9,8},{8,0},{4,12},{5,4},{... | collective-permute-start | bytes 233480 | tf_op jit(solution)/shard_map/ppermute | solution.py:176
  25.6 2.8 %collective-permute-start.16 = (bf16[128,2432]{1,0:T(8,128)(2,1)S(1)}, bf16[128,2432]{1,0:T(8,128)(2,1)S(1)}, u32[]{:S(2)}, u32[]{:S(2)}) collective-permute-start(bf16[128,2432]{1,0:T(8,128)(2,1)S(1)} %constant_dynamic-update-slice_fusion.8.refs_0_), channel_id=1, source_target_pairs={{0,4},{4,0},{1,5},{5,1},{2,6},{6,2},{3,7},{7,3},{11,15},{15,11},{1... | collective-permute-start | bytes 1867784 | tf_op jit(solution)/shard_map/ppermute | solution.py:176
  26.6 2.7 %collective-permute-start.5 = (bf16[128,2432]{1,0:T(8,128)(2,1)S(1)}, bf16[128,2432]{1,0:T(8,128)(2,1)S(1)}, u32[]{:S(2)}, u32[]{:S(2)}) collective-permute-start(bf16[128,2432]{1,0:T(8,128)(2,1)S(1)} %constant_dynamic-update-slice_fusion.refs_2_.refs_0_), channel_id=1, source_target_pairs={{0,4},{4,0},{1,5},{5,1},{2,6},{6,2},{3,7},{7,3},{11,15},{15,11},{1... | collective-permute-start | bytes 1867784 | tf_op jit(solution)/shard_map/ppermute | solution.py:176
  35.4 5.5 %collective-permute-start.18 = (bf16[128,1792]{1,0:T(8,128)(2,1)S(1)}, bf16[128,1792]{1,0:T(8,128)(2,1)S(1)}, u32[]{:S(2)}, u32[]{:S(2)}) collective-permute-start(bf16[128,1792]{1,0:T(8,128)(2,1)S(1)} %get-tuple-element.29), channel_id=1, source_target_pairs={{0,4},{4,0},{1,5},{5,1},{2,6},{6,2},{3,7},{7,3},{11,15},{15,11},{1... | collective-permute-start | bytes 1376264 | tf_op jit(solution)/shard_map/ppermute | solution.py:176
  35.6 7.8 %collective-permute-start.19 = (bf16[32,1792]{1,0:T(8,128)(2,1)S(1)}, bf16[32,1792]{1,0:T(8,128)(2,1)S(1)}, u32[]{:S(2)}, u32[]{:S(2)}) collective-permute-start(bf16[32,1792]{1,0:T(8,128)(2,1)S(1)} %add_convert_fusion.3), channel_id=1, source_target_pairs={{0,8},{4,5},{1,0},{5,6},{2,1},{6,7},{3,2},{7,15},{11,3},{15,14},{1... | collective-permute-start | bytes 344072 | tf_op jit(solution)/shard_map/ppermute | solution.py:176
  37.2 14.4 %collective-permute-start.23 = (bf16[16,1792]{1,0:T(8,128)(2,1)S(1)}, bf16[16,1792]{1,0:T(8,128)(2,1)S(1)}, u32[]{:S(2)}, u32[]{:S(2)}) collective-permute-start(bf16[16,1792]{1,0:T(8,128)(2,1)S(1)} %get-tuple-element.38), channel_id=1, source_target_pairs={{0,10},{4,7},{1,9},{5,15},{2,8},{6,14},{3,0},{7,13},{11,1},{15,12}... | collective-permute-start | bytes 172040 | tf_op jit(solution)/shard_map/ppermute | solution.py:176
  40.9 10.8 %collective-permute-start.24 = (bf16[16,1792]{1,0:T(8,128)(2,1)S(1)}, bf16[16,1792]{1,0:T(8,128)(2,1)S(1)}, u32[]{:S(2)}, u32[]{:S(2)}) collective-permute-start(bf16[16,1792]{1,0:T(8,128)(2,1)S(1)} %get-tuple-element.40), channel_id=1, source_target_pairs={{0,10},{4,7},{1,9},{5,15},{2,8},{6,14},{3,0},{7,13},{11,1},{15,12}... | collective-permute-start | bytes 172040 | tf_op jit(solution)/shard_map/ppermute | solution.py:176
  41.0 9.3 %collective-permute-start.21 = (bf16[32,1792]{1,0:T(8,128)(2,1)S(1)}, bf16[32,1792]{1,0:T(8,128)(2,1)S(1)}, u32[]{:S(2)}, u32[]{:S(2)}) collective-permute-start(bf16[32,1792]{1,0:T(8,128)(2,1)S(1)} %get-tuple-element.42), channel_id=1, source_target_pairs={{0,9},{4,6},{1,8},{5,7},{2,0},{6,15},{3,1},{7,14},{11,2},{15,13},{... | collective-permute-start | bytes 344072 | tf_op jit(solution)/shard_map/ppermute | solution.py:176
  42.7 7.6 %collective-permute-start.22 = (bf16[32,1792]{1,0:T(8,128)(2,1)S(1)}, bf16[32,1792]{1,0:T(8,128)(2,1)S(1)}, u32[]{:S(2)}, u32[]{:S(2)}) collective-permute-start(bf16[32,1792]{1,0:T(8,128)(2,1)S(1)} %get-tuple-element.43), channel_id=1, source_target_pairs={{0,8},{4,5},{1,0},{5,6},{2,1},{6,7},{3,2},{7,15},{11,3},{15,14},{1... | collective-permute-start | bytes 344072 | tf_op jit(solution)/shard_map/ppermute | solution.py:176
  43.4 8.1 %collective-permute-start.20 = (bf16[32,1792]{1,0:T(8,128)(2,1)S(1)}, bf16[32,1792]{1,0:T(8,128)(2,1)S(1)}, u32[]{:S(2)}, u32[]{:S(2)}) collective-permute-start(bf16[32,1792]{1,0:T(8,128)(2,1)S(1)} %add_convert_fusion.2.refs_5_), channel_id=1, source_target_pairs={{0,8},{4,5},{1,0},{5,6},{2,1},{6,7},{3,2},{7,15},{11,3},{15,14},{1... | collective-permute-start | bytes 344072 | tf_op jit(solution)/shard_map/ppermute | solution.py:176
  51.6 5.0 %collective-permute-start.26 = (bf16[16,3584]{1,0:T(8,128)(2,1)S(1)}, bf16[16,3584]{1,0:T(8,128)(2,1)S(1)}, u32[]{:S(2)}, u32[]{:S(2)}) collective-permute-start(bf16[16,3584]{1,0:T(8,128)(2,1)S(1)} %fusion.3), channel_id=1, source_target_pairs={{1,4},{2,5},{3,6},{11,7},{10,15},{9,14},{8,13},{0,12},{12,0},{4,1}... | collective-permute-start | bytes 344072 | tf_op jit(solution)/shard_map/ppermute | solution.py:176
  51.7 4.8 %collective-permute-start.25 = (bf16[16,3584]{1,0:T(8,128)(2,1)S(1)}, bf16[16,3584]{1,0:T(8,128)(2,1)S(1)}, u32[]{:S(2)}, u32[]{:S(2)}) collective-permute-start(bf16[16,3584]{1,0:T(8,128)(2,1)S(1)} %fusion.2), channel_id=1, source_target_pairs={{0,8},{4,5},{1,0},{5,6},{2,1},{6,7},{3,2},{7,15},{11,3},{15,14},{1... | collective-permute-start | bytes 344072 | tf_op jit(solution)/shard_map/ppermute | solution.py:176
  (6 other events, 44.9 us)

commit v7 on v6

--- a/solution.py
+++ b/solution.py
@@ -179,7 +179,8 @@
 def gather_ring(mine, gates, cuts, local_count, moves):
     forth, _, swap, _ = moves
     rows = mine.shape[0]
-    pair = jnp.concatenate([mine, move(mine, swap)], axis=0)
+    other, gates = lax.optimization_barrier((move(mine, swap), gates))
+    pair = jnp.concatenate([mine, other], axis=0)
     gates = jnp.concatenate([gates, move(gates, swap)], axis=0)
     blocks = [pair[:, a:b] for a, b in zip(cuts[:-1], cuts[1:], strict=True)]
     blocks[-1] = jnp.concatenate([blocks[-1], gates], axis=1)
@@ -216,32 +217,34 @@
     def own(start, count):
         return jnp.concatenate([part(i, start, count) for i in range(len(near))], axis=1)
 
-    far_block = jnp.concatenate(
-        [
-            move(part(i, half - rows, rows).astype(jnp.bfloat16), backs[local_count - 1])
-            for i in range(2)
-        ],
-        axis=1,
-    )
+    last = half - rows
+    far_first = move(part(0, last, rows).astype(jnp.bfloat16), backs[local_count - 2])
+    far_last = move(part(1, last, rows).astype(jnp.bfloat16), backs[local_count - 1])
+
+    def topped(value, first):
+        return jnp.concatenate([value[:rows] + first.astype(wide), value[rows:]], axis=0)
+
     straight, passed = [], None
     for hops in reversed(range(1, local_count - 1)):
         at = (2 * hops + 1) * rows
         value = part(0, at, 2 * rows)
         if passed is not None:
             value = value + passed.astype(wide)
+        if hops == 1:
+            value = topped(value, far_first)
         value = value.astype(jnp.bfloat16)
         passed = move(value, backs[1])
         straight.append(move(part(1, at, 2 * rows).astype(jnp.bfloat16), backs[hops]))
-    straight[-1] = with_work(straight[-1], value)
+    straight[0] = with_work(straight[0], value)
     held = [part(i, rows, 2 * rows) for i in range(2)]
     held[0] = held[0] + passed.astype(wide)
     for value in straight:
         held[1] = held[1] + value.astype(wide)
+    held[1] = topped(held[1], far_last)
     held = jnp.concatenate(held, axis=1)
-    held = jnp.concatenate([held[:rows] + far_block.astype(wide), held[rows:]], axis=0)
     held = held.astype(jnp.bfloat16)
-    moving = with_work(move(held[:rows], backs[1]), held)
-    crossed = move(held[rows:], back_swap)
+    moving = move(held[:rows], backs[1])
+    crossed = with_work(move(held[rows:], back_swap), held)
     while len(made) < len(beside):
         made.append(beside[len(made)](held))
     total = own(0, rows) + moving.astype(wide) + crossed.astype(wide)

time: 57.4 us -> 57 us (level)
  transfers between devices with their start and end apart: 27 -> 27, of which waited for: 7 -> 11; matrix products, arithmetic and copies ran while one was open for 2% -> 2% of each run, Pallas kernels for 17% -> 17%
where the time goes in v7:
time: 57 us; the launch traced here: 56.8 us
  starting transfers between devices  33.3 us (58%)
  Pallas kernels  11.8 us (21%)
  waiting for transfers between devices  6.99 us (12%)
  other arithmetic  2.93 us (5%)
  between operations  0.97 us (2%)
  local copies, waits for them, and re-layouts  0.75 us (1%)
    ppermute x27, starting transfers between devices, move(): return lax.ppermute(value, ('node', 'local'), pairs)  33.3 us
    pallas_call x6, Pallas kernels, call(): pl.pallas_call(kernel, in_specs=[ANY if i in anys else VMEM for i in rang...  11.8 us
    ppermute x27, waiting for transfers between devices, move(): return lax.ppermute(value, ('node', 'local'), pairs)  6.99 us
  transfers between devices with their start and end apart: 27, of which 11 were waited for; matrix products, arithmetic and copies ran while one was open for 2% of the time, Pallas kernels for 17%

profile of v7, /device:TPU:0, one launch (start us, length us, event | category | flops | bytes accessed | tf_op | source)
XLA Modules:
  0.0 56.8 jit_solution(14156009384203068027)
XLA Ops:
  3.9 2.8 %collective-permute-start.12 = (bf16[32,2432]{1,0:T(8,128)(2,1)S(1)}, bf16[32,2432]{1,0:T(8,128)(2,1)S(1)}, u32[]{:S(2)}, u32[]{:S(2)}) collective-permute-start(bf16[32,2432]{1,0:T(8,128)(2,1)S(1)} %get-tuple-element.48), channel_id=1, source_target_pairs={{0,1},{1,2},{2,3},{3,11},{11,10},{10,9},{9,8},{8,0},{4,12},{5,4},{... | collective-permute-start | bytes 466952 | tf_op jit(solution)/shard_map/ppermute | solution.py:176
  6.6 1.6 %collective-permute-start.1 = (bf16[32,2432]{1,0:T(8,128)(2,1)S(1)}, bf16[32,2432]{1,0:T(8,128)(2,1)S(1)}, u32[]{:S(2)}, u32[]{:S(2)}) collective-permute-start(bf16[32,2432]{1,0:T(8,128)(2,1)S(1)} %get-tuple-element.49), channel_id=1, source_target_pairs={{0,1},{1,2},{2,3},{3,11},{11,10},{10,9},{9,8},{8,0},{4,12},{5,4},{... | collective-permute-start | bytes 466952 | tf_op jit(solution)/shard_map/ppermute | solution.py:176
  8.2 1.6 %collective-permute-start.7 = (bf16[32,2432]{1,0:T(8,128)(2,1)S(1)}, bf16[32,2432]{1,0:T(8,128)(2,1)S(1)}, u32[]{:S(2)}, u32[]{:S(2)}) collective-permute-start(bf16[32,2432]{1,0:T(8,128)(2,1)S(1)} %maximum_maximum_fusion.1), channel_id=1, source_target_pairs={{0,1},{1,2},{2,3},{3,11},{11,10},{10,9},{9,8},{8,0},{4,12},{5,4},{... | collective-permute-start | bytes 466952 | tf_op jit(solution)/shard_map/ppermute | solution.py:176
  9.9 2.0 %collective-permute-start.13 = (bf16[32,2432]{1,0:T(8,128)(2,1)S(1)}, bf16[32,2432]{1,0:T(8,128)(2,1)S(1)}, u32[]{:S(2)}, u32[]{:S(2)}) collective-permute-start(bf16[32,2432]{1,0:T(8,128)(2,1)S(1)} %collective-permute-done.12), channel_id=1, source_target_pairs={{0,1},{1,2},{2,3},{3,11},{11,10},{10,9},{9,8},{8,0},{4,12},{5,4},{... | collective-permute-start | bytes 466952 | tf_op jit(solution)/shard_map/ppermute | solution.py:176
  11.9 1.6 %collective-permute-start.2 = (bf16[32,2432]{1,0:T(8,128)(2,1)S(1)}, bf16[32,2432]{1,0:T(8,128)(2,1)S(1)}, u32[]{:S(2)}, u32[]{:S(2)}) collective-permute-start(bf16[32,2432]{1,0:T(8,128)(2,1)S(1)} %collective-permute-done.1), channel_id=1, source_target_pairs={{0,1},{1,2},{2,3},{3,11},{11,10},{10,9},{9,8},{8,0},{4,12},{5,4},{... | collective-permute-start | bytes 466952 | tf_op jit(solution)/shard_map/ppermute | solution.py:176
  13.6 1.6 %collective-permute-start.8 = (bf16[32,2432]{1,0:T(8,128)(2,1)S(1)}, bf16[32,2432]{1,0:T(8,128)(2,1)S(1)}, u32[]{:S(2)}, u32[]{:S(2)}) collective-permute-start(bf16[32,2432]{1,0:T(8,128)(2,1)S(1)} %collective-permute-done.7), channel_id=1, source_target_pairs={{0,1},{1,2},{2,3},{3,11},{11,10},{10,9},{9,8},{8,0},{4,12},{5,4},{... | collective-permute-start | bytes 466952 | tf_op jit(solution)/shard_map/ppermute | solution.py:176
  15.2 1.9 %collective-permute-start.14 = (bf16[32,2432]{1,0:T(8,128)(2,1)S(1)}, bf16[32,2432]{1,0:T(8,128)(2,1)S(1)}, u32[]{:S(2)}, u32[]{:S(2)}) collective-permute-start(bf16[32,2432]{1,0:T(8,128)(2,1)S(1)} %collective-permute-done.13), channel_id=1, source_target_pairs={{0,1},{1,2},{2,3},{3,11},{11,10},{10,9},{9,8},{8,0},{4,12},{5,4},{... | collective-permute-start | bytes 466952 | tf_op jit(solution)/shard_map/ppermute | solution.py:176
  17.2 1.6 %collective-permute-start.3 = (bf16[32,2432]{1,0:T(8,128)(2,1)S(1)}, bf16[32,2432]{1,0:T(8,128)(2,1)S(1)}, u32[]{:S(2)}, u32[]{:S(2)}) collective-permute-start(bf16[32,2432]{1,0:T(8,128)(2,1)S(1)} %collective-permute-done.2), channel_id=1, source_target_pairs={{0,1},{1,2},{2,3},{3,11},{11,10},{10,9},{9,8},{8,0},{4,12},{5,4},{... | collective-permute-start | bytes 466952 | tf_op jit(solution)/shard_map/ppermute | solution.py:176
  18.8 1.6 %collective-permute-start.9 = (bf16[32,2432]{1,0:T(8,128)(2,1)S(1)}, bf16[32,2432]{1,0:T(8,128)(2,1)S(1)}, u32[]{:S(2)}, u32[]{:S(2)}) collective-permute-start(bf16[32,2432]{1,0:T(8,128)(2,1)S(1)} %collective-permute-done.8), channel_id=1, source_target_pairs={{0,1},{1,2},{2,3},{3,11},{11,10},{10,9},{9,8},{8,0},{4,12},{5,4},{... | collective-permute-start | bytes 466952 | tf_op jit(solution)/shard_map/ppermute | solution.py:176
  20.5 1.8 %collective-permute-start.15 = (bf16[16,2432]{1,0:T(8,128)(2,1)S(1)}, bf16[16,2432]{1,0:T(8,128)(2,1)S(1)}, u32[]{:S(2)}, u32[]{:S(2)}) collective-permute-start(bf16[16,2432]{1,0:T(8,128)(2,1)S(1)} %slice.155), channel_id=1, source_target_pairs={{0,1},{1,2},{2,3},{3,11},{11,10},{10,9},{9,8},{8,0},{4,12},{5,4},{... | collective-permute-start | bytes 233480 | tf_op jit(solution)/shard_map/ppermute | solution.py:176
  22.4 1.6 %collective-permute-start.4 = (bf16[16,2432]{1,0:T(8,128)(2,1)S(1)}, bf16[16,2432]{1,0:T(8,128)(2,1)S(1)}, u32[]{:S(2)}, u32[]{:S(2)}) collective-permute-start(bf16[16,2432]{1,0:T(8,128)(2,1)S(1)} %slice.149), channel_id=1, source_target_pairs={{0,1},{1,2},{2,3},{3,11},{11,10},{10,9},{9,8},{8,0},{4,12},{5,4},{... | collective-permute-start | bytes 233480 | tf_op jit(solution)/shard_map/ppermute | solution.py:176
  24.1 1.6 %collective-permute-start.10 = (bf16[16,2432]{1,0:T(8,128)(2,1)S(1)}, bf16[16,2432]{1,0:T(8,128)(2,1)S(1)}, u32[]{:S(2)}, u32[]{:S(2)}) collective-permute-start(bf16[16,2432]{1,0:T(8,128)(2,1)S(1)} %slice.153), channel_id=1, source_target_pairs={{0,1},{1,2},{2,3},{3,11},{11,10},{10,9},{9,8},{8,0},{4,12},{5,4},{... | collective-permute-start | bytes 233480 | tf_op jit(solution)/shard_map/ppermute | solution.py:176
  26.9 1.6 %collective-permute-done.10 = bf16[16,2432]{1,0:T(8,128)(2,1)S(1)} collective-permute-done((bf16[16,2432]{1,0:T(8,128)(2,1)S(1)}, bf16[16,2432]{1,0:T(8,128)(2,1)S(1)}, u32[]{:S(2)}, u32[]{:S(2)}) %collective-permute-start.10) | collective-permute-done | bytes 77856 | tf_op jit(solution)/shard_map/ppermute | solution.py:176
  29.5 1.5 %finish.1 = (f32[256,512]{1,0:T(8,128)S(1)}, f32[256,512]{1,0:T(8,128)S(1)}, f32[256,512]{1,0:T(8,128)S(1)}) custom-call(bf16[128,2432]{1,0:T(8,128)(2,1)S(1)} %constant_dynamic-update-slice_fusion.8.refs_0_, bf16[128,2432]{1,0:T(8,128)(2,1)S(1)} %collective-permute-done.16.refs_1_, bf16[128,2432]{1,0:T(8,128)(2,1)S(1)} %constant_dynamic-update-slice_fusion.refs_2_.refs_0_, ...), custom_call_target="tpu_custom_call" | custom-call | flops 2818572288 | bytes 11010048 | tf_op jit(solution)/shard_map/finish/pallas_call | solution.py:416
  31.5 2.3 %backward.1 = (f32[128,1792]{1,0:T(8,128)S(1)}, bf16[128,1792]{1,0:T(8,128)(2,1)S(1)}, bf16[256,1024]{1,0:T(8,128)(2,1)S(1)}, bf16[256,512]{1,0:T(8,128)(2,1)S(1)}) custom-call(bf16[128,2432]{1,0:T(8,128)(2,1)S(1)} %constant_dynamic-update-slice_fusion.refs_2_.refs_0_, bf16[128,2432]{1,0:T(8,128)(2,1)S(1)} %collective-permute-done.5.refs_3_.refs_1_, ...), custom_call_target="tpu_custom_call" | custom-call | flops 1879048192 | bytes 7340032 | tf_op jit(solution)/shard_map/backward/pallas_call | solution.py:416
  34.4 1.2 %spread.1 = (f32[128,1792]{1,0:T(8,128)S(1)}, bf16[128,1792]{1,0:T(8,128)(2,1)S(1)}) custom-call(bf16[256,1024]{1,0:T(8,128)(2,1)S(1)} %get-tuple-element.31.acts_ref.refs_4_, bf16[2,3584,256]{2,1,0:T(8,128)(2,1)S(1)} %copy-done, bf16[2,3584,256]{2,1,0:T(8,128)(2,1)S(1)} %copy-done.1), custom_call_target="tpu_custom_call" | custom-call | flops 939524096 | bytes 3670016 | tf_op jit(solution)/shard_map/spread/pallas_call | solution.py:416
  35.9 1.5 %collective-permute-start.19 = (bf16[32,1792]{1,0:T(8,128)(2,1)S(1)}, bf16[32,1792]{1,0:T(8,128)(2,1)S(1)}, u32[]{:S(2)}, u32[]{:S(2)}) collective-permute-start(bf16[32,1792]{1,0:T(8,128)(2,1)S(1)} %add_convert_fusion.3), channel_id=1, source_target_pairs={{0,8},{4,5},{1,0},{5,6},{2,1},{6,7},{3,2},{7,15},{11,3},{15,14},{1... | collective-permute-start | bytes 344072 | tf_op jit(solution)/shard_map/ppermute | solution.py:176
  37.4 2.6 %collective-permute-start.20 = (bf16[16,1792]{1,0:T(8,128)(2,1)S(1)}, bf16[16,1792]{1,0:T(8,128)(2,1)S(1)}, u32[]{:S(2)}, u32[]{:S(2)}) collective-permute-start(bf16[16,1792]{1,0:T(8,128)(2,1)S(1)} %get-tuple-element.44), channel_id=1, source_target_pairs={{0,9},{4,6},{1,8},{5,7},{2,0},{6,15},{3,1},{7,14},{11,2},{15,13},{... | collective-permute-start | bytes 172040 | tf_op jit(solution)/shard_map/ppermute | solution.py:176
  40.1 1.6 %collective-permute-start.22 = (bf16[32,1792]{1,0:T(8,128)(2,1)S(1)}, bf16[32,1792]{1,0:T(8,128)(2,1)S(1)}, u32[]{:S(2)}, u32[]{:S(2)}) collective-permute-start(bf16[32,1792]{1,0:T(8,128)(2,1)S(1)} %get-tuple-element.46), channel_id=1, source_target_pairs={{0,9},{4,6},{1,8},{5,7},{2,0},{6,15},{3,1},{7,14},{11,2},{15,13},{... | collective-permute-start | bytes 344072 | tf_op jit(solution)/shard_map/ppermute | solution.py:176
  42.2 1.3 %collective-permute-start.24 = (bf16[16,1792]{1,0:T(8,128)(2,1)S(1)}, bf16[16,1792]{1,0:T(8,128)(2,1)S(1)}, u32[]{:S(2)}, u32[]{:S(2)}) collective-permute-start(bf16[16,1792]{1,0:T(8,128)(2,1)S(1)} %get-tuple-element.42), channel_id=1, source_target_pairs={{0,10},{4,7},{1,9},{5,15},{2,8},{6,14},{3,0},{7,13},{11,1},{15,12}... | collective-permute-start | bytes 172040 | tf_op jit(solution)/shard_map/ppermute | solution.py:176
  43.6 1.6 %collective-permute-start.21 = (bf16[32,1792]{1,0:T(8,128)(2,1)S(1)}, bf16[32,1792]{1,0:T(8,128)(2,1)S(1)}, u32[]{:S(2)}, u32[]{:S(2)}) collective-permute-start(bf16[32,1792]{1,0:T(8,128)(2,1)S(1)} %pad_maximum_fusion.2.refs_5_), channel_id=1, source_target_pairs={{0,8},{4,5},{1,0},{5,6},{2,1},{6,7},{3,2},{7,15},{11,3},{15,14},{1... | collective-permute-start | bytes 344072 | tf_op jit(solution)/shard_map/ppermute | solution.py:176
  45.2 3.6 %input_grads.1 = (bf16[2,3584,256]{2,1,0:T(8,128)(2,1)}, bf16[2,3584,256]{2,1,0:T(8,128)(2,1)}) custom-call(bf16[128,2432]{1,0:T(8,128)(2,1)S(1)} %constant_dynamic-update-slice_fusion.8.refs_0_, bf16[128,2432]{1,0:T(8,128)(2,1)S(1)} %collective-permute-done.16.refs_1_, bf16[128,2432]{1,0:T(8,128)(2,1)S(1)} %constant_dynamic-update-slice_fusion.refs_2_.refs_0_, ...), custom_call_target="tpu_custom_call" | custom-call | flops 1879048192 | bytes 7340032 | tf_op jit(solution)/shard_map/input_grads/pallas_call | solution.py:416
  49.1 1.8 %collective-permute-done.21 = bf16[32,1792]{1,0:T(8,128)(2,1)S(1)} collective-permute-done((bf16[32,1792]{1,0:T(8,128)(2,1)S(1)}, bf16[32,1792]{1,0:T(8,128)(2,1)S(1)}, u32[]{:S(2)}, u32[]{:S(2)}) %collective-permute-start.21) | collective-permute-done | bytes 114720 | tf_op jit(solution)/shard_map/ppermute | solution.py:176
  52.0 2.3 %down_grad.1 = bf16[2,256,3584]{2,1,0:T(8,128)(2,1)} custom-call(bf16[128,2432]{1,0:T(8,128)(2,1)S(1)} %constant_dynamic-update-slice_fusion.refs_2_.refs_0_, bf16[128,2432]{1,0:T(8,128)(2,1)S(1)} %collective-permute-done.5.refs_3_.refs_1_, bf16[128,2432]{1,0:T(8,128)(2,1)S(1)} %constant_dynamic-update-slice_fusion.4.refs_2_, ...), custom_call_target="tpu_custom_call" | custom-call | flops 939524096 | bytes 3670016 | tf_op jit(solution)/shard_map/down_grad/pallas_call | solution.py:416
  (80 shorter events, 11.5 us)
Async XLA Ops:
  3.4 4.8 %collective-permute-start.6 = (bf16[16,128]{1,0:T(8,128)(2,1)S(1)}, bf16[16,128]{1,0:T(8,128)(2,1)S(1)}, u32[]{:S(2)}, u32[]{:S(2)}) collective-permute-start(bf16[16,128]{1,0:T(8,128)(2,1)S(1)} %multiply_convert_fusion), channel_id=1, source_target_pairs={{0,4},{4,0},{1,5},{5,1},{2,6},{6,2},{3,7},{7,3},{11,15},{15,11},{1... | collective-permute-start | bytes 12296 | tf_op jit(solution)/shard_map/ppermute | solution.py:176
  3.9 6.0 %collective-permute-start.12 = (bf16[32,2432]{1,0:T(8,128)(2,1)S(1)}, bf16[32,2432]{1,0:T(8,128)(2,1)S(1)}, u32[]{:S(2)}, u32[]{:S(2)}) collective-permute-start(bf16[32,2432]{1,0:T(8,128)(2,1)S(1)} %get-tuple-element.48), channel_id=1, source_target_pairs={{0,1},{1,2},{2,3},{3,11},{11,10},{10,9},{9,8},{8,0},{4,12},{5,4},{... | collective-permute-start | bytes 466952 | tf_op jit(solution)/shard_map/ppermute | solution.py:176
  6.6 5.3 %collective-permute-start.1 = (bf16[32,2432]{1,0:T(8,128)(2,1)S(1)}, bf16[32,2432]{1,0:T(8,128)(2,1)S(1)}, u32[]{:S(2)}, u32[]{:S(2)}) collective-permute-start(bf16[32,2432]{1,0:T(8,128)(2,1)S(1)} %get-tuple-element.49), channel_id=1, source_target_pairs={{0,1},{1,2},{2,3},{3,11},{11,10},{10,9},{9,8},{8,0},{4,12},{5,4},{... | collective-permute-start | bytes 466952 | tf_op jit(solution)/shard_map/ppermute | solution.py:176
  8.2 5.3 %collective-permute-start.7 = (bf16[32,2432]{1,0:T(8,128)(2,1)S(1)}, bf16[32,2432]{1,0:T(8,128)(2,1)S(1)}, u32[]{:S(2)}, u32[]{:S(2)}) collective-permute-start(bf16[32,2432]{1,0:T(8,128)(2,1)S(1)} %maximum_maximum_fusion.1), channel_id=1, source_target_pairs={{0,1},{1,2},{2,3},{3,11},{11,10},{10,9},{9,8},{8,0},{4,12},{5,4},{... | collective-permute-start | bytes 466952 | tf_op jit(solution)/shard_map/ppermute | solution.py:176
  9.9 5.3 %collective-permute-start.13 = (bf16[32,2432]{1,0:T(8,128)(2,1)S(1)}, bf16[32,2432]{1,0:T(8,128)(2,1)S(1)}, u32[]{:S(2)}, u32[]{:S(2)}) collective-permute-start(bf16[32,2432]{1,0:T(8,128)(2,1)S(1)} %collective-permute-done.12), channel_id=1, source_target_pairs={{0,1},{1,2},{2,3},{3,11},{11,10},{10,9},{9,8},{8,0},{4,12},{5,4},{... | collective-permute-start | bytes 466952 | tf_op jit(solution)/shard_map/ppermute | solution.py:176
  11.9 5.3 %collective-permute-start.2 = (bf16[32,2432]{1,0:T(8,128)(2,1)S(1)}, bf16[32,2432]{1,0:T(8,128)(2,1)S(1)}, u32[]{:S(2)}, u32[]{:S(2)}) collective-permute-start(bf16[32,2432]{1,0:T(8,128)(2,1)S(1)} %collective-permute-done.1), channel_id=1, source_target_pairs={{0,1},{1,2},{2,3},{3,11},{11,10},{10,9},{9,8},{8,0},{4,12},{5,4},{... | collective-permute-start | bytes 466952 | tf_op jit(solution)/shard_map/ppermute | solution.py:176
  13.6 5.3 %collective-permute-start.8 = (bf16[32,2432]{1,0:T(8,128)(2,1)S(1)}, bf16[32,2432]{1,0:T(8,128)(2,1)S(1)}, u32[]{:S(2)}, u32[]{:S(2)}) collective-permute-start(bf16[32,2432]{1,0:T(8,128)(2,1)S(1)} %collective-permute-done.7), channel_id=1, source_target_pairs={{0,1},{1,2},{2,3},{3,11},{11,10},{10,9},{9,8},{8,0},{4,12},{5,4},{... | collective-permute-start | bytes 466952 | tf_op jit(solution)/shard_map/ppermute | solution.py:176
  15.2 5.3 %collective-permute-start.14 = (bf16[32,2432]{1,0:T(8,128)(2,1)S(1)}, bf16[32,2432]{1,0:T(8,128)(2,1)S(1)}, u32[]{:S(2)}, u32[]{:S(2)}) collective-permute-start(bf16[32,2432]{1,0:T(8,128)(2,1)S(1)} %collective-permute-done.13), channel_id=1, source_target_pairs={{0,1},{1,2},{2,3},{3,11},{11,10},{10,9},{9,8},{8,0},{4,12},{5,4},{... | collective-permute-start | bytes 466952 | tf_op jit(solution)/shard_map/ppermute | solution.py:176
  17.2 5.2 %collective-permute-start.3 = (bf16[32,2432]{1,0:T(8,128)(2,1)S(1)}, bf16[32,2432]{1,0:T(8,128)(2,1)S(1)}, u32[]{:S(2)}, u32[]{:S(2)}) collective-permute-start(bf16[32,2432]{1,0:T(8,128)(2,1)S(1)} %collective-permute-done.2), channel_id=1, source_target_pairs={{0,1},{1,2},{2,3},{3,11},{11,10},{10,9},{9,8},{8,0},{4,12},{5,4},{... | collective-permute-start | bytes 466952 | tf_op jit(solution)/shard_map/ppermute | solution.py:176
  18.8 5.2 %collective-permute-start.9 = (bf16[32,2432]{1,0:T(8,128)(2,1)S(1)}, bf16[32,2432]{1,0:T(8,128)(2,1)S(1)}, u32[]{:S(2)}, u32[]{:S(2)}) collective-permute-start(bf16[32,2432]{1,0:T(8,128)(2,1)S(1)} %collective-permute-done.8), channel_id=1, source_target_pairs={{0,1},{1,2},{2,3},{3,11},{11,10},{10,9},{9,8},{8,0},{4,12},{5,4},{... | collective-permute-start | bytes 466952 | tf_op jit(solution)/shard_map/ppermute | solution.py:176
  20.5 5.2 %collective-permute-start.15 = (bf16[16,2432]{1,0:T(8,128)(2,1)S(1)}, bf16[16,2432]{1,0:T(8,128)(2,1)S(1)}, u32[]{:S(2)}, u32[]{:S(2)}) collective-permute-start(bf16[16,2432]{1,0:T(8,128)(2,1)S(1)} %slice.155), channel_id=1, source_target_pairs={{0,1},{1,2},{2,3},{3,11},{11,10},{10,9},{9,8},{8,0},{4,12},{5,4},{... | collective-permute-start | bytes 233480 | tf_op jit(solution)/shard_map/ppermute | solution.py:176
  22.4 4.4 %collective-permute-start.4 = (bf16[16,2432]{1,0:T(8,128)(2,1)S(1)}, bf16[16,2432]{1,0:T(8,128)(2,1)S(1)}, u32[]{:S(2)}, u32[]{:S(2)}) collective-permute-start(bf16[16,2432]{1,0:T(8,128)(2,1)S(1)} %slice.149), channel_id=1, source_target_pairs={{0,1},{1,2},{2,3},{3,11},{11,10},{10,9},{9,8},{8,0},{4,12},{5,4},{... | collective-permute-start | bytes 233480 | tf_op jit(solution)/shard_map/ppermute | solution.py:176
  24.1 4.4 %collective-permute-start.10 = (bf16[16,2432]{1,0:T(8,128)(2,1)S(1)}, bf16[16,2432]{1,0:T(8,128)(2,1)S(1)}, u32[]{:S(2)}, u32[]{:S(2)}) collective-permute-start(bf16[16,2432]{1,0:T(8,128)(2,1)S(1)} %slice.153), channel_id=1, source_target_pairs={{0,1},{1,2},{2,3},{3,11},{11,10},{10,9},{9,8},{8,0},{4,12},{5,4},{... | collective-permute-start | bytes 233480 | tf_op jit(solution)/shard_map/ppermute | solution.py:176
  25.8 2.9 %collective-permute-start.16 = (bf16[128,2432]{1,0:T(8,128)(2,1)S(1)}, bf16[128,2432]{1,0:T(8,128)(2,1)S(1)}, u32[]{:S(2)}, u32[]{:S(2)}) collective-permute-start(bf16[128,2432]{1,0:T(8,128)(2,1)S(1)} %constant_dynamic-update-slice_fusion.8.refs_0_), channel_id=1, source_target_pairs={{0,4},{4,0},{1,5},{5,1},{2,6},{6,2},{3,7},{7,3},{11,15},{15,11},{1... | collective-permute-start | bytes 1867784 | tf_op jit(solution)/shard_map/ppermute | solution.py:176
  26.9 2.7 %collective-permute-start.5 = (bf16[128,2432]{1,0:T(8,128)(2,1)S(1)}, bf16[128,2432]{1,0:T(8,128)(2,1)S(1)}, u32[]{:S(2)}, u32[]{:S(2)}) collective-permute-start(bf16[128,2432]{1,0:T(8,128)(2,1)S(1)} %constant_dynamic-update-slice_fusion.refs_2_.refs_0_), channel_id=1, source_target_pairs={{0,4},{4,0},{1,5},{5,1},{2,6},{6,2},{3,7},{7,3},{11,15},{15,11},{1... | collective-permute-start | bytes 1867784 | tf_op jit(solution)/shard_map/ppermute | solution.py:176
  35.7 4.4 %collective-permute-start.18 = (bf16[128,1792]{1,0:T(8,128)(2,1)S(1)}, bf16[128,1792]{1,0:T(8,128)(2,1)S(1)}, u32[]{:S(2)}, u32[]{:S(2)}) collective-permute-start(bf16[128,1792]{1,0:T(8,128)(2,1)S(1)} %get-tuple-element.33), channel_id=1, source_target_pairs={{0,4},{4,0},{1,5},{5,1},{2,6},{6,2},{3,7},{7,3},{11,15},{15,11},{1... | collective-permute-start | bytes 1376264 | tf_op jit(solution)/shard_map/ppermute | solution.py:176
  35.9 7.6 %collective-permute-start.19 = (bf16[32,1792]{1,0:T(8,128)(2,1)S(1)}, bf16[32,1792]{1,0:T(8,128)(2,1)S(1)}, u32[]{:S(2)}, u32[]{:S(2)}) collective-permute-start(bf16[32,1792]{1,0:T(8,128)(2,1)S(1)} %add_convert_fusion.3), channel_id=1, source_target_pairs={{0,8},{4,5},{1,0},{5,6},{2,1},{6,7},{3,2},{7,15},{11,3},{15,14},{1... | collective-permute-start | bytes 344072 | tf_op jit(solution)/shard_map/ppermute | solution.py:176
  37.4 6.1 %collective-permute-start.20 = (bf16[16,1792]{1,0:T(8,128)(2,1)S(1)}, bf16[16,1792]{1,0:T(8,128)(2,1)S(1)}, u32[]{:S(2)}, u32[]{:S(2)}) collective-permute-start(bf16[16,1792]{1,0:T(8,128)(2,1)S(1)} %get-tuple-element.44), channel_id=1, source_target_pairs={{0,9},{4,6},{1,8},{5,7},{2,0},{6,15},{3,1},{7,14},{11,2},{15,13},{... | collective-permute-start | bytes 172040 | tf_op jit(solution)/shard_map/ppermute | solution.py:176
  40.1 8.7 %collective-permute-start.22 = (bf16[32,1792]{1,0:T(8,128)(2,1)S(1)}, bf16[32,1792]{1,0:T(8,128)(2,1)S(1)}, u32[]{:S(2)}, u32[]{:S(2)}) collective-permute-start(bf16[32,1792]{1,0:T(8,128)(2,1)S(1)} %get-tuple-element.46), channel_id=1, source_target_pairs={{0,9},{4,6},{1,8},{5,7},{2,0},{6,15},{3,1},{7,14},{11,2},{15,13},{... | collective-permute-start | bytes 344072 | tf_op jit(solution)/shard_map/ppermute | solution.py:176
  41.7 7.1 %collective-permute-start.23 = (bf16[32,1792]{1,0:T(8,128)(2,1)S(1)}, bf16[32,1792]{1,0:T(8,128)(2,1)S(1)}, u32[]{:S(2)}, u32[]{:S(2)}) collective-permute-start(bf16[32,1792]{1,0:T(8,128)(2,1)S(1)} %get-tuple-element.47), channel_id=1, source_target_pairs={{0,8},{4,5},{1,0},{5,6},{2,1},{6,7},{3,2},{7,15},{11,3},{15,14},{1... | collective-permute-start | bytes 344072 | tf_op jit(solution)/shard_map/ppermute | solution.py:176
  42.2 6.8 %collective-permute-start.24 = (bf16[16,1792]{1,0:T(8,128)(2,1)S(1)}, bf16[16,1792]{1,0:T(8,128)(2,1)S(1)}, u32[]{:S(2)}, u32[]{:S(2)}) collective-permute-start(bf16[16,1792]{1,0:T(8,128)(2,1)S(1)} %get-tuple-element.42), channel_id=1, source_target_pairs={{0,10},{4,7},{1,9},{5,15},{2,8},{6,14},{3,0},{7,13},{11,1},{15,12}... | collective-permute-start | bytes 172040 | tf_op jit(solution)/shard_map/ppermute | solution.py:176
  43.6 7.2 %collective-permute-start.21 = (bf16[32,1792]{1,0:T(8,128)(2,1)S(1)}, bf16[32,1792]{1,0:T(8,128)(2,1)S(1)}, u32[]{:S(2)}, u32[]{:S(2)}) collective-permute-start(bf16[32,1792]{1,0:T(8,128)(2,1)S(1)} %pad_maximum_fusion.2.refs_5_), channel_id=1, source_target_pairs={{0,8},{4,5},{1,0},{5,6},{2,1},{6,7},{3,2},{7,15},{11,3},{15,14},{1... | collective-permute-start | bytes 344072 | tf_op jit(solution)/shard_map/ppermute | solution.py:176
  50.9 4.3 %collective-permute-start.26 = (bf16[16,3584]{1,0:T(8,128)(2,1)S(1)}, bf16[16,3584]{1,0:T(8,128)(2,1)S(1)}, u32[]{:S(2)}, u32[]{:S(2)}) collective-permute-start(bf16[16,3584]{1,0:T(8,128)(2,1)S(1)} %get-tuple-element.51), channel_id=1, source_target_pairs={{1,4},{2,5},{3,6},{11,7},{10,15},{9,14},{8,13},{0,12},{12,0},{4,1}... | collective-permute-start | bytes 344072 | tf_op jit(solution)/shard_map/ppermute | solution.py:176
  51.0 5.1 %collective-permute-start.25 = (bf16[16,3584]{1,0:T(8,128)(2,1)S(1)}, bf16[16,3584]{1,0:T(8,128)(2,1)S(1)}, u32[]{:S(2)}, u32[]{:S(2)}) collective-permute-start(bf16[16,3584]{1,0:T(8,128)(2,1)S(1)} %get-tuple-element.50), channel_id=1, source_target_pairs={{0,8},{4,5},{1,0},{5,6},{2,1},{6,7},{3,2},{7,15},{11,3},{15,14},{1... | collective-permute-start | bytes 344072 | tf_op jit(solution)/shard_map/ppermute | solution.py:176
  (6 other events, 45.3 us)

commit v8 on v7

--- a/solution.py
+++ b/solution.py
@@ -235,7 +235,7 @@
         value = value.astype(jnp.bfloat16)
         passed = move(value, backs[1])
         straight.append(move(part(1, at, 2 * rows).astype(jnp.bfloat16), backs[hops]))
-    straight[0] = with_work(straight[0], value)
+    straight[-1], passed = with_work((straight[-1], passed), value)
     held = [part(i, rows, 2 * rows) for i in range(2)]
     held[0] = held[0] + passed.astype(wide)
     for value in straight:

time: 57 us -> 57.5 us (level)
  starting transfers between devices: 33.3 us -> 34.4 us
    ppermute x27, starting transfers between devices: 33.3 us -> 34.4 us  [move(): return lax.ppermute(value, ('node', 'local'), pairs)]
  transfers between devices with their start and end apart: 27 -> 27, of which waited for: 11 -> 9; matrix products, arithmetic and copies ran while one was open for 2% -> 2% of each run, Pallas kernels for 17% -> 17%
where the time goes in v8:
time: 57.5 us; the launch traced here: 57.3 us
  starting transfers between devices  34.4 us (60%)
  Pallas kernels  11.8 us (21%)
  waiting for transfers between devices  6.45 us (11%)
  other arithmetic  2.94 us (5%)
  between operations  0.99 us (2%)
  local copies, waits for them, and re-layouts  0.75 us (1%)
    ppermute x27, starting transfers between devices, move(): return lax.ppermute(value, ('node', 'local'), pairs)  34.4 us
    pallas_call x6, Pallas kernels, call(): pl.pallas_call(kernel, in_specs=[ANY if i in anys else VMEM for i in rang...  11.8 us
    ppermute x27, waiting for transfers between devices, move(): return lax.ppermute(value, ('node', 'local'), pairs)  6.45 us
  transfers between devices with their start and end apart: 27, of which 9 were waited for; matrix products, arithmetic and copies ran while one was open for 2% of the time, Pallas kernels for 17%

profile of v8, /device:TPU:0, one launch (start us, length us, event | category | flops | bytes accessed | tf_op | source)
XLA Modules:
  0.0 57.3 jit_solution(1118262131623043398)
XLA Ops:
  3.9 2.8 %collective-permute-start.12 = (bf16[32,2432]{1,0:T(8,128)(2,1)S(1)}, bf16[32,2432]{1,0:T(8,128)(2,1)S(1)}, u32[]{:S(2)}, u32[]{:S(2)}) collective-permute-start(bf16[32,2432]{1,0:T(8,128)(2,1)S(1)} %get-tuple-element.50), channel_id=1, source_target_pairs={{0,1},{1,2},{2,3},{3,11},{11,10},{10,9},{9,8},{8,0},{4,12},{5,4},{... | collective-permute-start | bytes 466952 | tf_op jit(solution)/shard_map/ppermute | solution.py:176
  6.6 1.6 %collective-permute-start.1 = (bf16[32,2432]{1,0:T(8,128)(2,1)S(1)}, bf16[32,2432]{1,0:T(8,128)(2,1)S(1)}, u32[]{:S(2)}, u32[]{:S(2)}) collective-permute-start(bf16[32,2432]{1,0:T(8,128)(2,1)S(1)} %get-tuple-element.51), channel_id=1, source_target_pairs={{0,1},{1,2},{2,3},{3,11},{11,10},{10,9},{9,8},{8,0},{4,12},{5,4},{... | collective-permute-start | bytes 466952 | tf_op jit(solution)/shard_map/ppermute | solution.py:176
  8.2 1.6 %collective-permute-start.7 = (bf16[32,2432]{1,0:T(8,128)(2,1)S(1)}, bf16[32,2432]{1,0:T(8,128)(2,1)S(1)}, u32[]{:S(2)}, u32[]{:S(2)}) collective-permute-start(bf16[32,2432]{1,0:T(8,128)(2,1)S(1)} %maximum_maximum_fusion.1), channel_id=1, source_target_pairs={{0,1},{1,2},{2,3},{3,11},{11,10},{10,9},{9,8},{8,0},{4,12},{5,4},{... | collective-permute-start | bytes 466952 | tf_op jit(solution)/shard_map/ppermute | solution.py:176
  9.9 2.0 %collective-permute-start.13 = (bf16[32,2432]{1,0:T(8,128)(2,1)S(1)}, bf16[32,2432]{1,0:T(8,128)(2,1)S(1)}, u32[]{:S(2)}, u32[]{:S(2)}) collective-permute-start(bf16[32,2432]{1,0:T(8,128)(2,1)S(1)} %collective-permute-done.12), channel_id=1, source_target_pairs={{0,1},{1,2},{2,3},{3,11},{11,10},{10,9},{9,8},{8,0},{4,12},{5,4},{... | collective-permute-start | bytes 466952 | tf_op jit(solution)/shard_map/ppermute | solution.py:176
  11.9 1.6 %collective-permute-start.2 = (bf16[32,2432]{1,0:T(8,128)(2,1)S(1)}, bf16[32,2432]{1,0:T(8,128)(2,1)S(1)}, u32[]{:S(2)}, u32[]{:S(2)}) collective-permute-start(bf16[32,2432]{1,0:T(8,128)(2,1)S(1)} %collective-permute-done.1), channel_id=1, source_target_pairs={{0,1},{1,2},{2,3},{3,11},{11,10},{10,9},{9,8},{8,0},{4,12},{5,4},{... | collective-permute-start | bytes 466952 | tf_op jit(solution)/shard_map/ppermute | solution.py:176
  13.6 1.6 %collective-permute-start.8 = (bf16[32,2432]{1,0:T(8,128)(2,1)S(1)}, bf16[32,2432]{1,0:T(8,128)(2,1)S(1)}, u32[]{:S(2)}, u32[]{:S(2)}) collective-permute-start(bf16[32,2432]{1,0:T(8,128)(2,1)S(1)} %collective-permute-done.7), channel_id=1, source_target_pairs={{0,1},{1,2},{2,3},{3,11},{11,10},{10,9},{9,8},{8,0},{4,12},{5,4},{... | collective-permute-start | bytes 466952 | tf_op jit(solution)/shard_map/ppermute | solution.py:176
  15.2 1.9 %collective-permute-start.14 = (bf16[32,2432]{1,0:T(8,128)(2,1)S(1)}, bf16[32,2432]{1,0:T(8,128)(2,1)S(1)}, u32[]{:S(2)}, u32[]{:S(2)}) collective-permute-start(bf16[32,2432]{1,0:T(8,128)(2,1)S(1)} %collective-permute-done.13), channel_id=1, source_target_pairs={{0,1},{1,2},{2,3},{3,11},{11,10},{10,9},{9,8},{8,0},{4,12},{5,4},{... | collective-permute-start | bytes 466952 | tf_op jit(solution)/shard_map/ppermute | solution.py:176
  17.2 1.6 %collective-permute-start.3 = (bf16[32,2432]{1,0:T(8,128)(2,1)S(1)}, bf16[32,2432]{1,0:T(8,128)(2,1)S(1)}, u32[]{:S(2)}, u32[]{:S(2)}) collective-permute-start(bf16[32,2432]{1,0:T(8,128)(2,1)S(1)} %collective-permute-done.2), channel_id=1, source_target_pairs={{0,1},{1,2},{2,3},{3,11},{11,10},{10,9},{9,8},{8,0},{4,12},{5,4},{... | collective-permute-start | bytes 466952 | tf_op jit(solution)/shard_map/ppermute | solution.py:176
  18.8 1.6 %collective-permute-start.9 = (bf16[32,2432]{1,0:T(8,128)(2,1)S(1)}, bf16[32,2432]{1,0:T(8,128)(2,1)S(1)}, u32[]{:S(2)}, u32[]{:S(2)}) collective-permute-start(bf16[32,2432]{1,0:T(8,128)(2,1)S(1)} %collective-permute-done.8), channel_id=1, source_target_pairs={{0,1},{1,2},{2,3},{3,11},{11,10},{10,9},{9,8},{8,0},{4,12},{5,4},{... | collective-permute-start | bytes 466952 | tf_op jit(solution)/shard_map/ppermute | solution.py:176
  20.5 1.8 %collective-permute-start.15 = (bf16[16,2432]{1,0:T(8,128)(2,1)S(1)}, bf16[16,2432]{1,0:T(8,128)(2,1)S(1)}, u32[]{:S(2)}, u32[]{:S(2)}) collective-permute-start(bf16[16,2432]{1,0:T(8,128)(2,1)S(1)} %slice.155), channel_id=1, source_target_pairs={{0,1},{1,2},{2,3},{3,11},{11,10},{10,9},{9,8},{8,0},{4,12},{5,4},{... | collective-permute-start | bytes 233480 | tf_op jit(solution)/shard_map/ppermute | solution.py:176
  22.4 1.6 %collective-permute-start.4 = (bf16[16,2432]{1,0:T(8,128)(2,1)S(1)}, bf16[16,2432]{1,0:T(8,128)(2,1)S(1)}, u32[]{:S(2)}, u32[]{:S(2)}) collective-permute-start(bf16[16,2432]{1,0:T(8,128)(2,1)S(1)} %slice.149), channel_id=1, source_target_pairs={{0,1},{1,2},{2,3},{3,11},{11,10},{10,9},{9,8},{8,0},{4,12},{5,4},{... | collective-permute-start | bytes 233480 | tf_op jit(solution)/shard_map/ppermute | solution.py:176
  24.1 1.6 %collective-permute-start.10 = (bf16[16,2432]{1,0:T(8,128)(2,1)S(1)}, bf16[16,2432]{1,0:T(8,128)(2,1)S(1)}, u32[]{:S(2)}, u32[]{:S(2)}) collective-permute-start(bf16[16,2432]{1,0:T(8,128)(2,1)S(1)} %slice.153), channel_id=1, source_target_pairs={{0,1},{1,2},{2,3},{3,11},{11,10},{10,9},{9,8},{8,0},{4,12},{5,4},{... | collective-permute-start | bytes 233480 | tf_op jit(solution)/shard_map/ppermute | solution.py:176
  26.9 1.6 %collective-permute-done.10 = bf16[16,2432]{1,0:T(8,128)(2,1)S(1)} collective-permute-done((bf16[16,2432]{1,0:T(8,128)(2,1)S(1)}, bf16[16,2432]{1,0:T(8,128)(2,1)S(1)}, u32[]{:S(2)}, u32[]{:S(2)}) %collective-permute-start.10) | collective-permute-done | bytes 77856 | tf_op jit(solution)/shard_map/ppermute | solution.py:176
  29.5 1.5 %finish.1 = (f32[256,512]{1,0:T(8,128)S(1)}, f32[256,512]{1,0:T(8,128)S(1)}, f32[256,512]{1,0:T(8,128)S(1)}) custom-call(bf16[128,2432]{1,0:T(8,128)(2,1)S(1)} %constant_dynamic-update-slice_fusion.8.refs_0_, bf16[128,2432]{1,0:T(8,128)(2,1)S(1)} %collective-permute-done.16.refs_1_, bf16[128,2432]{1,0:T(8,128)(2,1)S(1)} %constant_dynamic-update-slice_fusion.refs_2_.refs_0_, ...), custom_call_target="tpu_custom_call" | custom-call | flops 2818572288 | bytes 11010048 | tf_op jit(solution)/shard_map/finish/pallas_call | solution.py:416
  31.5 2.3 %backward.1 = (f32[128,1792]{1,0:T(8,128)S(1)}, bf16[128,1792]{1,0:T(8,128)(2,1)S(1)}, bf16[256,1024]{1,0:T(8,128)(2,1)S(1)}, bf16[256,512]{1,0:T(8,128)(2,1)S(1)}) custom-call(bf16[128,2432]{1,0:T(8,128)(2,1)S(1)} %constant_dynamic-update-slice_fusion.refs_2_.refs_0_, bf16[128,2432]{1,0:T(8,128)(2,1)S(1)} %collective-permute-done.5.refs_3_.refs_1_, ...), custom_call_target="tpu_custom_call" | custom-call | flops 1879048192 | bytes 7340032 | tf_op jit(solution)/shard_map/backward/pallas_call | solution.py:416
  35.9 1.5 %collective-permute-start.20 = (bf16[32,1792]{1,0:T(8,128)(2,1)S(1)}, bf16[32,1792]{1,0:T(8,128)(2,1)S(1)}, u32[]{:S(2)}, u32[]{:S(2)}) collective-permute-start(bf16[32,1792]{1,0:T(8,128)(2,1)S(1)} %add_convert_fusion.2), channel_id=1, source_target_pairs={{0,8},{4,5},{1,0},{5,6},{2,1},{6,7},{3,2},{7,15},{11,3},{15,14},{1... | collective-permute-start | bytes 344072 | tf_op jit(solution)/shard_map/ppermute | solution.py:176
  37.4 2.6 %collective-permute-start.21 = (bf16[16,1792]{1,0:T(8,128)(2,1)S(1)}, bf16[16,1792]{1,0:T(8,128)(2,1)S(1)}, u32[]{:S(2)}, u32[]{:S(2)}) collective-permute-start(bf16[16,1792]{1,0:T(8,128)(2,1)S(1)} %get-tuple-element.48), channel_id=1, source_target_pairs={{0,9},{4,6},{1,8},{5,7},{2,0},{6,15},{3,1},{7,14},{11,2},{15,13},{... | collective-permute-start | bytes 172040 | tf_op jit(solution)/shard_map/ppermute | solution.py:176
  40.1 1.6 %collective-permute-start.19 = (bf16[32,1792]{1,0:T(8,128)(2,1)S(1)}, bf16[32,1792]{1,0:T(8,128)(2,1)S(1)}, u32[]{:S(2)}, u32[]{:S(2)}) collective-permute-start(bf16[32,1792]{1,0:T(8,128)(2,1)S(1)} %get-tuple-element.47), channel_id=1, source_target_pairs={{0,8},{4,5},{1,0},{5,6},{2,1},{6,7},{3,2},{7,15},{11,3},{15,14},{1... | collective-permute-start | bytes 344072 | tf_op jit(solution)/shard_map/ppermute | solution.py:176
  42.2 1.3 %collective-permute-start.24 = (bf16[16,1792]{1,0:T(8,128)(2,1)S(1)}, bf16[16,1792]{1,0:T(8,128)(2,1)S(1)}, u32[]{:S(2)}, u32[]{:S(2)}) collective-permute-start(bf16[16,1792]{1,0:T(8,128)(2,1)S(1)} %get-tuple-element.44), channel_id=1, source_target_pairs={{0,10},{4,7},{1,9},{5,15},{2,8},{6,14},{3,0},{7,13},{11,1},{15,12}... | collective-permute-start | bytes 172040 | tf_op jit(solution)/shard_map/ppermute | solution.py:176
  43.6 1.6 %collective-permute-start.22 = (bf16[32,1792]{1,0:T(8,128)(2,1)S(1)}, bf16[32,1792]{1,0:T(8,128)(2,1)S(1)}, u32[]{:S(2)}, u32[]{:S(2)}) collective-permute-start(bf16[32,1792]{1,0:T(8,128)(2,1)S(1)} %pad_maximum_fusion.2.refs_5_), channel_id=1, source_target_pairs={{0,8},{4,5},{1,0},{5,6},{2,1},{6,7},{3,2},{7,15},{11,3},{15,14},{1... | collective-permute-start | bytes 344072 | tf_op jit(solution)/shard_map/ppermute | solution.py:176
  45.2 3.6 %input_grads.1 = (bf16[2,3584,256]{2,1,0:T(8,128)(2,1)}, bf16[2,3584,256]{2,1,0:T(8,128)(2,1)}) custom-call(bf16[128,2432]{1,0:T(8,128)(2,1)S(1)} %constant_dynamic-update-slice_fusion.8.refs_0_, bf16[128,2432]{1,0:T(8,128)(2,1)S(1)} %collective-permute-done.16.refs_1_, bf16[128,2432]{1,0:T(8,128)(2,1)S(1)} %constant_dynamic-update-slice_fusion.refs_2_.refs_0_, ...), custom_call_target="tpu_custom_call" | custom-call | flops 1879048192 | bytes 7340032 | tf_op jit(solution)/shard_map/input_grads/pallas_call | solution.py:416
  50.2 2.0 %collective-permute-start.25 = (bf16[16,3584]{1,0:T(8,128)(2,1)S(1)}, bf16[16,3584]{1,0:T(8,128)(2,1)S(1)}, u32[]{:S(2)}, u32[]{:S(2)}) collective-permute-start(bf16[16,3584]{1,0:T(8,128)(2,1)S(1)} %get-tuple-element.52), channel_id=1, source_target_pairs={{0,8},{4,5},{1,0},{5,6},{2,1},{6,7},{3,2},{7,15},{11,3},{15,14},{1... | collective-permute-start | bytes 344072 | tf_op jit(solution)/shard_map/ppermute | solution.py:176
  52.2 2.3 %down_grad.1 = bf16[2,256,3584]{2,1,0:T(8,128)(2,1)} custom-call(bf16[128,2432]{1,0:T(8,128)(2,1)S(1)} %constant_dynamic-update-slice_fusion.refs_2_.refs_0_, bf16[128,2432]{1,0:T(8,128)(2,1)S(1)} %collective-permute-done.5.refs_3_.refs_1_, bf16[128,2432]{1,0:T(8,128)(2,1)S(1)} %constant_dynamic-update-slice_fusion.4.refs_2_, ...), custom_call_target="tpu_custom_call" | custom-call | flops 939524096 | bytes 3670016 | tf_op jit(solution)/shard_map/down_grad/pallas_call | solution.py:416
  54.5 2.1 %collective-permute-done.25 = bf16[16,3584]{1,0:T(8,128)(2,1)S(1)} collective-permute-done((bf16[16,3584]{1,0:T(8,128)(2,1)S(1)}, bf16[16,3584]{1,0:T(8,128)(2,1)S(1)}, u32[]{:S(2)}, u32[]{:S(2)}) %collective-permute-start.25) | collective-permute-done | bytes 114720 | tf_op jit(solution)/shard_map/ppermute | solution.py:176
  (80 shorter events, 10.9 us)
Async XLA Ops:
  3.4 4.8 %collective-permute-start.6 = (bf16[16,128]{1,0:T(8,128)(2,1)S(1)}, bf16[16,128]{1,0:T(8,128)(2,1)S(1)}, u32[]{:S(2)}, u32[]{:S(2)}) collective-permute-start(bf16[16,128]{1,0:T(8,128)(2,1)S(1)} %multiply_convert_fusion), channel_id=1, source_target_pairs={{0,4},{4,0},{1,5},{5,1},{2,6},{6,2},{3,7},{7,3},{11,15},{15,11},{1... | collective-permute-start | bytes 12296 | tf_op jit(solution)/shard_map/ppermute | solution.py:176
  3.9 6.0 %collective-permute-start.12 = (bf16[32,2432]{1,0:T(8,128)(2,1)S(1)}, bf16[32,2432]{1,0:T(8,128)(2,1)S(1)}, u32[]{:S(2)}, u32[]{:S(2)}) collective-permute-start(bf16[32,2432]{1,0:T(8,128)(2,1)S(1)} %get-tuple-element.50), channel_id=1, source_target_pairs={{0,1},{1,2},{2,3},{3,11},{11,10},{10,9},{9,8},{8,0},{4,12},{5,4},{... | collective-permute-start | bytes 466952 | tf_op jit(solution)/shard_map/ppermute | solution.py:176
  6.6 5.3 %collective-permute-start.1 = (bf16[32,2432]{1,0:T(8,128)(2,1)S(1)}, bf16[32,2432]{1,0:T(8,128)(2,1)S(1)}, u32[]{:S(2)}, u32[]{:S(2)}) collective-permute-start(bf16[32,2432]{1,0:T(8,128)(2,1)S(1)} %get-tuple-element.51), channel_id=1, source_target_pairs={{0,1},{1,2},{2,3},{3,11},{11,10},{10,9},{9,8},{8,0},{4,12},{5,4},{... | collective-permute-start | bytes 466952 | tf_op jit(solution)/shard_map/ppermute | solution.py:176
  8.2 5.3 %collective-permute-start.7 = (bf16[32,2432]{1,0:T(8,128)(2,1)S(1)}, bf16[32,2432]{1,0:T(8,128)(2,1)S(1)}, u32[]{:S(2)}, u32[]{:S(2)}) collective-permute-start(bf16[32,2432]{1,0:T(8,128)(2,1)S(1)} %maximum_maximum_fusion.1), channel_id=1, source_target_pairs={{0,1},{1,2},{2,3},{3,11},{11,10},{10,9},{9,8},{8,0},{4,12},{5,4},{... | collective-permute-start | bytes 466952 | tf_op jit(solution)/shard_map/ppermute | solution.py:176
  9.9 5.3 %collective-permute-start.13 = (bf16[32,2432]{1,0:T(8,128)(2,1)S(1)}, bf16[32,2432]{1,0:T(8,128)(2,1)S(1)}, u32[]{:S(2)}, u32[]{:S(2)}) collective-permute-start(bf16[32,2432]{1,0:T(8,128)(2,1)S(1)} %collective-permute-done.12), channel_id=1, source_target_pairs={{0,1},{1,2},{2,3},{3,11},{11,10},{10,9},{9,8},{8,0},{4,12},{5,4},{... | collective-permute-start | bytes 466952 | tf_op jit(solution)/shard_map/ppermute | solution.py:176
  11.9 5.3 %collective-permute-start.2 = (bf16[32,2432]{1,0:T(8,128)(2,1)S(1)}, bf16[32,2432]{1,0:T(8,128)(2,1)S(1)}, u32[]{:S(2)}, u32[]{:S(2)}) collective-permute-start(bf16[32,2432]{1,0:T(8,128)(2,1)S(1)} %collective-permute-done.1), channel_id=1, source_target_pairs={{0,1},{1,2},{2,3},{3,11},{11,10},{10,9},{9,8},{8,0},{4,12},{5,4},{... | collective-permute-start | bytes 466952 | tf_op jit(solution)/shard_map/ppermute | solution.py:176
  13.6 5.3 %collective-permute-start.8 = (bf16[32,2432]{1,0:T(8,128)(2,1)S(1)}, bf16[32,2432]{1,0:T(8,128)(2,1)S(1)}, u32[]{:S(2)}, u32[]{:S(2)}) collective-permute-start(bf16[32,2432]{1,0:T(8,128)(2,1)S(1)} %collective-permute-done.7), channel_id=1, source_target_pairs={{0,1},{1,2},{2,3},{3,11},{11,10},{10,9},{9,8},{8,0},{4,12},{5,4},{... | collective-permute-start | bytes 466952 | tf_op jit(solution)/shard_map/ppermute | solution.py:176
  15.2 5.3 %collective-permute-start.14 = (bf16[32,2432]{1,0:T(8,128)(2,1)S(1)}, bf16[32,2432]{1,0:T(8,128)(2,1)S(1)}, u32[]{:S(2)}, u32[]{:S(2)}) collective-permute-start(bf16[32,2432]{1,0:T(8,128)(2,1)S(1)} %collective-permute-done.13), channel_id=1, source_target_pairs={{0,1},{1,2},{2,3},{3,11},{11,10},{10,9},{9,8},{8,0},{4,12},{5,4},{... | collective-permute-start | bytes 466952 | tf_op jit(solution)/shard_map/ppermute | solution.py:176
  17.2 5.2 %collective-permute-start.3 = (bf16[32,2432]{1,0:T(8,128)(2,1)S(1)}, bf16[32,2432]{1,0:T(8,128)(2,1)S(1)}, u32[]{:S(2)}, u32[]{:S(2)}) collective-permute-start(bf16[32,2432]{1,0:T(8,128)(2,1)S(1)} %collective-permute-done.2), channel_id=1, source_target_pairs={{0,1},{1,2},{2,3},{3,11},{11,10},{10,9},{9,8},{8,0},{4,12},{5,4},{... | collective-permute-start | bytes 466952 | tf_op jit(solution)/shard_map/ppermute | solution.py:176
  18.8 5.2 %collective-permute-start.9 = (bf16[32,2432]{1,0:T(8,128)(2,1)S(1)}, bf16[32,2432]{1,0:T(8,128)(2,1)S(1)}, u32[]{:S(2)}, u32[]{:S(2)}) collective-permute-start(bf16[32,2432]{1,0:T(8,128)(2,1)S(1)} %collective-permute-done.8), channel_id=1, source_target_pairs={{0,1},{1,2},{2,3},{3,11},{11,10},{10,9},{9,8},{8,0},{4,12},{5,4},{... | collective-permute-start | bytes 466952 | tf_op jit(solution)/shard_map/ppermute | solution.py:176
  20.5 5.2 %collective-permute-start.15 = (bf16[16,2432]{1,0:T(8,128)(2,1)S(1)}, bf16[16,2432]{1,0:T(8,128)(2,1)S(1)}, u32[]{:S(2)}, u32[]{:S(2)}) collective-permute-start(bf16[16,2432]{1,0:T(8,128)(2,1)S(1)} %slice.155), channel_id=1, source_target_pairs={{0,1},{1,2},{2,3},{3,11},{11,10},{10,9},{9,8},{8,0},{4,12},{5,4},{... | collective-permute-start | bytes 233480 | tf_op jit(solution)/shard_map/ppermute | solution.py:176
  22.4 4.4 %collective-permute-start.4 = (bf16[16,2432]{1,0:T(8,128)(2,1)S(1)}, bf16[16,2432]{1,0:T(8,128)(2,1)S(1)}, u32[]{:S(2)}, u32[]{:S(2)}) collective-permute-start(bf16[16,2432]{1,0:T(8,128)(2,1)S(1)} %slice.149), channel_id=1, source_target_pairs={{0,1},{1,2},{2,3},{3,11},{11,10},{10,9},{9,8},{8,0},{4,12},{5,4},{... | collective-permute-start | bytes 233480 | tf_op jit(solution)/shard_map/ppermute | solution.py:176
  24.1 4.4 %collective-permute-start.10 = (bf16[16,2432]{1,0:T(8,128)(2,1)S(1)}, bf16[16,2432]{1,0:T(8,128)(2,1)S(1)}, u32[]{:S(2)}, u32[]{:S(2)}) collective-permute-start(bf16[16,2432]{1,0:T(8,128)(2,1)S(1)} %slice.153), channel_id=1, source_target_pairs={{0,1},{1,2},{2,3},{3,11},{11,10},{10,9},{9,8},{8,0},{4,12},{5,4},{... | collective-permute-start | bytes 233480 | tf_op jit(solution)/shard_map/ppermute | solution.py:176
  25.8 2.9 %collective-permute-start.16 = (bf16[128,2432]{1,0:T(8,128)(2,1)S(1)}, bf16[128,2432]{1,0:T(8,128)(2,1)S(1)}, u32[]{:S(2)}, u32[]{:S(2)}) collective-permute-start(bf16[128,2432]{1,0:T(8,128)(2,1)S(1)} %constant_dynamic-update-slice_fusion.8.refs_0_), channel_id=1, source_target_pairs={{0,4},{4,0},{1,5},{5,1},{2,6},{6,2},{3,7},{7,3},{11,15},{15,11},{1... | collective-permute-start | bytes 1867784 | tf_op jit(solution)/shard_map/ppermute | solution.py:176
  26.9 2.7 %collective-permute-start.5 = (bf16[128,2432]{1,0:T(8,128)(2,1)S(1)}, bf16[128,2432]{1,0:T(8,128)(2,1)S(1)}, u32[]{:S(2)}, u32[]{:S(2)}) collective-permute-start(bf16[128,2432]{1,0:T(8,128)(2,1)S(1)} %constant_dynamic-update-slice_fusion.refs_2_.refs_0_), channel_id=1, source_target_pairs={{0,4},{4,0},{1,5},{5,1},{2,6},{6,2},{3,7},{7,3},{11,15},{15,11},{1... | collective-permute-start | bytes 1867784 | tf_op jit(solution)/shard_map/ppermute | solution.py:176
  35.7 4.4 %collective-permute-start.18 = (bf16[128,1792]{1,0:T(8,128)(2,1)S(1)}, bf16[128,1792]{1,0:T(8,128)(2,1)S(1)}, u32[]{:S(2)}, u32[]{:S(2)}) collective-permute-start(bf16[128,1792]{1,0:T(8,128)(2,1)S(1)} %get-tuple-element.34), channel_id=1, source_target_pairs={{0,4},{4,0},{1,5},{5,1},{2,6},{6,2},{3,7},{7,3},{11,15},{15,11},{1... | collective-permute-start | bytes 1376264 | tf_op jit(solution)/shard_map/ppermute | solution.py:176
  35.9 7.6 %collective-permute-start.20 = (bf16[32,1792]{1,0:T(8,128)(2,1)S(1)}, bf16[32,1792]{1,0:T(8,128)(2,1)S(1)}, u32[]{:S(2)}, u32[]{:S(2)}) collective-permute-start(bf16[32,1792]{1,0:T(8,128)(2,1)S(1)} %add_convert_fusion.2), channel_id=1, source_target_pairs={{0,8},{4,5},{1,0},{5,6},{2,1},{6,7},{3,2},{7,15},{11,3},{15,14},{1... | collective-permute-start | bytes 344072 | tf_op jit(solution)/shard_map/ppermute | solution.py:176
  37.4 6.1 %collective-permute-start.21 = (bf16[16,1792]{1,0:T(8,128)(2,1)S(1)}, bf16[16,1792]{1,0:T(8,128)(2,1)S(1)}, u32[]{:S(2)}, u32[]{:S(2)}) collective-permute-start(bf16[16,1792]{1,0:T(8,128)(2,1)S(1)} %get-tuple-element.48), channel_id=1, source_target_pairs={{0,9},{4,6},{1,8},{5,7},{2,0},{6,15},{3,1},{7,14},{11,2},{15,13},{... | collective-permute-start | bytes 172040 | tf_op jit(solution)/shard_map/ppermute | solution.py:176
  40.1 8.7 %collective-permute-start.19 = (bf16[32,1792]{1,0:T(8,128)(2,1)S(1)}, bf16[32,1792]{1,0:T(8,128)(2,1)S(1)}, u32[]{:S(2)}, u32[]{:S(2)}) collective-permute-start(bf16[32,1792]{1,0:T(8,128)(2,1)S(1)} %get-tuple-element.47), channel_id=1, source_target_pairs={{0,8},{4,5},{1,0},{5,6},{2,1},{6,7},{3,2},{7,15},{11,3},{15,14},{1... | collective-permute-start | bytes 344072 | tf_op jit(solution)/shard_map/ppermute | solution.py:176
  41.7 8.2 %collective-permute-start.23 = (bf16[32,1792]{1,0:T(8,128)(2,1)S(1)}, bf16[32,1792]{1,0:T(8,128)(2,1)S(1)}, u32[]{:S(2)}, u32[]{:S(2)}) collective-permute-start(bf16[32,1792]{1,0:T(8,128)(2,1)S(1)} %get-tuple-element.46), channel_id=1, source_target_pairs={{0,9},{4,6},{1,8},{5,7},{2,0},{6,15},{3,1},{7,14},{11,2},{15,13},{... | collective-permute-start | bytes 344072 | tf_op jit(solution)/shard_map/ppermute | solution.py:176
  42.2 7.9 %collective-permute-start.24 = (bf16[16,1792]{1,0:T(8,128)(2,1)S(1)}, bf16[16,1792]{1,0:T(8,128)(2,1)S(1)}, u32[]{:S(2)}, u32[]{:S(2)}) collective-permute-start(bf16[16,1792]{1,0:T(8,128)(2,1)S(1)} %get-tuple-element.44), channel_id=1, source_target_pairs={{0,10},{4,7},{1,9},{5,15},{2,8},{6,14},{3,0},{7,13},{11,1},{15,12}... | collective-permute-start | bytes 172040 | tf_op jit(solution)/shard_map/ppermute | solution.py:176
  43.6 5.2 %collective-permute-start.22 = (bf16[32,1792]{1,0:T(8,128)(2,1)S(1)}, bf16[32,1792]{1,0:T(8,128)(2,1)S(1)}, u32[]{:S(2)}, u32[]{:S(2)}) collective-permute-start(bf16[32,1792]{1,0:T(8,128)(2,1)S(1)} %pad_maximum_fusion.2.refs_5_), channel_id=1, source_target_pairs={{0,8},{4,5},{1,0},{5,6},{2,1},{6,7},{3,2},{7,15},{11,3},{15,14},{1... | collective-permute-start | bytes 344072 | tf_op jit(solution)/shard_map/ppermute | solution.py:176
  50.2 4.4 %collective-permute-start.26 = (bf16[16,3584]{1,0:T(8,128)(2,1)S(1)}, bf16[16,3584]{1,0:T(8,128)(2,1)S(1)}, u32[]{:S(2)}, u32[]{:S(2)}) collective-permute-start(bf16[16,3584]{1,0:T(8,128)(2,1)S(1)} %get-tuple-element.53), channel_id=1, source_target_pairs={{1,4},{2,5},{3,6},{11,7},{10,15},{9,14},{8,13},{0,12},{12,0},{4,1}... | collective-permute-start | bytes 344072 | tf_op jit(solution)/shard_map/ppermute | solution.py:176
  50.2 6.3 %collective-permute-start.25 = (bf16[16,3584]{1,0:T(8,128)(2,1)S(1)}, bf16[16,3584]{1,0:T(8,128)(2,1)S(1)}, u32[]{:S(2)}, u32[]{:S(2)}) collective-permute-start(bf16[16,3584]{1,0:T(8,128)(2,1)S(1)} %get-tuple-element.52), channel_id=1, source_target_pairs={{0,8},{4,5},{1,0},{5,6},{2,1},{6,7},{3,2},{7,15},{11,3},{15,14},{1... | collective-permute-start | bytes 344072 | tf_op jit(solution)/shard_map/ppermute | solution.py:176
  (6 other events, 45.3 us)
